TPU v7x, 32 devices: a whole 2x2x4 slice. The times are simulated.
32 devices in a mesh: space: 4 (over y, core), date: 8 (over z, x).
Axes of the slice: x: 2, y: 2, z: 4, core: 2. Of those that a mesh axis runs over, the one named last changes fastest.
Arguments:
- obs: bfloat16 [7, 192, 32, 512], P(None, 'date', 'space'), may hold values from -30 to 30
- valid: int32 [192, 32, 512], P('date', 'space'), may hold values from 0 to 1
- days: int32 [192], P('date'), may hold values from 0 to 3649, as said below
Outputs:
- coefficients: float32 [7, 8, 32, 512], P(None, None, 'space', 'date')
- noise_scale: float32 [32, 512], P('space', 'date')
Inputs may be any that keep to these rules, and one draw needn't show every extreme that they name: `days`: day numbers of the acquisitions, in no particular order.
All inputs are finite; a program needn't handle non-finite values.
Results may differ from a plain program's by a relative error of at most 0.0003.
Values may be sent and summed in bfloat16 or wider, within the bound.
No kernel may reach another device: no remote copies, remote signals or barrier semaphores. Data moves between devices by JAX's collectives and lax.ppermute only.
A program may use at most 128 MiB of HBM per device.

v0:
```python
import math

import jax
import jax.numpy as jnp
import numpy as np
from jax import lax
from jax.sharding import PartitionSpec as P

ITERS = 2


tukey_const = 4.685
ridge_value = 1.0
scale_eps = 1e-06
highest = lax.Precision.HIGHEST
pair_first = np.array(
    [row_index for row_index in range(8) for col_index in range(row_index, 8)], dtype=np.int32
)
pair_second = np.array(
    [col_index for row_index in range(8) for col_index in range(row_index, 8)], dtype=np.int32
)


def padded_2(block, sides, width):
    for axis, dim in sides:
        count = lax.axis_size(axis)
        forward = [(i, i + 1) for i in range(count - 1)]
        backward = [(target, source) for source, target in forward]
        low = lax.ppermute(
            lax.slice_in_dim(block, block.shape[dim] - width, None, axis=dim), axis, forward
        )
        high = lax.ppermute(lax.slice_in_dim(block, 0, width, axis=dim), axis, backward)
        block = jnp.concatenate([low, block, high], axis=dim)
    return block


def design(day_numbers):
    day_float = day_numbers.astype(jnp.float32)
    columns = [jnp.ones_like(day_float), (day_float - 1825.0) / 1825.0]
    angle = day_float * (2.0 * math.pi / 365.25)
    for harmonic in range(1, 4):
        columns.append(jnp.cos(harmonic * angle))
        columns.append(jnp.sin(harmonic * angle))
    return jnp.stack(columns, axis=1)


def form_moments(design_rows, weighted, observed):
    products = design_rows[:, pair_first] * design_rows[:, pair_second]
    gram_terms = jnp.dot(
        products.T, weighted, precision=highest, preferred_element_type=jnp.float32
    )
    cross_terms = jnp.einsum(
        "dk,bdp->bkp",
        design_rows,
        weighted[None] * observed,
        precision=highest,
        preferred_element_type=jnp.float32,
    )
    return jnp.concatenate([gram_terms, cross_terms.reshape(-1, weighted.shape[1])], axis=0)


def solve_terms(summed, band_count):
    term_count = 8
    entries = {}
    position = 0
    for row_index in range(term_count):
        for col_index in range(row_index, term_count):
            entries[row_index, col_index] = summed[position]
            position += 1
    right_sides = summed[position:].reshape((band_count, term_count) + summed.shape[1:])
    lower_factor = {}
    for col_index in range(term_count):
        pivot_value = entries[col_index, col_index] + ridge_value
        for inner_index in range(col_index):
            pivot_value = (
                pivot_value
                - lower_factor[col_index, inner_index] * lower_factor[col_index, inner_index]
            )
        pivot_root = jnp.sqrt(pivot_value)
        lower_factor[col_index, col_index] = pivot_root
        for row_index in range(col_index + 1, term_count):
            entry_value = entries[col_index, row_index]
            for inner_index in range(col_index):
                entry_value = (
                    entry_value
                    - lower_factor[row_index, inner_index] * lower_factor[col_index, inner_index]
                )
            lower_factor[row_index, col_index] = entry_value / pivot_root
    forward = []
    for row_index in range(term_count):
        running = right_sides[:, row_index]
        for inner_index in range(row_index):
            running = running - lower_factor[row_index, inner_index][None] * forward[inner_index]
        forward.append(running / lower_factor[row_index, row_index][None])
    solved = [None] * term_count
    for row_index in reversed(range(term_count)):
        running = forward[row_index]
        for inner_index in range(row_index + 1, term_count):
            running = running - lower_factor[inner_index, row_index][None] * solved[inner_index]
        solved[row_index] = running / lower_factor[row_index, row_index][None]
    return (jnp.stack(solved, axis=1), entries[0, 0])


def residual_power(design_rows, observed, coefficient):
    fitted = jnp.einsum(
        "dk,bkp->bdp",
        design_rows,
        coefficient,
        precision=highest,
        preferred_element_type=jnp.float32,
    )
    misfit = observed - fitted
    return jnp.mean(misfit * misfit, axis=0)


def box_sum(padded, row_count, col_count):
    across = padded[0:row_count]
    for offset in range(1, 5):
        across = across + padded[offset : offset + row_count]
    window_sum = across[:, 0:col_count]
    for offset in range(1, 5):
        window_sum = window_sum + across[:, offset : offset + col_count]
    return window_sum


def window_counts(first_index, length, whole):
    global_index = first_index + jnp.arange(length, dtype=jnp.int32)
    return (jnp.minimum(global_index + 2, whole - 1) - jnp.maximum(global_index - 2, 0) + 1).astype(
        jnp.float32
    )


def spread_rows(spread, weight_total, row_count, col_count):
    full_spread = lax.psum(spread, "date")
    variance = full_spread / (1.0 + weight_total)
    padded = padded_2(variance.reshape(row_count, col_count), (("space", 0),), 2)
    return jnp.pad(padded, ((0, 0), (2, 2)))


def next_weight(resid_power, smooth, mask_float):
    scaled = jnp.minimum(
        resid_power / (tukey_const * tukey_const * (smooth[None] + scale_eps)), 1.0
    )
    return mask_float * (1.0 - scaled) * (1.0 - scaled)


def on_device(obs, valid, days):
    band_count, date_count, row_count, col_count = obs.shape
    date_devices = lax.axis_size("date")
    date_index = lax.axis_index("date")
    cols_local = col_count // date_devices
    row_first = lax.axis_index("space") * row_count
    grid_rows = row_count * lax.axis_size("space")
    pixels = row_count * col_count
    mask_float = valid.astype(jnp.float32).reshape(date_count, pixels)
    observed = obs.astype(jnp.float32).reshape(band_count, date_count, pixels)
    design_rows = design(days)
    col_first = 0
    slice_start = date_index * cols_local
    counts = (
        window_counts(row_first, row_count, grid_rows)[:, None]
        * window_counts(col_first, col_count, col_count)[None, :]
    )
    weighted = mask_float
    for step in range(ITERS):
        local_terms = form_moments(design_rows, weighted, observed)
        summed = lax.psum(local_terms, "date")
        coefficient, weight_total = solve_terms(summed, band_count)
        resid_power = residual_power(design_rows, observed, coefficient)
        spread = jnp.sum(weighted * resid_power, axis=0)
        padded = spread_rows(spread, weight_total, row_count, col_count)
        smooth = (box_sum(padded, row_count, col_count) / counts).reshape(pixels)
        if step + 1 < ITERS:
            weighted = next_weight(resid_power, smooth, mask_float)
    coefficient = coefficient.reshape(band_count, 8, row_count, col_count)
    noise_scale = jnp.sqrt(smooth + scale_eps).reshape(row_count, col_count)
    coefficients = lax.dynamic_slice_in_dim(coefficient, slice_start, cols_local, 3)
    noise_block = lax.dynamic_slice_in_dim(noise_scale, slice_start, cols_local, 1)
    return (coefficients, noise_block)


def solution(mesh):
    in_specs = (P(None, "date", "space", None), P("date", "space", None), P("date"))
    out_specs = (P(None, None, "space", "date"), P("space", "date"))
    return jax.shard_map(
        on_device, mesh=mesh, in_specs=in_specs, out_specs=out_specs, check_vma=False
    )
```

profile of v0, /device:TPU:0, one launch (start us, length us, event | category | flops | bytes accessed | tf_op | source)
XLA Modules:
  0.0 354.6 jit_solution(17178080810386421481)
XLA Ops:
  11.1 2.4 reshape.5086
  14.7 1.6 convolution_bitcast_fusion.3
  17.9 91.5 %all-reduce.5.cloned.1.call-done = f32[92,4096]{1,0:T(8,128)} async-done(((f32[92,4096]{1,0:T(8,128)}), f32[92,4096]{1,0:T(8,128)}) %all-reduce.5.cloned.1.call-update) | async-done | bytes 1507344 | tf_op jit(solution)/shard_map/psum | solution.py:167
  109.4 2.4 slice_add_fusion.28
  111.7 1.8 subtract_sqrt_fusion.11
  113.6 1.7 subtract_sqrt_fusion.10
  115.3 1.6 rsqrt_multiply_fusion.9
  118.4 2.0 subtract_divide_fusion.19
  120.4 3.7 %subtract_divide_fusion.11 = (f32[7,1,4096]{2,1,0:T(1,128)S(1)}, f32[7,1,4096]{2,1,0:T(1,128)S(1)}, f32[7,1,4096]{2,1,0:T(1,128)S(1)}, f32[7,1,4096]{2,1,0:T(1,1...) fusion(f32[7,1,4096]{2,1,0:T(1,128)S(1)} %get-tuple-element.150, ...), kind=kLoop, calls=%fused_computation.98 | loop fusion | flops 2236416 | bytes 2424832 | tf_op jit(solution)/shard_map/div | solution.py:100
  124.1 3.7 %stack.72 = f32[7,8,4096]{2,1,0:T(8,128)} concatenate(f32[7,1,4096]{2,1,0:T(1,128)S(1)} %get-tuple-element.89, f32[7,1,4096]{2,1,0:T(1,128)S(1)} %get-tuple-element.90, f32[7,1,4096]{2,1,0:T(1,128)S(1)} %get-tuple-element.91, f32[7,1,4096]{2,1,0:T(1,128)} %get-tuple-element.92, f32[7,1,4096]{2,1,0:T(1,128)} %get-tuple-element.93, f32[7,1,4096]{2,1,0:T(1,128)} %get-tuple-element.94, ...), dimensions={1} | concatenate | bytes 1835008 | tf_op jit(solution)/shard_map/stack | solution.py:101
  127.8 3.8 %fusion.6 = f32[24,4096]{1,0:T(8,128)S(1)} fusion(f32[7,24,4096]{2,1,0:T(8,128)S(1)} %reshape.5086, f32[7,8,4096]{2,1,0:T(8,128)} %stack.72, f32[24,8]{0,1:T(8,128)S(1)} %stack.71), kind=kOutput, calls=%fused_computation.14 | convolution fusion | flops 68026368 | bytes 4064000 | tf_op jit(solution)/shard_map/dk,bkp->bdp/dot_general | solution.py:105
  133.9 36.1 %psum.29 = f32[4096]{0:T(1024)} all-reduce(f32[4096]{0:T(1024)} %bitcast.399), channel_id=1, replica_groups=mesh['space'=4,'date'=8] {'date'}, use_global_device_ids=true, to_apply=%region_3.0 | all-reduce | flops 4096 | bytes 32768 | tf_op jit(solution)/shard_map/psum | solution.py:134
  173.9 1.5 collective-permute-start.1
  175.9 1.3 reshape.5080
  177.3 1.6 collective-permute-done.1
  179.7 1.3 broadcast_multiply_fusion.2
  181.7 1.6 convolution_bitcast_fusion.2
  185.3 87.8 %all-reduce.7.cloned.1.call-done = f32[92,4096]{1,0:T(8,128)} async-done(((f32[92,4096]{1,0:T(8,128)}), f32[92,4096]{1,0:T(8,128)}) %all-reduce.7.cloned.1.call-update) | async-done | bytes 1507344 | tf_op jit(solution)/shard_map/psum | solution.py:167
  273.1 1.8 slice_add_fusion.16
  274.8 1.9 subtract_sqrt_fusion.5
  276.7 1.7 subtract_sqrt_fusion.4
  278.4 1.6 rsqrt_multiply_fusion.6
  281.5 3.8 %fusion.144 = (f32[7,4096]{1,0:T(8,128)}, f32[7,1,4096]{2,1,0:T(1,128)S(1)}, f32[7,1,4096]{2,1,0:T(1,128)S(1)}, f32[7,1,4096]{2,1,0:T(1,128)S(1)}, f32[7,1,4096]...) fusion(f32[4096]{0:T(1024)S(1)} %bitcast.393, ...), kind=kLoop, calls=%fused_computation.432 | loop fusion | flops 1835008 | bytes 2539520 | tf_op jit(solution)/shard_map/div | solution.py:100
  288.6 1.4 fusion.151
  290.0 1.5 fusion.152
  291.5 1.6 fusion.153
  293.7 2.1 fusion.154
  295.9 3.6 %stack.82 = f32[7,8,4096]{2,1,0:T(8,128)} concatenate(f32[7,1,4096]{2,1,0:T(1,128)} %get-tuple-element.24, f32[7,1,4096]{2,1,0:T(1,128)} %copy-done.6, f32[7,1,4096]{2,1,0:T(1,128)S(1)} %get-tuple-element.20, f32[7,1,4096]{2,1,0:T(1,128)S(1)} %get-tuple-element.18, f32[7,1,4096]{2,1,0:T(1,128)S(1)} %get-tuple-element.16, f32[7,1,4096]{2,1,0:T(1,128)S(1)} %get-tuple-element.14, ...), dimensions={1} | concatenate | bytes 1835008 | tf_op jit(solution)/shard_map/stack | solution.py:101
  299.5 3.8 %fusion.7 = f32[24,4096]{1,0:T(8,128)S(1)} fusion(f32[7,24,4096]{2,1,0:T(8,128)S(1)} %reshape.5086, f32[7,8,4096]{2,1,0:T(8,128)} %stack.82, f32[24,8]{0,1:T(8,128)S(1)} %stack.71), kind=kOutput, calls=%fused_computation.15 | convolution fusion | flops 68026368 | bytes 4064000 | tf_op jit(solution)/shard_map/dk,bkp->bdp/dot_general | solution.py:105
  304.5 35.5 %psum.31 = f32[4096]{0:T(1024)S(1)} all-reduce(f32[4096]{0:T(1024)S(1)} %bitcast.400), channel_id=1, replica_groups=mesh['space'=4,'date'=8] {'date'}, use_global_device_ids=true, to_apply=%region_7.8 | all-reduce | flops 4096 | bytes 32768 | tf_op jit(solution)/shard_map/psum | solution.py:134
  344.2 1.9 collective-permute-done.3
  346.4 1.4 fusion.128
  (116 shorter events, 29.0 us)
Async XLA Ops:
  7.2 102.2 %all-reduce.5.cloned.1.call-start = ((), (), s32[]{:S(2)}) async-start(), calls=%async_computation | async-start | bytes 3145728 | tf_op jit(solution)/shard_map/psum | solution.py:167
  13.5 0.6 copy-start.15
  17.6 255.4 %all-reduce.7.cloned.1.call-start = ((), (), s32[]{:S(2)}) async-start(), calls=%async_computation.1 | async-start | bytes 3145728 | tf_op jit(solution)/shard_map/psum | solution.py:167
  109.4 7.5 %copy-start.5 = (f32[92,4096]{1,0:T(8,128)S(1)}, f32[92,4096]{1,0:T(8,128)}, u32[]{:S(2)}) copy-start(f32[92,4096]{1,0:T(8,128)} %all-reduce.5.cloned.1.call-done) | copy-start | bytes 4521988
  131.6 1.0 copy-start
  132.6 0.8 copy-start.2
  170.8 0.6 copy-start.19
  172.0 5.3 %collective-permute-start = (f32[2,512]{1,0:T(2,128)}, f32[2,512]{1,0:T(2,128)S(1)}, u32[]{:S(2)}, u32[]{:S(2)}) collective-permute-start(f32[2,512]{1,0:T(2,128)} %slice.432), channel_id=1, source_target_pairs={{0,8},{8,16},{16,24},{1,9},{9,17},{17,25},{2,10},{10,18},{18,26},{... | collective-permute-start | bytes 12296 | tf_op jit(solution)/shard_map/ppermute | solution.py:29
  173.9 5.0 %collective-permute-start.1 = (f32[2,512]{1,0:T(2,128)}, f32[2,512]{1,0:T(2,128)S(1)}, u32[]{:S(2)}, u32[]{:S(2)}) collective-permute-start(f32[2,512]{1,0:T(2,128)} %slice.434), channel_id=1, source_target_pairs={{8,0},{16,8},{24,16},{9,1},{17,9},{25,17},{10,2},{18,10},{26,18},{... | collective-permute-start | bytes 12296 | tf_op jit(solution)/shard_map/ppermute | solution.py:32
  181.0 0.6 copy-start.17
  181.7 1.6 copy-start.16
  273.0 7.0 %copy-start.4 = (f32[92,4096]{1,0:T(8,128)S(1)}, f32[92,4096]{1,0:T(8,128)}, u32[]{:S(2)}) copy-start(f32[92,4096]{1,0:T(8,128)} %all-reduce.7.cloned.1.call-done) | copy-start | bytes 4521988
  293.1 0.6 copy-start.6
  303.2 1.0 copy-start.1
  303.3 1.1 copy-start.3
  303.3 1.1 copy-start.18
  303.3 39.4 %copy-start.11 = (f32[7,4096]{1,0:T(8,128)S(1)}, f32[7,4096]{1,0:T(8,128)}, u32[]{:S(2)}) copy-start(f32[7,4096]{1,0:T(8,128)} %get-tuple-element.23) | copy-start | bytes 344068
  303.3 39.5 %copy-start.10 = (f32[7,4096]{1,0:T(8,128)S(1)}, f32[7,4096]{1,0:T(8,128)}, u32[]{:S(2)}) copy-start(f32[7,4096]{1,0:T(8,128)} %get-tuple-element.21) | copy-start | bytes 344068
  303.3 39.6 %copy-start.14 = (f32[7,4096]{1,0:T(8,128)S(1)}, f32[7,4096]{1,0:T(8,128)}, u32[]{:S(2)}) copy-start(f32[7,4096]{1,0:T(8,128)} %get-tuple-element.19) | copy-start | bytes 344068
  303.3 39.6 %copy-start.9 = (f32[7,4096]{1,0:T(8,128)S(1)}, f32[7,4096]{1,0:T(8,128)}, u32[]{:S(2)}) copy-start(f32[7,4096]{1,0:T(8,128)} %get-tuple-element.17) | copy-start | bytes 344068
  303.4 39.7 %copy-start.13 = (f32[7,4096]{1,0:T(8,128)S(1)}, f32[7,4096]{1,0:T(8,128)}, u32[]{:S(2)}) copy-start(f32[7,4096]{1,0:T(8,128)} %get-tuple-element.15) | copy-start | bytes 344068
  303.4 39.8 %copy-start.8 = (f32[7,4096]{1,0:T(8,128)S(1)}, f32[7,4096]{1,0:T(8,128)}, u32[]{:S(2)}) copy-start(f32[7,4096]{1,0:T(8,128)} %get-tuple-element.13) | copy-start | bytes 344068
  304.4 38.9 %copy-start.12 = (f32[7,4096]{1,0:T(8,128)S(1)}, f32[7,4096]{1,0:T(8,128)}, u32[]{:S(2)}) copy-start(f32[7,4096]{1,0:T(8,128)} %get-tuple-element.11) | copy-start | bytes 344068
  304.4 38.9 %copy-start.7 = (f32[7,4096]{1,0:T(8,128)S(1)}, f32[7,4096]{1,0:T(8,128)}, u32[]{:S(2)}) copy-start(f32[7,4096]{1,0:T(8,128)} %get-tuple-element.2) | copy-start | bytes 344068
  340.1 4.2 %collective-permute-start.2 = (f32[2,512]{1,0:T(2,128)S(1)}, f32[2,512]{1,0:T(2,128)S(1)}, u32[]{:S(2)}, u32[]{:S(2)}) collective-permute-start(f32[2,512]{1,0:T(2,128)S(1)} %slice.491), channel_id=1, source_target_pairs={{0,8},{8,16},{16,24},{1,9},{9,17},{17,25},{2,10},{10,18},{18,26},{... | collective-permute-start | bytes 12296 | tf_op jit(solution)/shard_map/ppermute | solution.py:29
  341.4 4.8 %collective-permute-start.3 = (f32[2,512]{1,0:T(2,128)S(1)}, f32[2,512]{1,0:T(2,128)S(1)}, u32[]{:S(2)}, u32[]{:S(2)}) collective-permute-start(f32[2,512]{1,0:T(2,128)S(1)} %slice.493), channel_id=1, source_target_pairs={{8,0},{16,8},{24,16},{9,1},{17,9},{25,17},{10,2},{18,10},{26,18},{... | collective-permute-start | bytes 12296 | tf_op jit(solution)/shard_map/ppermute | solution.py:32
Sparse Core Ops, SparseCore 0:
  17.7 91.5 all-reduce.4
  185.4 87.6 all-reduce.6
where the time goes:
time: 358 us; the launch traced here: 355 us
  waiting for transfers between devices  183 us (51%)
  blocking collectives  71.6 us (20%)
  other arithmetic  46.9 us (13%)
  local copies, waits for them, and re-layouts  20.9 us (6%)
  between operations  14.6 us (4%)
  matrix products  12 us (3%)
  starting transfers between devices  5.62 us (2%)
    psum x2, waiting for transfers between devices, on_device(): summed = lax.psum(local_terms, 'date')  179 us
    psum x2, blocking collectives, spread_rows(): full_spread = lax.psum(spread, 'date')  71.6 us
    div x9, other arithmetic, solve_terms(): solved[row_index] = running / lower_factor[row_index, row_index][None]  17.5 us
    sqrt x12, other arithmetic, solve_terms(): pivot_root = jnp.sqrt(pivot_value)  7.69 us
    dot_general x2, matrix products, residual_power(): jnp.einsum('dk,bkp->bdp', design_rows, coefficient, precision=highest, pr...  7.52 us
    another operation x3, local copies, waits for them, and re-layouts, solve_terms(): return (jnp.stack(solved, axis=1), entries[0, 0])  7.37 us
  transfers between devices with their start and end apart: 6, of which 4 were waited for; matrix products, arithmetic and copies ran while one was open for 1% of the time, Pallas kernels for 0%

commit v1 on v0

v1 whole, which is shorter than its diff:
```python
import functools
import math

import jax
import jax.numpy as jnp
import numpy as np
from jax import lax
from jax.experimental import pallas as pl
from jax.experimental.pallas import tpu as pltpu
from jax.sharding import PartitionSpec as P

ITERS = 2
TERMS = 8
LANES = 128
TUKEY = 4.685
RIDGE = 1.0
EPS = 1e-06
VMEM_BYTES = 48 * 1024 * 1024
pairs = [(i, j) for i in range(TERMS) for j in range(i, TERMS)]
pair_first = np.array([i for i, _ in pairs], dtype=np.int32)
pair_second = np.array([j for _, j in pairs], dtype=np.int32)
f32 = jnp.float32
bf16 = jnp.bfloat16


def design(day_numbers):
    day_float = day_numbers.astype(f32)
    columns = [jnp.ones_like(day_float), (day_float - 1825.0) / 1825.0]
    angle = day_float * (2.0 * math.pi / 365.25)
    for harmonic in range(1, 4):
        columns.append(jnp.cos(harmonic * angle))
        columns.append(jnp.sin(harmonic * angle))
    return jnp.stack(columns, axis=1)


def split3(x):
    high = lax.reduce_precision(x, 8, 7)
    rest = x - high
    mid = lax.reduce_precision(rest, 8, 7)
    low = rest - mid
    return high.astype(bf16), mid.astype(bf16), low.astype(bf16)


def split3_kernel(x):
    high = x.astype(bf16)
    rest = x - high.astype(f32)
    mid = rest.astype(bf16)
    low = (rest - mid.astype(f32)).astype(bf16)
    return high, mid, low


def pack_kernel(tiles, date_total, me_ref, obs_ref, valid_ref, *outs):
    me = me_ref[0]
    odd = lax.rem(me, 2) == 1
    bands = obs_ref.shape[0]
    dates = obs_ref.shape[1]
    half = dates // 2
    row = lax.broadcasted_iota(jnp.int32, (half, 8, LANES), 1)
    lane = lax.broadcasted_iota(jnp.int32, (half, 8, LANES), 2)
    top = row < 4
    left = lane < 64
    for place, tile_step in enumerate(tiles):
        tile = lax.div(me, 2) ^ tile_step
        start = pl.multiple_of(tile * LANES, LANES)
        for band in range(bands + 1):
            if band < bands:
                block = obs_ref[band, :, :, pl.ds(start, LANES)].astype(f32)
            else:
                block = valid_ref[:, :, pl.ds(start, LANES)].astype(f32)
            block = block.reshape(half, 2, 8, LANES)
            first, second = block[:, 0], block[:, 1]

            def turned(x):
                down = pltpu.roll(x, 4, 1)
                return down, pltpu.roll(x, 64, 2), pltpu.roll(down, 64, 2)

            down_1, side_1, both_1 = turned(first)
            down_2, side_2, both_2 = turned(second)
            even_block = jnp.where(
                top, jnp.where(left, first, both_1), jnp.where(left, down_2, side_2)
            )
            odd_block = jnp.where(
                top, jnp.where(left, side_1, down_1), jnp.where(left, both_2, second)
            )
            same = jnp.where(odd, odd_block, even_block)
            other = jnp.where(odd, even_block, odd_block)
            rows = dates * 4
            outs[2 * place][band * rows : (band + 1) * rows, :] = same.reshape(rows, LANES).astype(
                bf16
            )
            outs[2 * place + 1][band * rows : (band + 1) * rows, :] = other.reshape(
                rows, LANES
            ).astype(bf16)


def packed_blocks(obs, valid, count, me, width):
    bands, dates, rows, cols = obs.shape
    group = LANES // width
    parts = rows // group
    if width == 64 and rows == 8:
        shape = jax.ShapeDtypeStruct(((bands + 1) * dates * parts, LANES), bf16)
        blocks = [None] * count
        half = count // 4
        for tiles in (tuple(range(half, 2 * half)), tuple(range(half))):
            given = pl.pallas_call(
                functools.partial(pack_kernel, tiles, dates),
                out_shape=[shape] * (2 * len(tiles)),
                in_specs=[
                    pl.BlockSpec(memory_space=pltpu.SMEM),
                    pl.BlockSpec(memory_space=pltpu.VMEM),
                    pl.BlockSpec(memory_space=pltpu.VMEM),
                ],
                out_specs=[pl.BlockSpec(memory_space=pltpu.VMEM)] * (2 * len(tiles)),
                compiler_params=pltpu.CompilerParams(vmem_limit_bytes=VMEM_BYTES),
                name="pack",
            )(me.reshape(1), obs, valid)
            for place, tile_step in enumerate(tiles):
                blocks[2 * tile_step] = given[2 * place]
                blocks[2 * tile_step + 1] = given[2 * place + 1]
        return blocks
    whole = jnp.concatenate([obs, valid.astype(bf16)[None]], axis=0)
    whole = whole.reshape(bands + 1, dates, group, parts, count, width)
    whole = whole.transpose(4, 0, 1, 3, 2, 5)
    whole = whole.reshape(count, (bands + 1) * dates * parts, LANES)
    return [lax.dynamic_index_in_dim(whole, me ^ k, 0, keepdims=False) for k in range(count)]


def solve(gram, cross, bands):
    lower = {}
    scaled = {}
    inverse = []
    for col in range(TERMS):
        pivot = gram[col, col] + RIDGE
        for inner in range(col):
            pivot = pivot - lower[col, inner] * scaled[col, inner]
        inverse.append(1.0 / pivot)
        for row in range(col + 1, TERMS):
            entry = gram[col, row]
            for inner in range(col):
                entry = entry - lower[row, inner] * scaled[col, inner]
            scaled[row, col] = entry
            lower[row, col] = entry * inverse[col]
    beta = {}
    for band in range(bands):
        forward = []
        for row in range(TERMS):
            running = cross[row, band]
            for inner in range(row):
                running = running - lower[row, inner] * forward[inner]
            forward.append(running)
        solved = [None] * TERMS
        for row in reversed(range(TERMS)):
            running = forward[row] * inverse[row]
            for inner in range(row + 1, TERMS):
                running = running - lower[inner, row] * solved[inner]
            solved[row] = running
        for row in range(TERMS):
            beta[row, band] = solved[row]
    return beta


def dot(a, b):
    return jnp.dot(a, b, preferred_element_type=f32)


def add_parts(total, size):
    return sum(total[i * size : (i + 1) * size] for i in range(total.shape[0] // size))


def fit_and_spread(parts, bands, gram_sum, cross_sum, y_ref, weight_of, x_ref, power_ref):
    gram = {ij: gram_sum[n * parts : (n + 1) * parts] for n, ij in enumerate(pairs)}
    cross = {
        (k, b): cross_sum[k * parts : (k + 1) * parts, b * LANES : (b + 1) * LANES]
        for k in range(TERMS)
        for b in range(bands)
    }
    beta = solve(gram, cross, bands)
    flat = jnp.concatenate(
        [jnp.concatenate([beta[k, b] for k in range(TERMS)], axis=0) for b in range(bands)], axis=1
    )
    high, mid, low = split3_kernel(flat)
    right = jnp.concatenate([high, high, high, mid, mid, low], axis=0)
    rows = y_ref.shape[0]
    step = 96
    spread = jnp.zeros((8, LANES), f32)
    for start in range(0, rows, step):
        fitted = dot(x_ref[start : start + step, :], right)
        misfit = y_ref[start : start + step, :].astype(f32) - fitted
        power = jnp.zeros((step, LANES), f32)
        for b in range(bands):
            part = misfit[:, b * LANES : (b + 1) * LANES]
            power = power + part * part
        power = power / bands
        if power_ref is not None:
            power_ref[start : start + step, :] = power
        weighted = weight_of(start, step) * power
        spread = spread + jnp.sum(weighted.reshape(step // 8, 8, LANES), axis=0)
    spread = add_parts(spread, parts)
    return beta, spread / (1.0 + gram[0, 0])


def first_kernel(count, bands, parts, *refs):
    blocks = refs[:count]
    left_ref, gram_left_ref, x_ref = refs[count : count + 3]
    y_ref, mask_ref, power_ref, variance_ref = refs[count + 3 : count + 7]
    product_ref = refs[count + 7]
    rows = blocks[0].shape[0] // (bands + 1)
    for k in range(count):
        mask = blocks[k][bands * rows : (bands + 1) * rows, :]
        mask_ref[k * rows : (k + 1) * rows, :] = mask
        for b in range(bands):
            y = blocks[k][b * rows : (b + 1) * rows, :]
            y_ref[k * rows : (k + 1) * rows, b * LANES : (b + 1) * LANES] = y
            product_ref[k * rows : (k + 1) * rows, b * LANES : (b + 1) * LANES] = y * mask
    cross_sum = add_parts(dot(left_ref[...], product_ref[...]), TERMS * parts)
    gram_sum = add_parts(dot(gram_left_ref[...], mask_ref[...]), len(pairs) * parts)

    def weight_of(start, step):
        return mask_ref[start : start + step, :].astype(f32)

    _, variance = fit_and_spread(
        parts, bands, gram_sum, cross_sum, y_ref, weight_of, x_ref, power_ref
    )
    for place in range(variance_ref.shape[0]):
        variance_ref[place, 0:parts, :] = variance


def smoothed(place_ref, field_ref, parts, width, rows, spaces, count):
    group = LANES // width
    space = place_ref[0]
    me = place_ref[1]

    def rows_of(space_now, date_now):
        block = field_ref[space_now * count + date_now, 0:parts, :]
        return [block if h == 0 else pltpu.roll(block, LANES - h * width, 1) for h in range(group)]

    lane = lax.broadcasted_iota(jnp.int32, (rows, LANES), 1)
    sums = []
    for ds in (-1, 0, 1):
        space_now = jnp.clip(space + ds, 0, spaces - 1)
        row_ok = jnp.where((space + ds >= 0) & (space + ds < spaces), 1.0, 0.0)
        across = jnp.zeros((rows, LANES), f32)
        for dd in (-1, 0, 1):
            date_now = jnp.clip(me + dd, 0, count - 1)
            ok = jnp.where((me + dd >= 0) & (me + dd < count), row_ok, 0.0)
            block = jnp.concatenate(rows_of(space_now, date_now), axis=0)
            block = jnp.where(lane < width, block, 0.0) * ok
            for offset in range(-2, 3):
                shift = dd * width - offset
                if abs(shift) >= width and dd * offset <= 0:
                    continue
                moved = block if shift == 0 else pltpu.roll(block, shift % LANES, 1)
                source = lane + offset - dd * width
                across = across + jnp.where((source >= 0) & (source < width), moved, 0.0)
        sums.append(across)
    tall = jnp.concatenate([sums[0][rows - 2 :], sums[1], sums[2][:2]], axis=0)
    total = tall[0:rows]
    for offset in range(1, 5):
        total = total + tall[offset : offset + rows]
    row_index = lax.broadcasted_iota(jnp.int32, (rows, LANES), 0) + space * rows
    col_index = lane + me * width

    def window(index, whole):
        return (jnp.minimum(index + 2, whole - 1) - jnp.maximum(index - 2, 0) + 1).astype(f32)

    smooth = total / (window(row_index, spaces * rows) * window(col_index, count * width))
    return smooth


def to_lanes(tall, parts, width):
    group = LANES // width
    lane = lax.broadcasted_iota(jnp.int32, (parts, LANES), 1)
    out = tall[0:parts]
    for h in range(1, group):
        moved = pltpu.roll(tall[h * parts : (h + 1) * parts], h * width, 1)
        out = jnp.where(lane >= h * width, moved, out)
    return out


def to_rows(block, width):
    group = LANES // width
    tall = [block if h == 0 else pltpu.roll(block, LANES - h * width, 1) for h in range(group)]
    return jnp.concatenate(tall, axis=0)[:, 0:width]


def second_kernel(shape, *refs):
    bands, parts, width, rows, spaces, count = shape
    place_ref, field_ref, y_ref, mask_ref, power_ref = refs[:5]
    left_ref, gram_left_ref, x_ref = refs[5:8]
    coefficient_ref, variance_ref = refs[8:10]
    weight_ref, w_parts, wy_parts = refs[10], refs[11:14], refs[14:17]
    smooth = smoothed(place_ref, field_ref, parts, width, rows, spaces, count)
    smooth = to_lanes(smooth, parts, width)
    scale = 1.0 / (TUKEY * TUKEY * (smooth + EPS))
    scale = jnp.concatenate([scale] * (8 // parts), axis=0)
    total = y_ref.shape[0]
    step = 96
    for start in range(0, total, step):
        power = power_ref[start : start + step, :].reshape(step // 8, 8, LANES)
        left_over = 1.0 - jnp.minimum(power * scale[None], 1.0)
        mask = mask_ref[start : start + step, :].astype(f32)
        weight = mask * (left_over * left_over).reshape(step, LANES)
        weight_ref[start : start + step, :] = weight
        for ref, part in zip(w_parts, split3_kernel(weight)):
            ref[start : start + step, :] = part
        for b in range(bands):
            y = y_ref[start : start + step, b * LANES : (b + 1) * LANES].astype(f32)
            for ref, part in zip(wy_parts, split3_kernel(weight * y)):
                ref[start : start + step, b * LANES : (b + 1) * LANES] = part

    def moments(a_ref, b_refs, size):
        whole = add_parts(dot(a_ref[...], b_refs[0][...]), size)
        whole = whole + add_parts(dot(a_ref[0 : 2 * size, :], b_refs[1][...]), size)
        return whole + dot(a_ref[0:size, :], b_refs[2][...])

    cross_sum = moments(left_ref, wy_parts, TERMS * parts)
    gram_sum = moments(gram_left_ref, w_parts, len(pairs) * parts)

    def weight_of(start, step):
        return weight_ref[start : start + step, :]

    beta, variance = fit_and_spread(
        parts, bands, gram_sum, cross_sum, y_ref, weight_of, x_ref, None
    )
    for place in range(variance_ref.shape[0]):
        variance_ref[place, 0:parts, :] = variance
    for b in range(bands):
        for k in range(TERMS):
            coefficient_ref[b, k] = to_rows(beta[k, b], width)


def last_kernel(shape, place_ref, field_ref, noise_ref):
    bands, parts, width, rows, spaces, count = shape
    smooth = smoothed(place_ref, field_ref, parts, width, rows, spaces, count)
    noise_ref[...] = jnp.sqrt(smooth[:, 0:width] + EPS)


def on_device(obs, valid, days):
    bands, dates, rows, cols = obs.shape
    count = lax.axis_size("date")
    spaces = lax.axis_size("space")
    me = lax.axis_index("date")
    width = cols // count
    group = LANES // width
    parts = rows // group
    total = count * dates * parts
    shape = (bands, parts, width, rows, spaces, count)
    vmem = pl.BlockSpec(memory_space=pltpu.VMEM)
    smem = pl.BlockSpec(memory_space=pltpu.SMEM)
    params = pltpu.CompilerParams(vmem_limit_bytes=VMEM_BYTES)

    blocks = packed_blocks(obs, valid, count, me, width)
    received = [blocks[0]] + [None] * (count - 1)
    for k in sorted(range(1, count), key=lambda k: (-(k // (count // 2)), k)):
        received[k] = lax.ppermute(blocks[k], "date", [(i, i ^ k) for i in range(count)])

    all_days = lax.all_gather(days, "date", axis=0, tiled=False)
    order = me ^ jnp.arange(count, dtype=jnp.int32)
    x = design(jnp.take(all_days, order, axis=0).reshape(-1))
    same_part = jnp.asarray(np.eye(parts, dtype=np.float32))

    def per_row(columns):
        wide = columns[:, None, :, None] * same_part[None, :, None, :]
        return wide.reshape(total, columns.shape[1] * parts)

    x_parts = [part.astype(f32) for part in split3(x)]
    product_parts = [
        part.astype(f32) for part in split3(x[:, pair_first] * x[:, pair_second])
    ]
    left = jnp.concatenate([per_row(p).T for p in x_parts], axis=0).astype(bf16)
    gram_left = jnp.concatenate([per_row(p).T for p in product_parts], axis=0).astype(bf16)
    high, mid, low = [per_row(p) for p in x_parts]
    x_wide = jnp.concatenate([high, mid, low, high, mid, high], axis=1).astype(bf16)

    place = jnp.stack([lax.axis_index("space"), me]).astype(jnp.int32)
    send = jax.ShapeDtypeStruct((spaces * count, 8, LANES), f32)
    wide = (total, bands * LANES)
    narrow = (total, LANES)
    y, mask, power, variance = pl.pallas_call(
        functools.partial(first_kernel, count, bands, parts),
        out_shape=[
            jax.ShapeDtypeStruct(wide, bf16),
            jax.ShapeDtypeStruct(narrow, bf16),
            jax.ShapeDtypeStruct(narrow, f32),
            send,
        ],
        in_specs=[vmem] * (count + 3),
        out_specs=[vmem] * 4,
        scratch_shapes=[pltpu.VMEM(wide, bf16)],
        compiler_params=params,
        name="first",
    )(*received, left, gram_left, x_wide)
    field = lax.all_to_all(variance, ("space", "date"), 0, 0, tiled=True)
    coefficients, variance = pl.pallas_call(
        functools.partial(second_kernel, shape),
        out_shape=[jax.ShapeDtypeStruct((bands, TERMS, rows, width), f32), send],
        in_specs=[smem] + [vmem] * 7,
        out_specs=[vmem] * 2,
        scratch_shapes=[pltpu.VMEM(narrow, f32)]
        + [pltpu.VMEM(narrow, bf16)] * 3
        + [pltpu.VMEM(wide, bf16)] * 3,
        compiler_params=params,
        name="second",
    )(place, field, y, mask, power, left, gram_left, x_wide)
    field = lax.all_to_all(variance, ("space", "date"), 0, 0, tiled=True)
    noise = pl.pallas_call(
        functools.partial(last_kernel, shape),
        out_shape=jax.ShapeDtypeStruct((rows, width), f32),
        in_specs=[smem, vmem],
        out_specs=vmem,
        compiler_params=params,
        name="last",
    )(place, field)
    return coefficients, noise


def solution(mesh):
    in_specs = (P(None, "date", "space", None), P("date", "space", None), P("date"))
    out_specs = (P(None, None, "space", "date"), P("space", "date"))
    return jax.shard_map(
        on_device, mesh=mesh, in_specs=in_specs, out_specs=out_specs, check_vma=False
    )
```

time: 358 us -> 155 us (0.43)
  waiting for transfers between devices: 183 us -> 12.3 us
  local copies, waits for them, and re-layouts: 20.9 us -> 73.1 us
  blocking collectives: 71.6 us -> 25.3 us
  other arithmetic: 46.9 us -> 13.3 us
  starting transfers between devices: 5.62 us -> 20.5 us
  between operations: 14.6 us -> 1.58 us
  matrix products: 12 us -> 0 us
  Pallas kernels: 0 us -> 8.69 us
    psum x2 -> x0, waiting for transfers between devices: 179 us -> none  [on_device(): summed = lax.psum(local_terms, 'date')]
    psum x2 -> x0, blocking collectives: 71.6 us -> none  [spread_rows(): full_spread = lax.psum(spread, 'date')]
    mul x0 -> x3, local copies, waits for them, and re-layouts: none -> 44.5 us  [per_row(): wide = columns[:, None, :, None] * same_part[None, :, None, :]]
    div x20 -> x0, other arithmetic: 24.5 us -> none  [the longest x9 17.5 us: solve_terms(): solved[row_index] = running / lower_factor[row_index, row_index][None]]
    unnamed x0 -> x1, blocking collectives: none -> 15.3 us
    dot_general x6 -> x0, matrix products: 12 us -> none  [the longest x2 7.52 us: residual_power(): jnp.einsum('dk,bkp->bdp', design_rows, coefficient, precision=highest, pr...]
    another operation x3, other arithmetic: 1.79 us -> 11.9 us
    all_to_all x0 -> x1, blocking collectives: none -> 9.99 us  [on_device(): field = lax.all_to_all(variance, ('space', 'date'), 0, 0, tiled=True)]
  transfers between devices with their start and end apart: 6 -> 8, of which waited for: 4 -> 3; matrix products, arithmetic and copies ran while one was open for 1% -> 49% of each run, Pallas kernels for 0% -> 0%
where the time goes in v1:
time: 155 us
  local copies, waits for them, and re-layouts  73.1 us (47%)
  blocking collectives  25.3 us (16%)
  starting transfers between devices  20.5 us (13%)
  other arithmetic  13.3 us (9%)
  waiting for transfers between devices  12.3 us (8%)
  Pallas kernels  8.69 us (6%)
  between operations  1.58 us (1%)
    mul x3, local copies, waits for them, and re-layouts, per_row(): wide = columns[:, None, :, None] * same_part[None, :, None, :]  44.5 us
    unnamed x1, blocking collectives  15.3 us
    another operation x6, local copies, waits for them, and re-layouts  13.5 us
    ppermute x7, starting transfers between devices, on_device(): lax.ppermute(blocks[k], 'date', [(i, i ^ k) for i in range(count)])  12.8 us
    another operation x2, other arithmetic  11.8 us
    unnamed x39, local copies, waits for them, and re-layouts  11.2 us
    all_to_all x1, blocking collectives, on_device(): field = lax.all_to_all(variance, ('space', 'date'), 0, 0, tiled=True)  9.99 us
    all_to_all x1, starting transfers between devices, on_device(): field = lax.all_to_all(variance, ('space', 'date'), 0, 0, tiled=True)  7.73 us
  transfers between devices with their start and end apart: 8, of which 3 were waited for; matrix products, arithmetic and copies ran while one was open for 49% of the time, Pallas kernels for 0%

profile of v1, /device:TPU:0, one launch (start us, length us, event | category | flops | bytes accessed | tf_op | source)
XLA Modules:
  0.0 154.8 jit_solution(17093542903737897188)
XLA Ops:
  0.7 1.3 copy-done
  2.1 1.0 copy-done.1
  3.7 3.0 %collective-permute-start = (bf16[768,128]{1,0:T(8,128)(2,1)S(1)}, bf16[768,128]{1,0:T(8,128)(2,1)S(1)}, u32[]{:S(2)}, u32[]{:S(2)}) collective-permute-start(bf16[768,128]{1,0:T(8,128)(2,1)S(1)} %get-tuple-element.17), channel_id=1, source_target_pairs={{0,1},{1,0},{2,3},{3,2},{4,5},{5,4},{6,7},{7,6},{8,9},{9,8},{10,11... | collective-permute-start | bytes 589832 | tf_op jit(solution)/shard_map/ppermute | solution.py:355
  6.7 1.6 %collective-permute-start.1 = (bf16[768,128]{1,0:T(8,128)(2,1)S(1)}, bf16[768,128]{1,0:T(8,128)(2,1)S(1)}, u32[]{:S(2)}, u32[]{:S(2)}) collective-permute-start(bf16[768,128]{1,0:T(8,128)(2,1)S(1)} %get-tuple-element.18), channel_id=1, source_target_pairs={{0,2},{1,3},{2,0},{3,1},{4,6},{5,7},{6,4},{7,5},{8,10},{9,11},{10,... | collective-permute-start | bytes 589832 | tf_op jit(solution)/shard_map/ppermute | solution.py:355
  8.9 3.1 %collective-permute-start.3 = (bf16[768,128]{1,0:T(8,128)(2,1)S(1)}, bf16[768,128]{1,0:T(8,128)(2,1)S(1)}, u32[]{:S(2)}, u32[]{:S(2)}) collective-permute-start(bf16[768,128]{1,0:T(8,128)(2,1)S(1)} %get-tuple-element.20), channel_id=1, source_target_pairs={{0,4},{1,5},{2,6},{3,7},{4,0},{5,1},{6,2},{7,3},{8,12},{9,13},{10,... | collective-permute-start | bytes 589832 | tf_op jit(solution)/shard_map/ppermute | solution.py:355
  11.9 1.3 collective-permute-start.4
  14.7 15.3 %all-reduce = s32[192]{0:T(256)S(1)} all-reduce(s32[192]{0:T(256)S(1)} %dynamic-update-slice), channel_id=2, replica_groups=mesh['space'=4,'date'=8] {'date'}, use_global_device_ids=true, to_apply=%add | all-reduce | flops 192 | bytes 1536
  32.7 9.2 %multiply_convert_fusion.2 = (bf16[192,4,36,4]{1,0,3,2:T(8,128)(2,1)}, bf16[192,4,36,4]{1,0,3,2:T(8,128)(2,1)}, bf16[192,4,36,4]{1,0,3,2:T(8,128)(2,1)}) fusion(f32[4,4]{0,1:T(4,128)S(1)} %copy-done.13, f32[192,36]{0,1:T(8,128)S(1)} %get-tuple-element.30, f32[192,36]{0,1:T(8,128)S(1)} %get-tuple-element.31, f32[192,36]{0,1:T(8,128)S(1)} %get-tuple-element.32), kind=kLoop, calls=%fused_computation.5 | loop fusion | flops 663552 | bytes 746560 | tf_op jit(solution)/shard_map/convert.14
  41.9 14.8 %mul.226 = bf16[768,144]{0,1:T(8,128)(2,1)} reshape(bf16[192,4,36,4]{1,0,3,2:T(8,128)(2,1)} %get-tuple-element.45) | data formatting | bytes 442368 | tf_op jit(solution)/shard_map/mul | solution.py:363
  56.7 14.8 %mul.220 = bf16[768,144]{0,1:T(8,128)(2,1)} reshape(bf16[192,4,36,4]{1,0,3,2:T(8,128)(2,1)} %get-tuple-element.43) | data formatting | bytes 442368 | tf_op jit(solution)/shard_map/mul | solution.py:363
  71.6 14.8 %mul.223 = bf16[768,144]{0,1:T(8,128)(2,1)} reshape(bf16[192,4,36,4]{1,0,3,2:T(8,128)(2,1)} %get-tuple-element.44) | data formatting | bytes 442368 | tf_op jit(solution)/shard_map/mul | solution.py:363
  86.4 2.7 %multiply_convert_fusion.5 = (bf16[192,4,8,4]{1,0,3,2:T(8,128)(2,1)}, bf16[192,4,8,4]{1,0,3,2:T(8,128)(2,1)}, bf16[192,4,8,4]{1,0,3,2:T(8,128)(2,1)}) fusion(f32[4,4]{0,1:T(4,128)S(1)} %copy-done.13, f32[192,8]{0,1:T(8,128)S(1)} %get-tuple-element.33, f32[192,8]{0,1:T(8,128)S(1)} %get-tuple-element.35, f32[192,8]{0,1:T(8,128)S(1)} %get-tuple-element.34), kind=kLoop, calls=%fused_computation.8 | loop fusion | flops 147456 | bytes 165952 | tf_op jit(solution)/shard_map/convert.20
  89.1 3.8 %reshape.411 = bf16[768,32]{0,1:T(8,128)(2,1)S(1)} reshape(bf16[192,4,8,4]{1,0,3,2:T(8,128)(2,1)} %get-tuple-element.46) | data formatting | bytes 98304 | tf_op jit(solution)/shard_map/convert.20
  93.1 4.0 %reshape.412 = bf16[768,32]{0,1:T(8,128)(2,1)S(1)} reshape(bf16[192,4,8,4]{1,0,3,2:T(8,128)(2,1)} %get-tuple-element.47) | data formatting | bytes 98304 | tf_op jit(solution)/shard_map/convert.19
  98.0 3.8 %reshape.413 = bf16[768,32]{0,1:T(8,128)(2,1)S(1)} reshape(bf16[192,4,8,4]{1,0,3,2:T(8,128)(2,1)} %get-tuple-element.48) | data formatting | bytes 98304 | tf_op jit(solution)/shard_map/convert.18
  102.6 1.4 concatenate.29.refs_10_.refs_7_
  104.1 2.5 %collective-permute-start.5 = (bf16[768,128]{1,0:T(8,128)(2,1)S(1)}, bf16[768,128]{1,0:T(8,128)(2,1)S(1)}, u32[]{:S(2)}, u32[]{:S(2)}) collective-permute-start(bf16[768,128]{1,0:T(8,128)(2,1)S(1)} %get-tuple-element.22), channel_id=1, source_target_pairs={{0,6},{1,7},{2,4},{3,5},{4,2},{5,3},{6,0},{7,1},{8,14},{9,15},{10,... | collective-permute-start | bytes 589832 | tf_op jit(solution)/shard_map/ppermute | solution.py:355
  106.6 1.3 collective-permute-start.6
  108.0 1.2 pad_maximum_fusion.refs_9_.refs_6_
  111.2 2.3 %collective-permute-done.5.refs_6_ = bf16[768,128]{1,0:T(8,128)(2,1)S(1)} collective-permute-done((bf16[768,128]{1,0:T(8,128)(2,1)S(1)}, bf16[768,128]{1,0:T(8,128)(2,1)S(1)}, u32[]{:S(2)}, u32[]{:S(2)}) %collective-permute-start.5) | collective-permute-done | bytes 196640 | tf_op jit(solution)/shard_map/ppermute | solution.py:355
  113.5 2.4 %collective-permute-done.6.refs_7_ = bf16[768,128]{1,0:T(8,128)(2,1)S(1)} collective-permute-done((bf16[768,128]{1,0:T(8,128)(2,1)S(1)}, bf16[768,128]{1,0:T(8,128)(2,1)S(1)}, u32[]{:S(2)}, u32[]{:S(2)}) %collective-permute-start.6) | collective-permute-done | bytes 196640 | tf_op jit(solution)/shard_map/ppermute | solution.py:355
  115.9 0.9 copy-done.3
  116.8 0.9 copy-done.5
  117.7 0.9 copy-done.7
  118.7 0.9 copy-done.9
  119.6 1.9 %first.1 = (bf16[768,896]{1,0:T(8,128)(2,1)S(1)}, bf16[768,128]{1,0:T(8,128)(2,1)S(1)}, f32[768,128]{1,0:T(8,128)S(1)}, f32[32,8,128]{2,1,0:T(8,128)S(1)}) custom-call(bf16[768,128]{1,0:T(8,128)(2,1)S(1)} %get-tuple-element.16.refs_0_, bf16[768,128]{1,0:T(8,128)(2,1)S(1)} %collective-permute-done.refs_1_, bf16[768,128]{1,0:T(8,128)(2,1)S(1)} %copy-done.3, ...), custom_call_target="tpu_custom_call" | custom-call | tf_op jit(solution)/shard_map/first/pallas_call | solution.py:379
  122.8 7.7 %all-to-all-start = ((f32[32,8,128]{2,1,0:T(8,128)}), f32[32,8,128]{2,1,0:T(8,128)S(1)}, u32[]{:S(2)}, u32[]{:S(2)}) async-start(f32[32,8,128]{2,1,0:T(8,128)} %copy-done.12), calls=%async_computation | async-start | bytes 262144 | tf_op jit(solution)/shard_map/all_to_all | solution.py:393
  130.6 7.7 %all-to-all-done.refs_1_ = f32[32,8,128]{2,1,0:T(8,128)S(1)} async-done(((f32[32,8,128]{2,1,0:T(8,128)}), f32[32,8,128]{2,1,0:T(8,128)S(1)}, u32[]{:S(2)}, u32[]{:S(2)}) %all-to-all-start) | async-done | bytes 131104 | tf_op jit(solution)/shard_map/all_to_all | solution.py:393
  138.3 0.9 copy-done.11
  139.2 4.3 %second.1 = (f32[7,8,8,64]{3,2,1,0:T(8,128)}, f32[32,8,128]{2,1,0:T(8,128)S(1)}) custom-call(s32[2]{0:T(128)S(1)} %pad_add_fusion.refs_0_.place_ref, f32[32,8,128]{2,1,0:T(8,128)S(1)} %all-to-all-done.refs_1_, bf16[768,896]{1,0:T(8,128)(2,1)S(1)} %get-tuple-element.25.refs_2_, bf16[768,128]{1,0:T(8,128)(2,1)S(1)} %copy-done.11, ...), custom_call_target="tpu_custom_call" | custom-call | tf_op jit(solution)/shard_map/second/pallas_call | solution.py:394
  143.5 10.0 %all_to_all.10.field_ref = f32[32,8,128]{2,1,0:T(8,128)S(1)} all-to-all(f32[32,8,128]{2,1,0:T(8,128)S(1)} %get-tuple-element.29), channel_id=1, replica_groups=mesh['space'=4,'date'=8] {'space','date'}, dimensions={0} | all-to-all | bytes 262144 | tf_op jit(solution)/shard_map/all_to_all | solution.py:405
  153.5 1.3 last.1
  (66 shorter events, 10.0 us)
Async XLA Ops:
  0.6 12.6 %copy-start.17 = (u32[32]{0:T(128)S(1)}, u32[32]{0:T(128)}, u32[]{:S(2)}) copy-start(u32[32]{0:T(128)} %constant.58) | copy-start | bytes 388
  0.6 30.7 %copy-start.15 = (s32[36]{0:T(128)S(1)}, s32[36]{0:T(128)}, u32[]{:S(2)}) copy-start(s32[36]{0:T(128)} %constant.54) | copy-start | bytes 436
  0.7 31.4 %copy-start.14 = (s32[36]{0:T(128)S(1)}, s32[36]{0:T(128)}, u32[]{:S(2)}) copy-start(s32[36]{0:T(128)} %constant.55) | copy-start | bytes 436
  0.7 32.1 %copy-start.13 = (f32[4,4]{0,1:T(4,128)S(1)}, f32[4,4]{0,1:T(4,128)}, u32[]{:S(2)}) copy-start(f32[4,4]{0,1:T(4,128)} %constant.48.clone) | copy-start | bytes 196
  0.7 13.8 %copy-start.16 = (s32[24]{0:T(128)S(1)}, s32[24]{0:T(128)}, u32[]{:S(2)}) copy-start(s32[24]{0:T(128)} %param.10) | copy-start | bytes 292
  0.7 1.4 copy-start
  2.1 1.0 copy-start.1
  3.7 100.4 %collective-permute-start = (bf16[768,128]{1,0:T(8,128)(2,1)S(1)}, bf16[768,128]{1,0:T(8,128)(2,1)S(1)}, u32[]{:S(2)}, u32[]{:S(2)}) collective-permute-start(bf16[768,128]{1,0:T(8,128)(2,1)S(1)} %get-tuple-element.17), channel_id=1, source_target_pairs={{0,1},{1,0},{2,3},{3,2},{4,5},{5,4},{6,7},{7,6},{8,9},{9,8},{10,11... | collective-permute-start | bytes 589832 | tf_op jit(solution)/shard_map/ppermute | solution.py:355
  6.7 99.9 %collective-permute-start.1 = (bf16[768,128]{1,0:T(8,128)(2,1)S(1)}, bf16[768,128]{1,0:T(8,128)(2,1)S(1)}, u32[]{:S(2)}, u32[]{:S(2)}) collective-permute-start(bf16[768,128]{1,0:T(8,128)(2,1)S(1)} %get-tuple-element.18), channel_id=1, source_target_pairs={{0,2},{1,3},{2,0},{3,1},{4,6},{5,7},{6,4},{7,5},{8,10},{9,11},{10,... | collective-permute-start | bytes 589832 | tf_op jit(solution)/shard_map/ppermute | solution.py:355
  8.2 100.9 %collective-permute-start.2 = (bf16[768,128]{1,0:T(8,128)(2,1)S(1)}, bf16[768,128]{1,0:T(8,128)(2,1)S(1)}, u32[]{:S(2)}, u32[]{:S(2)}) collective-permute-start(bf16[768,128]{1,0:T(8,128)(2,1)S(1)} %get-tuple-element.19), channel_id=1, source_target_pairs={{0,3},{1,2},{2,1},{3,0},{4,7},{5,6},{6,5},{7,4},{8,11},{9,10},{10,... | collective-permute-start | bytes 589832 | tf_op jit(solution)/shard_map/ppermute | solution.py:355
  8.9 101.0 %collective-permute-start.3 = (bf16[768,128]{1,0:T(8,128)(2,1)S(1)}, bf16[768,128]{1,0:T(8,128)(2,1)S(1)}, u32[]{:S(2)}, u32[]{:S(2)}) collective-permute-start(bf16[768,128]{1,0:T(8,128)(2,1)S(1)} %get-tuple-element.20), channel_id=1, source_target_pairs={{0,4},{1,5},{2,6},{3,7},{4,0},{5,1},{6,2},{7,3},{8,12},{9,13},{10,... | collective-permute-start | bytes 589832 | tf_op jit(solution)/shard_map/ppermute | solution.py:355
  11.9 98.6 %collective-permute-start.4 = (bf16[768,128]{1,0:T(8,128)(2,1)S(1)}, bf16[768,128]{1,0:T(8,128)(2,1)S(1)}, u32[]{:S(2)}, u32[]{:S(2)}) collective-permute-start(bf16[768,128]{1,0:T(8,128)(2,1)S(1)} %get-tuple-element.21), channel_id=1, source_target_pairs={{0,5},{1,4},{2,7},{3,6},{4,1},{5,0},{6,3},{7,2},{8,13},{9,12},{10,... | collective-permute-start | bytes 589832 | tf_op jit(solution)/shard_map/ppermute | solution.py:355
  104.1 9.4 %collective-permute-start.5 = (bf16[768,128]{1,0:T(8,128)(2,1)S(1)}, bf16[768,128]{1,0:T(8,128)(2,1)S(1)}, u32[]{:S(2)}, u32[]{:S(2)}) collective-permute-start(bf16[768,128]{1,0:T(8,128)(2,1)S(1)} %get-tuple-element.22), channel_id=1, source_target_pairs={{0,6},{1,7},{2,4},{3,5},{4,2},{5,3},{6,0},{7,1},{8,14},{9,15},{10,... | collective-permute-start | bytes 589832 | tf_op jit(solution)/shard_map/ppermute | solution.py:355
  106.6 1.3 copy-start.2
  106.6 9.3 %collective-permute-start.6 = (bf16[768,128]{1,0:T(8,128)(2,1)S(1)}, bf16[768,128]{1,0:T(8,128)(2,1)S(1)}, u32[]{:S(2)}, u32[]{:S(2)}) collective-permute-start(bf16[768,128]{1,0:T(8,128)(2,1)S(1)} %get-tuple-element.23), channel_id=1, source_target_pairs={{0,7},{1,6},{2,5},{3,4},{4,3},{5,2},{6,1},{7,0},{8,15},{9,14},{10,... | collective-permute-start | bytes 589832 | tf_op jit(solution)/shard_map/ppermute | solution.py:355
  109.2 0.7 copy-start.4
  109.8 0.7 copy-start.6
  110.5 0.7 copy-start.8
  115.9 0.9 copy-start.3
  116.8 0.9 copy-start.5
  117.7 0.9 copy-start.7
  118.7 0.9 copy-start.9
  121.5 0.7 copy-start.10
  122.1 0.7 copy-start.12
  122.8 15.5 %all-to-all-start = ((f32[32,8,128]{2,1,0:T(8,128)}), f32[32,8,128]{2,1,0:T(8,128)S(1)}, u32[]{:S(2)}, u32[]{:S(2)}) async-start(f32[32,8,128]{2,1,0:T(8,128)} %copy-done.12), calls=%async_computation | async-start | bytes 262144 | tf_op jit(solution)/shard_map/all_to_all | solution.py:393
  138.3 0.9 copy-start.11

commit v2 on v1

v2 whole, which is shorter than its diff:
```python
import functools
import math

import jax
import jax.numpy as jnp
from jax import lax
from jax.experimental import pallas as pl
from jax.experimental.pallas import tpu as pltpu
from jax.sharding import PartitionSpec as P

TERMS = 8
LANES = 128
TUKEY = 4.685
RIDGE = 1.0
EPS = 1e-06
VMEM_BYTES = 16 * 1024 * 1024
INFO_ROWS = 16
pairs = [(i, j) for i in range(TERMS) for j in range(i, TERMS)]
f32 = jnp.float32
bf16 = jnp.bfloat16


def split3_kernel(x):
    high = x.astype(bf16)
    rest = x - high.astype(f32)
    mid = rest.astype(bf16)
    low = (rest - mid.astype(f32)).astype(bf16)
    return high, mid, low


def design_info(day_row, dates):
    row = lax.broadcasted_iota(jnp.int32, (TERMS, LANES), 0)
    lane = lax.broadcasted_iota(jnp.int32, (TERMS, LANES), 1)
    day = jnp.broadcast_to(day_row.astype(f32), (TERMS, LANES))
    angle = (row >> 1).astype(f32) * (day * (2.0 * math.pi / 365.25))
    wave = jnp.where((row & 1) == 0, jnp.cos(angle), jnp.sin(angle))
    x = jnp.where(row == 0, 1.0, jnp.where(row == 1, (day - 1825.0) / 1825.0, wave))
    x = jnp.where(lane < dates, x, 0.0)
    high, mid, low = [part.astype(f32) for part in split3_kernel(x)]
    return jnp.concatenate([high + pltpu.roll(low, 64, 1), mid], axis=0).astype(bf16)


def info_kernel(dates, day_ref, out_ref):
    out_ref[...] = design_info(day_ref[...], dates)


def pack_kernel(tiles, me_ref, day_ref, obs_ref, valid_ref, *outs):
    me = me_ref[0]
    odd = lax.rem(me, 2) == 1
    bands = obs_ref.shape[0]
    dates = obs_ref.shape[1]
    half = dates // 2
    info = design_info(day_ref[...], dates)
    for out in outs:
        out[out.shape[0] - INFO_ROWS :, :] = info
    row = lax.broadcasted_iota(jnp.int32, (half, 8, LANES), 1)
    lane = lax.broadcasted_iota(jnp.int32, (half, 8, LANES), 2)
    top = row < 4
    left = lane < 64
    for place, tile_step in enumerate(tiles):
        tile = lax.div(me, 2) ^ tile_step
        start = pl.multiple_of(tile * LANES, LANES)
        for band in range(bands + 1):
            if band < bands:
                block = obs_ref[band, :, :, pl.ds(start, LANES)].astype(f32)
            else:
                block = valid_ref[:, :, pl.ds(start, LANES)].astype(f32)
            block = block.reshape(half, 2, 8, LANES)
            first, second = block[:, 0], block[:, 1]

            def turned(x):
                down = pltpu.roll(x, 4, 1)
                return down, pltpu.roll(x, 64, 2), pltpu.roll(down, 64, 2)

            down_1, side_1, both_1 = turned(first)
            down_2, side_2, both_2 = turned(second)
            even_block = jnp.where(
                top, jnp.where(left, first, both_1), jnp.where(left, down_2, side_2)
            )
            odd_block = jnp.where(
                top, jnp.where(left, side_1, down_1), jnp.where(left, both_2, second)
            )
            same = jnp.where(odd, odd_block, even_block)
            other = jnp.where(odd, even_block, odd_block)
            rows = dates * 4
            outs[2 * place][band * rows : (band + 1) * rows, :] = same.reshape(rows, LANES).astype(
                bf16
            )
            outs[2 * place + 1][band * rows : (band + 1) * rows, :] = other.reshape(
                rows, LANES
            ).astype(bf16)


def packed_blocks(obs, valid, days, count, me, width):
    bands, dates, rows, cols = obs.shape
    group = LANES // width
    parts = rows // group
    vmem = pl.BlockSpec(memory_space=pltpu.VMEM)
    day_row = jnp.pad(days, (0, LANES - dates)).reshape(1, LANES)
    size = (bands + 1) * dates * parts
    if width == 64 and rows == 8:
        shape = jax.ShapeDtypeStruct((size + INFO_ROWS, LANES), bf16)
        blocks = [None] * count
        half = count // 4
        for tiles in (tuple(range(half, 2 * half)), tuple(range(half))):
            given = pl.pallas_call(
                functools.partial(pack_kernel, tiles),
                out_shape=[shape] * (2 * len(tiles)),
                in_specs=[pl.BlockSpec(memory_space=pltpu.SMEM), vmem, vmem, vmem],
                out_specs=[vmem] * (2 * len(tiles)),
                compiler_params=pltpu.CompilerParams(vmem_limit_bytes=VMEM_BYTES),
                name="pack",
            )(me.reshape(1), day_row, obs, valid)
            for place, tile_step in enumerate(tiles):
                blocks[2 * tile_step] = given[2 * place]
                blocks[2 * tile_step + 1] = given[2 * place + 1]
        return blocks
    info = pl.pallas_call(
        functools.partial(info_kernel, dates),
        out_shape=jax.ShapeDtypeStruct((INFO_ROWS, LANES), bf16),
        in_specs=[vmem],
        out_specs=vmem,
        name="info",
    )(day_row)
    whole = jnp.concatenate([obs, valid.astype(bf16)[None]], axis=0)
    whole = whole.reshape(bands + 1, dates, group, parts, count, width)
    whole = whole.transpose(4, 0, 1, 3, 2, 5)
    whole = whole.reshape(count, size, LANES)
    whole = jnp.concatenate(
        [whole, jnp.broadcast_to(info[None], (count, INFO_ROWS, LANES))], axis=1
    )
    return [lax.dynamic_index_in_dim(whole, me ^ k, 0, keepdims=False) for k in range(count)]


def solve(gram, cross, bands):
    lower = {}
    scaled = {}
    inverse = []
    for col in range(TERMS):
        pivot = gram[col, col] + RIDGE
        for inner in range(col):
            pivot = pivot - lower[col, inner] * scaled[col, inner]
        inverse.append(1.0 / pivot)
        for row in range(col + 1, TERMS):
            entry = gram[col, row]
            for inner in range(col):
                entry = entry - lower[row, inner] * scaled[col, inner]
            scaled[row, col] = entry
            lower[row, col] = entry * inverse[col]
    beta = {}
    for band in range(bands):
        forward = []
        for row in range(TERMS):
            running = cross[row, band]
            for inner in range(row):
                running = running - lower[row, inner] * forward[inner]
            forward.append(running)
        solved = [None] * TERMS
        for row in reversed(range(TERMS)):
            running = forward[row] * inverse[row]
            for inner in range(row + 1, TERMS):
                running = running - lower[inner, row] * solved[inner]
            solved[row] = running
        for row in range(TERMS):
            beta[row, band] = solved[row]
    return beta


def dot(a, b):
    return jnp.dot(a, b, preferred_element_type=f32)


def add_parts(total, size):
    return sum(total[i * size : (i + 1) * size] for i in range(total.shape[0] // size))


def dot_nt(a, b):
    return lax.dot_general(a, b, (((1,), (1,)), ((), ())), preferred_element_type=f32)


def one_hot(shape, first, second):
    row = lax.broadcasted_iota(jnp.int32, shape, 0)
    col = lax.broadcasted_iota(jnp.int32, shape, 1)
    return jnp.where(first(row) == second(col), 1.0, 0.0)


def design_of(infos, dates, parts):
    count = len(infos)
    total = count * dates * parts
    wide = -(-count * dates // LANES) * LANES
    shift = parts.bit_length() - 1
    low_bits = parts - 1
    lane = lax.broadcasted_iota(jnp.int32, (TERMS, LANES), 1)
    sums = [jnp.zeros((TERMS, wide), f32) for _ in range(3)]
    for n, info in enumerate(infos):
        info = info.astype(f32)
        top = info[0:TERMS]
        high = jnp.where(lane < 64, top, 0.0)
        low = jnp.where(lane < 64, pltpu.roll(top, 64, 1), 0.0)
        for c, part in enumerate((high, info[TERMS:], low)):
            if wide > LANES:
                part = jnp.concatenate([part, jnp.zeros((TERMS, wide - LANES), f32)], axis=1)
            if n:
                part = pltpu.roll(part, n * dates, 1)
            sums[c] = sums[c] + part
    x = sums[0] + sums[1] + sums[2]
    stacked = jnp.concatenate(sums + [jnp.zeros((TERMS, wide), f32)], axis=0).astype(bf16)
    spread = one_hot((total, wide), lambda t: t >> shift, lambda d: d).astype(bf16)
    size = TERMS * parts
    repeat = one_hot((3 * size, 4 * TERMS), lambda r: r >> shift, lambda c: c).astype(bf16)
    rows = dot(repeat, stacked)
    same = one_hot((3 * size, total), lambda r: r & low_bits, lambda t: t & low_bits)
    left = (dot_nt(rows.astype(bf16), spread) * same).astype(bf16)
    high, mid, low = rows[0:size], rows[size : 2 * size], rows[2 * size :]
    six = jnp.concatenate([high, mid, low, high, mid, high], axis=0).astype(bf16)
    same = one_hot((total, 6 * size), lambda t: t & low_bits, lambda r: r & low_bits)
    x_wide = (dot_nt(spread, six) * same).astype(bf16)
    products = jnp.concatenate(
        [x[i : i + 1] * x[i:] for i in range(TERMS)] + [jnp.zeros((4, wide), f32)], axis=0
    )
    padded = products.shape[0]
    used = len(pairs) * parts
    product_parts = jnp.concatenate(
        [part.astype(f32) for part in split3_kernel(products)], axis=0
    ).astype(bf16)
    gram_left = []
    same = one_hot((used, total), lambda r: r & low_bits, lambda t: t & low_bits)
    for c in range(3):
        repeat = one_hot((used, 3 * padded), lambda r: (r >> shift) + c * padded, lambda n: n)
        rows = dot(repeat.astype(bf16), product_parts)
        gram_left.append((dot_nt(rows.astype(bf16), spread) * same).astype(bf16))
    return left, gram_left, x_wide


def absorb(blocks, bands, dates, parts, outs, product_ref):
    left_ref, gram_left_ref, x_ref, y_ref, mask_ref = outs
    rows = dates * parts
    left, gram_left, x_wide = design_of(
        [block[(bands + 1) * rows :, :] for block in blocks], dates, parts
    )
    left_ref[...] = left
    x_ref[...] = x_wide
    used = len(pairs) * parts
    for c in range(3):
        gram_left_ref[c * used : (c + 1) * used, :] = gram_left[c]
    for n, block in enumerate(blocks):
        here = slice(n * rows, (n + 1) * rows)
        mask = block[bands * rows : (bands + 1) * rows, :]
        mask_ref[here, :] = mask
        for b in range(bands):
            y = block[b * rows : (b + 1) * rows, :]
            y_ref[here, b * LANES : (b + 1) * LANES] = y
            product_ref[here, b * LANES : (b + 1) * LANES] = y * mask
    cross_sum = add_parts(dot(left_ref[...], product_ref[...]), TERMS * parts)
    gram_sum = add_parts(dot(gram_left_ref[...], mask_ref[...]), used)
    return cross_sum, gram_sum


def absorb_kernel(shape, *refs):
    bands, dates, parts = shape
    blocks, outs, sums, product_ref = refs[:-8], refs[-8:-3], refs[-3:-1], refs[-1]
    cross_sum, gram_sum = absorb(blocks, bands, dates, parts, outs, product_ref)
    sums[0][...] = cross_sum
    sums[1][...] = gram_sum


def fit_and_spread(parts, bands, gram_sum, cross_sum, halves):
    gram = {ij: gram_sum[n * parts : (n + 1) * parts] for n, ij in enumerate(pairs)}
    cross = {
        (k, b): cross_sum[k * parts : (k + 1) * parts, b * LANES : (b + 1) * LANES]
        for k in range(TERMS)
        for b in range(bands)
    }
    beta = solve(gram, cross, bands)
    flat = jnp.concatenate(
        [jnp.concatenate([beta[k, b] for k in range(TERMS)], axis=0) for b in range(bands)], axis=1
    )
    high, mid, low = split3_kernel(flat)
    right = jnp.concatenate([high, high, high, mid, mid, low], axis=0)
    step = 96
    spread = jnp.zeros((8, LANES), f32)
    for y_ref, x_ref, power_ref, weight_of in halves:
        for start in range(0, y_ref.shape[0], step):
            here = slice(start, start + step)
            misfit = y_ref[here, :].astype(f32) - dot(x_ref[here, :], right)
            power = jnp.zeros((step, LANES), f32)
            for b in range(bands):
                part = misfit[:, b * LANES : (b + 1) * LANES]
                power = power + part * part
            power = power / bands
            if power_ref is not None:
                power_ref[here, :] = power
            weighted = weight_of(here) * power
            spread = spread + jnp.sum(weighted.reshape(step // 8, 8, LANES), axis=0)
    spread = add_parts(spread, parts)
    return beta, spread / (1.0 + gram[0, 0])


def first_kernel(shape, half_count, *refs):
    bands, dates, parts = shape
    blocks = refs[:half_count]
    early_x, early_y, early_mask, early_cross, early_gram = refs[half_count : half_count + 5]
    outs = refs[half_count + 5 : half_count + 10]
    early_power, late_power, variance_ref, product_ref = refs[half_count + 10 :]
    cross_sum, gram_sum = absorb(blocks, bands, dates, parts, outs, product_ref)
    _, _, x_ref, y_ref, mask_ref = outs
    halves = [
        (early_y, early_x, early_power, lambda here: early_mask[here, :].astype(f32)),
        (y_ref, x_ref, late_power, lambda here: mask_ref[here, :].astype(f32)),
    ]
    _, variance = fit_and_spread(
        parts, bands, gram_sum + early_gram[...], cross_sum + early_cross[...], halves
    )
    for place in range(variance_ref.shape[0]):
        variance_ref[place] = variance


def smoothed(place_ref, field_ref, parts, width, rows, spaces, count):
    group = LANES // width
    space = place_ref[0]
    me = place_ref[1]

    def rows_of(space_now, date_now):
        block = field_ref[space_now * count + date_now]
        return [block if h == 0 else pltpu.roll(block, LANES - h * width, 1) for h in range(group)]

    lane = lax.broadcasted_iota(jnp.int32, (rows, LANES), 1)
    sums = []
    for ds in (-1, 0, 1):
        space_now = jnp.clip(space + ds, 0, spaces - 1)
        row_ok = jnp.where((space + ds >= 0) & (space + ds < spaces), 1.0, 0.0)
        across = jnp.zeros((rows, LANES), f32)
        for dd in (-1, 0, 1):
            date_now = jnp.clip(me + dd, 0, count - 1)
            ok = jnp.where((me + dd >= 0) & (me + dd < count), row_ok, 0.0)
            block = jnp.concatenate(rows_of(space_now, date_now), axis=0)
            block = jnp.where(lane < width, block, 0.0) * ok
            for offset in range(-2, 3):
                shift = dd * width - offset
                if abs(shift) >= width and dd * offset <= 0:
                    continue
                moved = block if shift == 0 else pltpu.roll(block, shift % LANES, 1)
                source = lane + offset - dd * width
                across = across + jnp.where((source >= 0) & (source < width), moved, 0.0)
        sums.append(across)
    tall = jnp.concatenate([sums[0][rows - 2 :], sums[1], sums[2][:2]], axis=0)
    total = tall[0:rows]
    for offset in range(1, 5):
        total = total + tall[offset : offset + rows]
    row_index = lax.broadcasted_iota(jnp.int32, (rows, LANES), 0) + space * rows
    col_index = lane + me * width

    def window(index, whole):
        return (jnp.minimum(index + 2, whole - 1) - jnp.maximum(index - 2, 0) + 1).astype(f32)

    smooth = total / (window(row_index, spaces * rows) * window(col_index, count * width))
    return smooth


def to_lanes(tall, parts, width):
    group = LANES // width
    lane = lax.broadcasted_iota(jnp.int32, (parts, LANES), 1)
    out = tall[0:parts]
    for h in range(1, group):
        moved = pltpu.roll(tall[h * parts : (h + 1) * parts], h * width, 1)
        out = jnp.where(lane >= h * width, moved, out)
    return out


def to_rows(block, width):
    group = LANES // width
    tall = [block if h == 0 else pltpu.roll(block, LANES - h * width, 1) for h in range(group)]
    return jnp.concatenate(tall, axis=0)[:, 0:width]


def second_kernel(shape, *refs):
    bands, parts, width, rows, spaces, count = shape
    place_ref, field_ref = refs[:2]
    halves = [refs[2:8], refs[8:14]]
    coefficient_ref, variance_ref = refs[14:16]
    weight_ref, w_parts, wy_parts = refs[16], refs[17:20], refs[20:23]
    smooth = smoothed(place_ref, field_ref, parts, width, rows, spaces, count)
    smooth = to_lanes(smooth, parts, width)
    scale = 1.0 / (TUKEY * TUKEY * (smooth + EPS))
    scale = jnp.concatenate([scale] * (8 // parts), axis=0)
    half = halves[0][3].shape[0]
    step = 96
    for n, (_, _, _, y_ref, mask_ref, power_ref) in enumerate(halves):
        for start in range(0, half, step):
            here = slice(start, start + step)
            there = slice(n * half + start, n * half + start + step)
            power = power_ref[here, :].reshape(step // 8, 8, LANES)
            left_over = 1.0 - jnp.minimum(power * scale[None], 1.0)
            mask = mask_ref[here, :].astype(f32)
            weight = mask * (left_over * left_over).reshape(step, LANES)
            weight_ref[there, :] = weight
            for ref, part in zip(w_parts, split3_kernel(weight)):
                ref[there, :] = part
            for b in range(bands):
                y = y_ref[here, b * LANES : (b + 1) * LANES].astype(f32)
                for ref, part in zip(wy_parts, split3_kernel(weight * y)):
                    ref[there, b * LANES : (b + 1) * LANES] = part

    def moments(place, b_refs, size):
        total = 0.0
        for n in range(2):
            a_ref = halves[n][place]
            there = slice(n * half, (n + 1) * half)
            total = total + add_parts(dot(a_ref[...], b_refs[0][there, :]), size)
            total = total + add_parts(dot(a_ref[0 : 2 * size, :], b_refs[1][there, :]), size)
            total = total + dot(a_ref[0:size, :], b_refs[2][there, :])
        return total

    cross_sum = moments(0, wy_parts, TERMS * parts)
    gram_sum = moments(1, w_parts, len(pairs) * parts)
    beta, variance = fit_and_spread(
        parts,
        bands,
        gram_sum,
        cross_sum,
        [
            (halves[0][3], halves[0][2], None, lambda here: weight_ref[here, :]),
            (
                halves[1][3],
                halves[1][2],
                None,
                lambda here: weight_ref[here.start + half : here.stop + half, :],
            ),
        ],
    )
    for place in range(variance_ref.shape[0]):
        variance_ref[place] = variance
    for b in range(bands):
        for k in range(TERMS):
            coefficient_ref[b, k] = to_rows(beta[k, b], width)


def last_kernel(shape, place_ref, field_ref, noise_ref):
    bands, parts, width, rows, spaces, count = shape
    smooth = smoothed(place_ref, field_ref, parts, width, rows, spaces, count)
    noise_ref[...] = jnp.sqrt(smooth[:, 0:width] + EPS)


def on_device(obs, valid, days):
    bands, dates, rows, cols = obs.shape
    count = lax.axis_size("date")
    spaces = lax.axis_size("space")
    me = lax.axis_index("date")
    width = cols // count
    group = LANES // width
    parts = rows // group
    half_count = count // 2
    half = half_count * dates * parts
    shape = (bands, parts, width, rows, spaces, count)
    vmem = pl.BlockSpec(memory_space=pltpu.VMEM)
    smem = pl.BlockSpec(memory_space=pltpu.SMEM)
    params = pltpu.CompilerParams(vmem_limit_bytes=VMEM_BYTES)

    blocks = packed_blocks(obs, valid, days, count, me, width)
    received = [blocks[0]] + [None] * (count - 1)
    for k in range(half_count, count):
        received[k] = lax.ppermute(blocks[k], "date", [(i, i ^ k) for i in range(count)])
    for k in range(1, half_count):
        block = blocks[k]
        if k > 1:
            block, received[k - 1] = lax.optimization_barrier((block, received[k - 1]))
        received[k] = lax.ppermute(block, "date", [(i, i ^ k) for i in range(count)])

    wide = (half, bands * LANES)
    narrow = (half, LANES)
    half_shapes = [
        jax.ShapeDtypeStruct((3 * TERMS * parts, half), bf16),
        jax.ShapeDtypeStruct((3 * len(pairs) * parts, half), bf16),
        jax.ShapeDtypeStruct((half, 6 * TERMS * parts), bf16),
        jax.ShapeDtypeStruct(wide, bf16),
        jax.ShapeDtypeStruct(narrow, bf16),
    ]
    sums = [
        jax.ShapeDtypeStruct((TERMS * parts, bands * LANES), f32),
        jax.ShapeDtypeStruct((len(pairs) * parts, LANES), f32),
    ]
    power = jax.ShapeDtypeStruct(narrow, f32)
    send = jax.ShapeDtypeStruct((spaces * count, parts, LANES), f32)
    *early, early_cross, early_gram = pl.pallas_call(
        functools.partial(absorb_kernel, (bands, dates, parts)),
        out_shape=half_shapes + sums,
        in_specs=[vmem] * half_count,
        out_specs=[vmem] * 7,
        scratch_shapes=[pltpu.VMEM(wide, bf16)],
        compiler_params=params,
        name="absorb",
    )(*received[:half_count])
    *late, early_power, late_power, variance = pl.pallas_call(
        functools.partial(first_kernel, (bands, dates, parts), half_count),
        out_shape=half_shapes + [power, power, send],
        in_specs=[vmem] * (half_count + 5),
        out_specs=[vmem] * 8,
        scratch_shapes=[pltpu.VMEM(wide, bf16)],
        compiler_params=params,
        name="first",
    )(*received[half_count:], early[2], early[3], early[4], early_cross, early_gram)

    place = jnp.stack([lax.axis_index("space"), me]).astype(jnp.int32)
    field = lax.all_to_all(variance, ("space", "date"), 0, 0, tiled=True)
    coefficients, variance = pl.pallas_call(
        functools.partial(second_kernel, shape),
        out_shape=[jax.ShapeDtypeStruct((bands, TERMS, rows, width), f32), send],
        in_specs=[smem] + [vmem] * 13,
        out_specs=[vmem] * 2,
        scratch_shapes=[pltpu.VMEM((2 * half, LANES), f32)]
        + [pltpu.VMEM((2 * half, LANES), bf16)] * 3
        + [pltpu.VMEM((2 * half, bands * LANES), bf16)] * 3,
        compiler_params=params,
        name="second",
    )(place, field, *early, early_power, *late, late_power)
    field = lax.all_to_all(variance, ("space", "date"), 0, 0, tiled=True)
    noise = pl.pallas_call(
        functools.partial(last_kernel, shape),
        out_shape=jax.ShapeDtypeStruct((rows, width), f32),
        in_specs=[smem, vmem],
        out_specs=vmem,
        compiler_params=params,
        name="last",
    )(place, field)
    return coefficients, noise


def solution(mesh):
    in_specs = (P(None, "date", "space", None), P("date", "space", None), P("date"))
    out_specs = (P(None, None, "space", "date"), P("space", "date"))
    return jax.shard_map(
        on_device, mesh=mesh, in_specs=in_specs, out_specs=out_specs, check_vma=False
    )
```

time: 155 us -> 85 us (0.55)
  local copies, waits for them, and re-layouts: 73.1 us -> 2.99 us
  waiting for transfers between devices: 12.3 us -> 36.3 us
  blocking collectives: 25.3 us -> 8.95 us
  other arithmetic: 13.3 us -> 0.08 us
  starting transfers between devices: 20.5 us -> 25.2 us
  Pallas kernels: 8.69 us -> 10.6 us
    mul x3 -> x0, local copies, waits for them, and re-layouts: 44.5 us -> none  [per_row(): wide = columns[:, None, :, None] * same_part[None, :, None, :]]
    ppermute x7 -> x4, waiting for transfers between devices: 4.68 us -> 20.3 us  [on_device(): lax.ppermute(blocks[k], 'date', [(i, i ^ k) for i in range(count)])]
    unnamed x1 -> x0, blocking collectives: 15.3 us -> none
    another operation x8 -> x0, local copies, waits for them, and re-layouts: 13.5 us -> none
    another operation x2 -> x0, other arithmetic: 11.8 us -> none
    unnamed x39 -> x4, local copies, waits for them, and re-layouts: 11.2 us -> 2.33 us
    ppermute x0 -> x3, waiting for transfers between devices: none -> 8.73 us  [on_device(): lax.ppermute(block, 'date', [(i, i ^ k) for i in range(count)])]
    ppermute x0 -> x3, starting transfers between devices: none -> 7.26 us  [on_device(): lax.ppermute(block, 'date', [(i, i ^ k) for i in range(count)])]
  transfers between devices with their start and end apart: 8 -> 8, of which waited for: 3 -> 5; matrix products, arithmetic and copies ran while one was open for 49% -> 0% of each run, Pallas kernels for 0% -> 2%
where the time goes in v2:
time: 85 us; the launch traced here: 84.7 us
  waiting for transfers between devices  36.3 us (43%)
  starting transfers between devices  25.2 us (30%)
  Pallas kernels  10.6 us (12%)
  blocking collectives  8.95 us (11%)
  local copies, waits for them, and re-layouts  2.99 us (4%)
    ppermute x4, waiting for transfers between devices, on_device(): lax.ppermute(blocks[k], 'date', [(i, i ^ k) for i in range(count)])  20.3 us
    all_to_all x1, starting transfers between devices, on_device(): field = lax.all_to_all(variance, ('space', 'date'), 0, 0, tiled=True)  10.3 us
    all_to_all x1, blocking collectives, on_device(): field = lax.all_to_all(variance, ('space', 'date'), 0, 0, tiled=True)  8.95 us
    ppermute x3, waiting for transfers between devices, on_device(): lax.ppermute(block, 'date', [(i, i ^ k) for i in range(count)])  8.73 us
    ppermute x4, starting transfers between devices, on_device(): lax.ppermute(blocks[k], 'date', [(i, i ^ k) for i in range(count)])  7.65 us
    ppermute x3, starting transfers between devices, on_device(): lax.ppermute(block, 'date', [(i, i ^ k) for i in range(count)])  7.26 us
    all_to_all x1, waiting for transfers between devices, on_device(): field = lax.all_to_all(variance, ('space', 'date'), 0, 0, tiled=True)  7.2 us
    pallas_call x1, Pallas kernels, on_device(): pl.pallas_call(functools.partial(second_kernel, shape), out_shape=[jax.Sh...  4.15 us
  transfers between devices with their start and end apart: 8, of which 5 were waited for; matrix products, arithmetic and copies ran while one was open for 0% of the time, Pallas kernels for 2%

profile of v2, /device:TPU:0, one launch (start us, length us, event | category | flops | bytes accessed | tf_op | source)
XLA Modules:
  0.0 84.7 jit_solution(15263009119018698874)
XLA Ops:
  0.6 0.7 pad_bitcast_fusion.day_ref
  1.3 0.0 copy-start
  1.3 1.3 %copy-done = bf16[7,24,8,512]{3,2,1,0:T(8,128)(2,1)S(1)} copy-done((bf16[7,24,8,512]{3,2,1,0:T(8,128)(2,1)S(1)}, bf16[7,24,8,512]{3,2,1,0:T(8,128)(2,1)}, u32[]{:S(2)}) %copy-start) | copy-done | bytes 1376280
  2.6 0.0 copy-start.1
  2.6 1.0 %copy-done.1 = s32[24,8,512]{2,1,0:T(8,128)S(1)} copy-done((s32[24,8,512]{2,1,0:T(8,128)S(1)}, s32[24,8,512]{2,1,0:T(8,128)}, u32[]{:S(2)}) %copy-start.1) | copy-done | bytes 393240
  3.6 0.6 pack.3
  4.2 3.0 %collective-permute-start.4 = (bf16[784,128]{1,0:T(8,128)(2,1)S(1)}, bf16[784,128]{1,0:T(8,128)(2,1)S(1)}, u32[]{:S(2)}, u32[]{:S(2)}) collective-permute-start(bf16[784,128]{1,0:T(8,128)(2,1)S(1)} %get-tuple-element.37), channel_id=1, source_target_pairs={{0,1},{1,0},{2,3},{3,2},{4,5},{5,4},{6,7},{7,6},{8,9},{9,8},{10,11... | collective-permute-start | bytes 602120 | tf_op jit(solution)/shard_map/ppermute | solution.py:467
  7.2 5.0 %collective-permute-done.4.refs_1_ = bf16[784,128]{1,0:T(8,128)(2,1)S(1)} collective-permute-done((bf16[784,128]{1,0:T(8,128)(2,1)S(1)}, bf16[784,128]{1,0:T(8,128)(2,1)S(1)}, u32[]{:S(2)}, u32[]{:S(2)}) %collective-permute-start.4) | collective-permute-done | bytes 200736 | tf_op jit(solution)/shard_map/ppermute | solution.py:467
  12.2 1.8 %collective-permute-start.5 = (bf16[784,128]{1,0:T(8,128)(2,1)S(1)}, bf16[784,128]{1,0:T(8,128)(2,1)S(1)}, u32[]{:S(2)}, u32[]{:S(2)}) collective-permute-start(bf16[784,128]{1,0:T(8,128)(2,1)S(1)} %get-tuple-element.40), channel_id=1, source_target_pairs={{0,2},{1,3},{2,0},{3,1},{4,6},{5,7},{6,4},{7,5},{8,10},{9,11},{10,... | collective-permute-start | bytes 602120 | tf_op jit(solution)/shard_map/ppermute | solution.py:467
  14.1 0.6 pack.2
  14.7 3.7 %collective-permute-done.5.refs_2_ = bf16[784,128]{1,0:T(8,128)(2,1)S(1)} collective-permute-done((bf16[784,128]{1,0:T(8,128)(2,1)S(1)}, bf16[784,128]{1,0:T(8,128)(2,1)S(1)}, u32[]{:S(2)}, u32[]{:S(2)}) %collective-permute-start.5) | collective-permute-done | bytes 200736 | tf_op jit(solution)/shard_map/ppermute | solution.py:467
  18.4 2.4 %collective-permute-start.6 = (bf16[784,128]{1,0:T(8,128)(2,1)S(1)}, bf16[784,128]{1,0:T(8,128)(2,1)S(1)}, u32[]{:S(2)}, u32[]{:S(2)}) collective-permute-start(bf16[784,128]{1,0:T(8,128)(2,1)S(1)} %get-tuple-element.42), channel_id=1, source_target_pairs={{0,3},{1,2},{2,1},{3,0},{4,7},{5,6},{6,5},{7,4},{8,11},{9,10},{10,... | collective-permute-start | bytes 602120 | tf_op jit(solution)/shard_map/ppermute | solution.py:467
  20.8 2.6 %collective-permute-start = (bf16[784,128]{1,0:T(8,128)(2,1)S(1)}, bf16[784,128]{1,0:T(8,128)(2,1)S(1)}, u32[]{:S(2)}, u32[]{:S(2)}) collective-permute-start(bf16[784,128]{1,0:T(8,128)(2,1)S(1)} %get-tuple-element.31), channel_id=1, source_target_pairs={{0,4},{1,5},{2,6},{3,7},{4,0},{5,1},{6,2},{7,3},{8,12},{9,13},{10,... | collective-permute-start | bytes 602120 | tf_op jit(solution)/shard_map/ppermute | solution.py:462
  23.4 0.3 collective-permute-start.1
  23.7 2.5 %collective-permute-start.2 = (bf16[784,128]{1,0:T(8,128)(2,1)S(1)}, bf16[784,128]{1,0:T(8,128)(2,1)S(1)}, u32[]{:S(2)}, u32[]{:S(2)}) collective-permute-start(bf16[784,128]{1,0:T(8,128)(2,1)S(1)} %get-tuple-element.33), channel_id=1, source_target_pairs={{0,6},{1,7},{2,4},{3,5},{4,2},{5,3},{6,0},{7,1},{8,14},{9,15},{10,... | collective-permute-start | bytes 602120 | tf_op jit(solution)/shard_map/ppermute | solution.py:462
  26.2 2.3 %collective-permute-start.3 = (bf16[784,128]{1,0:T(8,128)(2,1)S(1)}, bf16[784,128]{1,0:T(8,128)(2,1)S(1)}, u32[]{:S(2)}, u32[]{:S(2)}) collective-permute-start(bf16[784,128]{1,0:T(8,128)(2,1)S(1)} %get-tuple-element.34), channel_id=1, source_target_pairs={{0,7},{1,6},{2,5},{3,4},{4,3},{5,2},{6,1},{7,0},{8,15},{9,14},{10,... | collective-permute-start | bytes 602120 | tf_op jit(solution)/shard_map/ppermute | solution.py:462
  28.5 0.0 collective-permute-done.6.refs_3_
  28.5 1.2 %absorb.1 = (bf16[96,384]{1,0:T(8,128)(2,1)S(1)}, bf16[432,384]{1,0:T(8,128)(2,1)S(1)}, bf16[384,192]{1,0:T(8,128)(2,1)S(1)}, bf16[384,896]{1,0:T(8,128)(2,1)S(1...) custom-call(bf16[784,128]{1,0:T(8,128)(2,1)S(1)} %get-tuple-element.35.refs_0_, ...), custom_call_target="tpu_custom_call" | custom-call | tf_op jit(solution)/shard_map/absorb/pallas_call | solution.py:484
  29.7 16.1 %collective-permute-done.refs_0_ = bf16[784,128]{1,0:T(8,128)(2,1)S(1)} collective-permute-done((bf16[784,128]{1,0:T(8,128)(2,1)S(1)}, bf16[784,128]{1,0:T(8,128)(2,1)S(1)}, u32[]{:S(2)}, u32[]{:S(2)}) %collective-permute-start) | collective-permute-done | bytes 200736 | tf_op jit(solution)/shard_map/ppermute | solution.py:462
  45.8 4.2 %collective-permute-done.1.refs_1_ = bf16[784,128]{1,0:T(8,128)(2,1)S(1)} collective-permute-done((bf16[784,128]{1,0:T(8,128)(2,1)S(1)}, bf16[784,128]{1,0:T(8,128)(2,1)S(1)}, u32[]{:S(2)}, u32[]{:S(2)}) %collective-permute-start.1) | collective-permute-done | bytes 200736 | tf_op jit(solution)/shard_map/ppermute | solution.py:462
  50.1 0.0 collective-permute-done.2.refs_2_
  50.1 0.0 collective-permute-done.3.refs_3_
  50.1 2.7 %first.1 = (bf16[96,384]{1,0:T(8,128)(2,1)S(1)}, bf16[432,384]{1,0:T(8,128)(2,1)S(1)}, bf16[384,192]{1,0:T(8,128)(2,1)S(1)}, bf16[384,896]{1,0:T(8,128)(2,1)S(1)...) custom-call(bf16[784,128]{1,0:T(8,128)(2,1)S(1)} %collective-permute-d, ...), custom_call_target="tpu_custom_call" | custom-call | tf_op jit(solution)/shard_map/first/pallas_call | solution.py:493
  52.7 10.3 %all-to-all-start = ((f32[32,4,128]{2,1,0:T(4,128)}), f32[32,4,128]{2,1,0:T(4,128)S(1)}, u32[]{:S(2)}, u32[]{:S(2)}) async-start(f32[32,4,128]{2,1,0:T(4,128)} %get-tuple-element.48), calls=%async_computation | async-start | bytes 131072 | tf_op jit(solution)/shard_map/all_to_all | solution.py:504
  63.0 0.1 pad_add_fusion.refs_0_.place_ref
  63.1 7.2 %all-to-all-done.refs_1_ = f32[32,4,128]{2,1,0:T(4,128)S(1)} async-done(((f32[32,4,128]{2,1,0:T(4,128)}), f32[32,4,128]{2,1,0:T(4,128)S(1)}, u32[]{:S(2)}, u32[]{:S(2)}) %all-to-all-start) | async-done | bytes 65568 | tf_op jit(solution)/shard_map/all_to_all | solution.py:504
  70.3 4.2 %second.1 = (f32[7,8,8,64]{3,2,1,0:T(8,128)}, f32[32,4,128]{2,1,0:T(4,128)S(1)}) custom-call(s32[2]{0:T(128)S(1)} %pad_add_fusion.refs_0_.place_ref, f32[32,4,128]{2,1,0:T(4,128)S(1)} %all-to-all-done.refs_1_, bf16[96,384]{1,0:T(8,128)(2,1)S(1)} %get-tuple-element.49.refs_2_, bf16[432,384]{1,0:T(8,128)(2,1)S(1)} %get-tuple-element.50.refs_3_, ...), custom_call_target="tpu_custom_call" | custom-call | tf_op jit(solution)/shard_map/second/pallas_call | solution.py:505
  74.5 9.0 %all_to_all.10.field_ref = f32[32,4,128]{2,1,0:T(4,128)S(1)} all-to-all(f32[32,4,128]{2,1,0:T(4,128)S(1)} %get-tuple-element.59), channel_id=1, replica_groups=mesh['space'=4,'date'=8] {'space','date'}, dimensions={0} | all-to-all | bytes 131072 | tf_op jit(solution)/shard_map/all_to_all | solution.py:516
  83.4 1.3 %last.1 = f32[8,64]{1,0:T(8,128)} custom-call(s32[2]{0:T(128)S(1)} %pad_add_fusion.refs_0_.place_ref, f32[32,4,128]{2,1,0:T(4,128)S(1)} %all_to_all.10.field_ref), custom_call_target="tpu_custom_call" | custom-call | tf_op jit(solution)/shard_map/last/pallas_call | solution.py:517
Async XLA Ops:
  1.3 1.3 %copy-start = (bf16[7,24,8,512]{3,2,1,0:T(8,128)(2,1)S(1)}, bf16[7,24,8,512]{3,2,1,0:T(8,128)(2,1)}, u32[]{:S(2)}) copy-start(bf16[7,24,8,512]{3,2,1,0:T(8,128)(2,1)} %obs_ref.3) | copy-start | bytes 4128772
  2.6 1.0 %copy-start.1 = (s32[24,8,512]{2,1,0:T(8,128)S(1)}, s32[24,8,512]{2,1,0:T(8,128)}, u32[]{:S(2)}) copy-start(s32[24,8,512]{2,1,0:T(8,128)} %valid_ref.3) | copy-start | bytes 1179652
  4.2 8.0 %collective-permute-start.4 = (bf16[784,128]{1,0:T(8,128)(2,1)S(1)}, bf16[784,128]{1,0:T(8,128)(2,1)S(1)}, u32[]{:S(2)}, u32[]{:S(2)}) collective-permute-start(bf16[784,128]{1,0:T(8,128)(2,1)S(1)} %get-tuple-element.37), channel_id=1, source_target_pairs={{0,1},{1,0},{2,3},{3,2},{4,5},{5,4},{6,7},{7,6},{8,9},{9,8},{10,11... | collective-permute-start | bytes 602120 | tf_op jit(solution)/shard_map/ppermute | solution.py:467
  12.2 6.2 %collective-permute-start.5 = (bf16[784,128]{1,0:T(8,128)(2,1)S(1)}, bf16[784,128]{1,0:T(8,128)(2,1)S(1)}, u32[]{:S(2)}, u32[]{:S(2)}) collective-permute-start(bf16[784,128]{1,0:T(8,128)(2,1)S(1)} %get-tuple-element.40), channel_id=1, source_target_pairs={{0,2},{1,3},{2,0},{3,1},{4,6},{5,7},{6,4},{7,5},{8,10},{9,11},{10,... | collective-permute-start | bytes 602120 | tf_op jit(solution)/shard_map/ppermute | solution.py:467
  18.4 10.1 %collective-permute-start.6 = (bf16[784,128]{1,0:T(8,128)(2,1)S(1)}, bf16[784,128]{1,0:T(8,128)(2,1)S(1)}, u32[]{:S(2)}, u32[]{:S(2)}) collective-permute-start(bf16[784,128]{1,0:T(8,128)(2,1)S(1)} %get-tuple-element.42), channel_id=1, source_target_pairs={{0,3},{1,2},{2,1},{3,0},{4,7},{5,6},{6,5},{7,4},{8,11},{9,10},{10,... | collective-permute-start | bytes 602120 | tf_op jit(solution)/shard_map/ppermute | solution.py:467
  20.8 25.0 %collective-permute-start = (bf16[784,128]{1,0:T(8,128)(2,1)S(1)}, bf16[784,128]{1,0:T(8,128)(2,1)S(1)}, u32[]{:S(2)}, u32[]{:S(2)}) collective-permute-start(bf16[784,128]{1,0:T(8,128)(2,1)S(1)} %get-tuple-element.31), channel_id=1, source_target_pairs={{0,4},{1,5},{2,6},{3,7},{4,0},{5,1},{6,2},{7,3},{8,12},{9,13},{10,... | collective-permute-start | bytes 602120 | tf_op jit(solution)/shard_map/ppermute | solution.py:462
  23.4 26.6 %collective-permute-start.1 = (bf16[784,128]{1,0:T(8,128)(2,1)S(1)}, bf16[784,128]{1,0:T(8,128)(2,1)S(1)}, u32[]{:S(2)}, u32[]{:S(2)}) collective-permute-start(bf16[784,128]{1,0:T(8,128)(2,1)S(1)} %get-tuple-element.32), channel_id=1, source_target_pairs={{0,5},{1,4},{2,7},{3,6},{4,1},{5,0},{6,3},{7,2},{8,13},{9,12},{10,... | collective-permute-start | bytes 602120 | tf_op jit(solution)/shard_map/ppermute | solution.py:462
  23.7 26.3 %collective-permute-start.2 = (bf16[784,128]{1,0:T(8,128)(2,1)S(1)}, bf16[784,128]{1,0:T(8,128)(2,1)S(1)}, u32[]{:S(2)}, u32[]{:S(2)}) collective-permute-start(bf16[784,128]{1,0:T(8,128)(2,1)S(1)} %get-tuple-element.33), channel_id=1, source_target_pairs={{0,6},{1,7},{2,4},{3,5},{4,2},{5,3},{6,0},{7,1},{8,14},{9,15},{10,... | collective-permute-start | bytes 602120 | tf_op jit(solution)/shard_map/ppermute | solution.py:462
  26.2 23.8 %collective-permute-start.3 = (bf16[784,128]{1,0:T(8,128)(2,1)S(1)}, bf16[784,128]{1,0:T(8,128)(2,1)S(1)}, u32[]{:S(2)}, u32[]{:S(2)}) collective-permute-start(bf16[784,128]{1,0:T(8,128)(2,1)S(1)} %get-tuple-element.34), channel_id=1, source_target_pairs={{0,7},{1,6},{2,5},{3,4},{4,3},{5,2},{6,1},{7,0},{8,15},{9,14},{10,... | collective-permute-start | bytes 602120 | tf_op jit(solution)/shard_map/ppermute | solution.py:462
  52.7 17.6 %all-to-all-start = ((f32[32,4,128]{2,1,0:T(4,128)}), f32[32,4,128]{2,1,0:T(4,128)S(1)}, u32[]{:S(2)}, u32[]{:S(2)}) async-start(f32[32,4,128]{2,1,0:T(4,128)} %get-tuple-element.48), calls=%async_computation | async-start | bytes 131072 | tf_op jit(solution)/shard_map/all_to_all | solution.py:504

commit v3 on v2

--- a/solution.py
+++ b/solution.py
@@ -15,6 +15,7 @@
 EPS = 1e-06
 VMEM_BYTES = 16 * 1024 * 1024
 INFO_ROWS = 16
+PACK_VMEM_BYTES = 60 * 1024 * 1024
 pairs = [(i, j) for i in range(TERMS) for j in range(i, TERMS)]
 f32 = jnp.float32
 bf16 = jnp.bfloat16
@@ -28,10 +29,13 @@
     return high, mid, low
 
 
-def design_info(day_row, dates):
+def design_info(day_ref, dates):
     row = lax.broadcasted_iota(jnp.int32, (TERMS, LANES), 0)
     lane = lax.broadcasted_iota(jnp.int32, (TERMS, LANES), 1)
-    day = jnp.broadcast_to(day_row.astype(f32), (TERMS, LANES))
+    day = jnp.zeros((TERMS, LANES), jnp.int32)
+    for n in range(dates):
+        day = jnp.where(lane == n, day_ref[n], day)
+    day = day.astype(f32)
     angle = (row >> 1).astype(f32) * (day * (2.0 * math.pi / 365.25))
     wave = jnp.where((row & 1) == 0, jnp.cos(angle), jnp.sin(angle))
     x = jnp.where(row == 0, 1.0, jnp.where(row == 1, (day - 1825.0) / 1825.0, wave))
@@ -41,31 +45,47 @@
 
 
 def info_kernel(dates, day_ref, out_ref):
-    out_ref[...] = design_info(day_ref[...], dates)
-
-
-def pack_kernel(tiles, me_ref, day_ref, obs_ref, valid_ref, *outs):
-    me = me_ref[0]
+    out_ref[...] = design_info(day_ref, dates)
+
+
+def pack_kernel(count, day_ref, obs_ref, valid_ref, *refs):
+    half = count // 2
+    outs = refs[:count]
+    obs_here, valid_here, out_here, in_sems, out_sems = refs[count:]
+    me = lax.axis_index("date")
     odd = lax.rem(me, 2) == 1
-    bands = obs_ref.shape[0]
-    dates = obs_ref.shape[1]
-    half = dates // 2
-    info = design_info(day_ref[...], dates)
-    for out in outs:
-        out[out.shape[0] - INFO_ROWS :, :] = info
-    row = lax.broadcasted_iota(jnp.int32, (half, 8, LANES), 1)
-    lane = lax.broadcasted_iota(jnp.int32, (half, 8, LANES), 2)
+    bands, dates = obs_ref.shape[:2]
+    rows = dates * 4
+    steps = (*range(half // 2, half), *range(half // 2))
+    arrivals = []
+    for place, step in enumerate(steps):
+        tile = lax.div(me, 2) ^ step
+        lanes = pl.ds(pl.multiple_of(tile * LANES, LANES), LANES)
+        arrivals.append(
+            (
+                pltpu.make_async_copy(
+                    obs_ref.at[:, :, :, lanes], obs_here.at[place], in_sems.at[2 * place]
+                ),
+                pltpu.make_async_copy(
+                    valid_ref.at[:, :, lanes], valid_here.at[place], in_sems.at[2 * place + 1]
+                ),
+            )
+        )
+        for copy in arrivals[place]:
+            copy.start()
+    info = design_info(day_ref, dates)
+    pairs_of_dates = dates // 2
+    row = lax.broadcasted_iota(jnp.int32, (pairs_of_dates, 8, LANES), 1)
+    lane = lax.broadcasted_iota(jnp.int32, (pairs_of_dates, 8, LANES), 2)
     top = row < 4
     left = lane < 64
-    for place, tile_step in enumerate(tiles):
-        tile = lax.div(me, 2) ^ tile_step
-        start = pl.multiple_of(tile * LANES, LANES)
+    leaving = []
+    for place, step in enumerate(steps):
+        for copy in arrivals[place]:
+            copy.wait()
         for band in range(bands + 1):
-            if band < bands:
-                block = obs_ref[band, :, :, pl.ds(start, LANES)].astype(f32)
-            else:
-                block = valid_ref[:, :, pl.ds(start, LANES)].astype(f32)
-            block = block.reshape(half, 2, 8, LANES)
+            block = (obs_here[place, band] if band < bands else valid_here[place]).astype(f32)
+            block = block.reshape(pairs_of_dates, 2, 8, LANES)
             first, second = block[:, 0], block[:, 1]
 
             def turned(x):
@@ -82,13 +102,19 @@
             )
             same = jnp.where(odd, odd_block, even_block)
             other = jnp.where(odd, even_block, odd_block)
-            rows = dates * 4
-            outs[2 * place][band * rows : (band + 1) * rows, :] = same.reshape(rows, LANES).astype(
-                bf16
+            here = slice(band * rows, (band + 1) * rows)
+            out_here[2 * place, here, :] = same.reshape(rows, LANES).astype(bf16)
+            out_here[2 * place + 1, here, :] = other.reshape(rows, LANES).astype(bf16)
+        for n in (0, 1):
+            out_here[2 * place + n, (bands + 1) * rows :, :] = info
+            leaving.append(
+                pltpu.make_async_copy(
+                    out_here.at[2 * place + n], outs[2 * step + n], out_sems.at[2 * place + n]
+                )
             )
-            outs[2 * place + 1][band * rows : (band + 1) * rows, :] = other.reshape(
-                rows, LANES
-            ).astype(bf16)
+            leaving[-1].start()
+    for copy in leaving:
+        copy.wait()
 
 
 def packed_blocks(obs, valid, days, count, me, width):
@@ -96,32 +122,34 @@
     group = LANES // width
     parts = rows // group
     vmem = pl.BlockSpec(memory_space=pltpu.VMEM)
-    day_row = jnp.pad(days, (0, LANES - dates)).reshape(1, LANES)
+    smem = pl.BlockSpec(memory_space=pltpu.SMEM)
     size = (bands + 1) * dates * parts
+    half = count // 2
     if width == 64 and rows == 8:
         shape = jax.ShapeDtypeStruct((size + INFO_ROWS, LANES), bf16)
-        blocks = [None] * count
-        half = count // 4
-        for tiles in (tuple(range(half, 2 * half)), tuple(range(half))):
-            given = pl.pallas_call(
-                functools.partial(pack_kernel, tiles),
-                out_shape=[shape] * (2 * len(tiles)),
-                in_specs=[pl.BlockSpec(memory_space=pltpu.SMEM), vmem, vmem, vmem],
-                out_specs=[vmem] * (2 * len(tiles)),
-                compiler_params=pltpu.CompilerParams(vmem_limit_bytes=VMEM_BYTES),
-                name="pack",
-            )(me.reshape(1), day_row, obs, valid)
-            for place, tile_step in enumerate(tiles):
-                blocks[2 * tile_step] = given[2 * place]
-                blocks[2 * tile_step + 1] = given[2 * place + 1]
-        return blocks
+        hbm = pl.BlockSpec(memory_space=pltpu.HBM)
+        return pl.pallas_call(
+            functools.partial(pack_kernel, count),
+            out_shape=[shape] * count,
+            in_specs=[smem, hbm, hbm],
+            out_specs=[hbm] * count,
+            scratch_shapes=[
+                pltpu.VMEM((half, bands, dates, rows, LANES), bf16),
+                pltpu.VMEM((half, dates, rows, LANES), jnp.int32),
+                pltpu.VMEM((count, size + INFO_ROWS, LANES), bf16),
+                pltpu.SemaphoreType.DMA((count,)),
+                pltpu.SemaphoreType.DMA((count,)),
+            ],
+            compiler_params=pltpu.CompilerParams(vmem_limit_bytes=PACK_VMEM_BYTES),
+            name="pack",
+        )(days, obs, valid)
     info = pl.pallas_call(
         functools.partial(info_kernel, dates),
         out_shape=jax.ShapeDtypeStruct((INFO_ROWS, LANES), bf16),
-        in_specs=[vmem],
+        in_specs=[smem],
         out_specs=vmem,
         name="info",
-    )(day_row)
+    )(days)
     whole = jnp.concatenate([obs, valid.astype(bf16)[None]], axis=0)
     whole = whole.reshape(bands + 1, dates, group, parts, count, width)
     whole = whole.transpose(4, 0, 1, 3, 2, 5)
@@ -256,15 +284,23 @@
     return cross_sum, gram_sum
 
 
+def single_blocks(refs):
+    blocks = []
+    for ref in refs:
+        blocks += [ref] if len(ref.shape) == 2 else [ref.at[n] for n in range(ref.shape[0])]
+    return blocks
+
+
 def absorb_kernel(shape, *refs):
     bands, dates, parts = shape
-    blocks, outs, sums, product_ref = refs[:-8], refs[-8:-3], refs[-3:-1], refs[-1]
+    outs, sums, product_ref = refs[-8:-3], refs[-3:-1], refs[-1]
+    blocks = single_blocks(refs[:-8])
     cross_sum, gram_sum = absorb(blocks, bands, dates, parts, outs, product_ref)
     sums[0][...] = cross_sum
     sums[1][...] = gram_sum
 
 
-def fit_and_spread(parts, bands, gram_sum, cross_sum, halves):
+def fit_and_spread(parts, bands, gram_sum, cross_sum, groups):
     gram = {ij: gram_sum[n * parts : (n + 1) * parts] for n, ij in enumerate(pairs)}
     cross = {
         (k, b): cross_sum[k * parts : (k + 1) * parts, b * LANES : (b + 1) * LANES]
@@ -279,7 +315,7 @@
     right = jnp.concatenate([high, high, high, mid, mid, low], axis=0)
     step = 96
     spread = jnp.zeros((8, LANES), f32)
-    for y_ref, x_ref, power_ref, weight_of in halves:
+    for y_ref, x_ref, power_ref, weight_of in groups:
         for start in range(0, y_ref.shape[0], step):
             here = slice(start, start + step)
             misfit = y_ref[here, :].astype(f32) - dot(x_ref[here, :], right)
@@ -296,29 +332,29 @@
     return beta, spread / (1.0 + gram[0, 0])
 
 
-def first_kernel(shape, half_count, *refs):
+def first_kernel(shape, arrays, *refs):
     bands, dates, parts = shape
-    blocks = refs[:half_count]
-    early_x, early_y, early_mask, early_cross, early_gram = refs[half_count : half_count + 5]
-    outs = refs[half_count + 5 : half_count + 10]
-    early_power, late_power, variance_ref, product_ref = refs[half_count + 10 :]
+    blocks = single_blocks(refs[:arrays])
+    early_x, early_y, early_mask, early_cross, early_gram = refs[arrays : arrays + 5]
+    outs = refs[arrays + 5 : arrays + 10]
+    early_power, late_power, variance_ref, product_ref = refs[arrays + 10 :]
     cross_sum, gram_sum = absorb(blocks, bands, dates, parts, outs, product_ref)
     _, _, x_ref, y_ref, mask_ref = outs
-    halves = [
+    groups = [
         (early_y, early_x, early_power, lambda here: early_mask[here, :].astype(f32)),
         (y_ref, x_ref, late_power, lambda here: mask_ref[here, :].astype(f32)),
     ]
     _, variance = fit_and_spread(
-        parts, bands, gram_sum + early_gram[...], cross_sum + early_cross[...], halves
+        parts, bands, gram_sum + early_gram[...], cross_sum + early_cross[...], groups
     )
     for place in range(variance_ref.shape[0]):
         variance_ref[place] = variance
 
 
-def smoothed(place_ref, field_ref, parts, width, rows, spaces, count):
+def smoothed(field_ref, parts, width, rows, spaces, count):
     group = LANES // width
-    space = place_ref[0]
-    me = place_ref[1]
+    space = lax.axis_index("space")
+    me = lax.axis_index("date")
 
     def rows_of(space_now, date_now):
         block = field_ref[space_now * count + date_now]
@@ -375,20 +411,20 @@
 
 def second_kernel(shape, *refs):
     bands, parts, width, rows, spaces, count = shape
-    place_ref, field_ref = refs[:2]
-    halves = [refs[2:8], refs[8:14]]
-    coefficient_ref, variance_ref = refs[14:16]
-    weight_ref, w_parts, wy_parts = refs[16], refs[17:20], refs[20:23]
-    smooth = smoothed(place_ref, field_ref, parts, width, rows, spaces, count)
+    field_ref = refs[0]
+    groups = [refs[1:7], refs[7:13]]
+    coefficient_ref, variance_ref = refs[13:15]
+    weight_ref, w_parts, wy_parts = refs[15], refs[16:19], refs[19:22]
+    smooth = smoothed(field_ref, parts, width, rows, spaces, count)
     smooth = to_lanes(smooth, parts, width)
     scale = 1.0 / (TUKEY * TUKEY * (smooth + EPS))
     scale = jnp.concatenate([scale] * (8 // parts), axis=0)
-    half = halves[0][3].shape[0]
+    early = groups[0][3].shape[0]
     step = 96
-    for n, (_, _, _, y_ref, mask_ref, power_ref) in enumerate(halves):
-        for start in range(0, half, step):
+    for base, (_, _, _, y_ref, mask_ref, power_ref) in zip((0, early), groups):
+        for start in range(0, y_ref.shape[0], step):
             here = slice(start, start + step)
-            there = slice(n * half + start, n * half + start + step)
+            there = slice(base + start, base + start + step)
             power = power_ref[here, :].reshape(step // 8, 8, LANES)
             left_over = 1.0 - jnp.minimum(power * scale[None], 1.0)
             mask = mask_ref[here, :].astype(f32)
@@ -403,9 +439,9 @@
 
     def moments(place, b_refs, size):
         total = 0.0
-        for n in range(2):
-            a_ref = halves[n][place]
-            there = slice(n * half, (n + 1) * half)
+        for base, group in zip((0, early), groups):
+            a_ref = group[place]
+            there = slice(base, base + group[3].shape[0])
             total = total + add_parts(dot(a_ref[...], b_refs[0][there, :]), size)
             total = total + add_parts(dot(a_ref[0 : 2 * size, :], b_refs[1][there, :]), size)
             total = total + dot(a_ref[0:size, :], b_refs[2][there, :])
@@ -419,12 +455,12 @@
         gram_sum,
         cross_sum,
         [
-            (halves[0][3], halves[0][2], None, lambda here: weight_ref[here, :]),
+            (groups[0][3], groups[0][2], None, lambda here: weight_ref[here, :]),
             (
-                halves[1][3],
-                halves[1][2],
+                groups[1][3],
+                groups[1][2],
                 None,
-                lambda here: weight_ref[here.start + half : here.stop + half, :],
+                lambda here: weight_ref[here.start + early : here.stop + early, :],
             ),
         ],
     )
@@ -435,9 +471,9 @@
             coefficient_ref[b, k] = to_rows(beta[k, b], width)
 
 
-def last_kernel(shape, place_ref, field_ref, noise_ref):
+def last_kernel(shape, field_ref, noise_ref):
     bands, parts, width, rows, spaces, count = shape
-    smooth = smoothed(place_ref, field_ref, parts, width, rows, spaces, count)
+    smooth = smoothed(field_ref, parts, width, rows, spaces, count)
     noise_ref[...] = jnp.sqrt(smooth[:, 0:width] + EPS)
 
 
@@ -449,79 +485,91 @@
     width = cols // count
     group = LANES // width
     parts = rows // group
-    half_count = count // 2
-    half = half_count * dates * parts
+    half = count // 2
+    quarter = half // 2
+    early_count, late_count = half + quarter, quarter
+    early_rows = early_count * dates * parts
+    late_rows = late_count * dates * parts
     shape = (bands, parts, width, rows, spaces, count)
     vmem = pl.BlockSpec(memory_space=pltpu.VMEM)
-    smem = pl.BlockSpec(memory_space=pltpu.SMEM)
     params = pltpu.CompilerParams(vmem_limit_bytes=VMEM_BYTES)
 
     blocks = packed_blocks(obs, valid, days, count, me, width)
     received = [blocks[0]] + [None] * (count - 1)
-    for k in range(half_count, count):
-        received[k] = lax.ppermute(blocks[k], "date", [(i, i ^ k) for i in range(count)])
-    for k in range(1, half_count):
+
+    def swap(k, after=None):
         block = blocks[k]
-        if k > 1:
-            block, received[k - 1] = lax.optimization_barrier((block, received[k - 1]))
+        if after is not None:
+            block, received[after] = lax.optimization_barrier((block, received[after]))
         received[k] = lax.ppermute(block, "date", [(i, i ^ k) for i in range(count)])
 
-    wide = (half, bands * LANES)
-    narrow = (half, LANES)
-    half_shapes = [
-        jax.ShapeDtypeStruct((3 * TERMS * parts, half), bf16),
-        jax.ShapeDtypeStruct((3 * len(pairs) * parts, half), bf16),
-        jax.ShapeDtypeStruct((half, 6 * TERMS * parts), bf16),
-        jax.ShapeDtypeStruct(wide, bf16),
-        jax.ShapeDtypeStruct(narrow, bf16),
-    ]
+    for k in range(half, count, 2):
+        swap(k)
+    for k in range(1, half):
+        swap(k)
+    for k in range(half + 1, count, 2):
+        swap(k, after=k - 1)
+    early_blocks = [*received[:half], *received[half::2]]
+    late_blocks = received[half + 1 :: 2]
+
+    def group_shapes(total):
+        return [
+            jax.ShapeDtypeStruct((3 * TERMS * parts, total), bf16),
+            jax.ShapeDtypeStruct((3 * len(pairs) * parts, total), bf16),
+            jax.ShapeDtypeStruct((total, 6 * TERMS * parts), bf16),
+            jax.ShapeDtypeStruct((total, bands * LANES), bf16),
+            jax.ShapeDtypeStruct((total, LANES), bf16),
+        ]
+
+    def power(total):
+        return jax.ShapeDtypeStruct((total, LANES), f32)
+
     sums = [
         jax.ShapeDtypeStruct((TERMS * parts, bands * LANES), f32),
         jax.ShapeDtypeStruct((len(pairs) * parts, LANES), f32),
     ]
-    power = jax.ShapeDtypeStruct(narrow, f32)
     send = jax.ShapeDtypeStruct((spaces * count, parts, LANES), f32)
     *early, early_cross, early_gram = pl.pallas_call(
         functools.partial(absorb_kernel, (bands, dates, parts)),
-        out_shape=half_shapes + sums,
-        in_specs=[vmem] * half_count,
+        out_shape=group_shapes(early_rows) + sums,
+        in_specs=[vmem] * len(early_blocks),
         out_specs=[vmem] * 7,
-        scratch_shapes=[pltpu.VMEM(wide, bf16)],
+        scratch_shapes=[pltpu.VMEM((early_rows, bands * LANES), bf16)],
         compiler_params=params,
         name="absorb",
-    )(*received[:half_count])
+    )(*early_blocks)
     *late, early_power, late_power, variance = pl.pallas_call(
-        functools.partial(first_kernel, (bands, dates, parts), half_count),
-        out_shape=half_shapes + [power, power, send],
-        in_specs=[vmem] * (half_count + 5),
+        functools.partial(first_kernel, (bands, dates, parts), len(late_blocks)),
+        out_shape=group_shapes(late_rows) + [power(early_rows), power(late_rows), send],
+        in_specs=[vmem] * (len(late_blocks) + 5),
         out_specs=[vmem] * 8,
-        scratch_shapes=[pltpu.VMEM(wide, bf16)],
+        scratch_shapes=[pltpu.VMEM((late_rows, bands * LANES), bf16)],
         compiler_params=params,
         name="first",
-    )(*received[half_count:], early[2], early[3], early[4], early_cross, early_gram)
-
-    place = jnp.stack([lax.axis_index("space"), me]).astype(jnp.int32)
+    )(*late_blocks, early[2], early[3], early[4], early_cross, early_gram)
+
     field = lax.all_to_all(variance, ("space", "date"), 0, 0, tiled=True)
+    total = early_rows + late_rows
     coefficients, variance = pl.pallas_call(
         functools.partial(second_kernel, shape),
         out_shape=[jax.ShapeDtypeStruct((bands, TERMS, rows, width), f32), send],
-        in_specs=[smem] + [vmem] * 13,
+        in_specs=[vmem] * 13,
         out_specs=[vmem] * 2,
-        scratch_shapes=[pltpu.VMEM((2 * half, LANES), f32)]
-        + [pltpu.VMEM((2 * half, LANES), bf16)] * 3
-        + [pltpu.VMEM((2 * half, bands * LANES), bf16)] * 3,
+        scratch_shapes=[pltpu.VMEM((total, LANES), f32)]
+        + [pltpu.VMEM((total, LANES), bf16)] * 3
+        + [pltpu.VMEM((total, bands * LANES), bf16)] * 3,
         compiler_params=params,
         name="second",
-    )(place, field, *early, early_power, *late, late_power)
+    )(field, *early, early_power, *late, late_power)
     field = lax.all_to_all(variance, ("space", "date"), 0, 0, tiled=True)
     noise = pl.pallas_call(
         functools.partial(last_kernel, shape),
         out_shape=jax.ShapeDtypeStruct((rows, width), f32),
-        in_specs=[smem, vmem],
+        in_specs=[vmem],
         out_specs=vmem,
         compiler_params=params,
         name="last",
-    )(place, field)
+    )(field)
     return coefficients, noise
 
 

time: 85 us -> 71 us (0.84)
  waiting for transfers between devices: 36.3 us -> 22 us
  blocking collectives: 8.95 us -> 23.1 us
  starting transfers between devices: 25.2 us -> 12.7 us
  local copies, waits for them, and re-layouts: 2.99 us -> 0.93 us
    all_to_all x1 -> x2, blocking collectives: 8.95 us -> 23.1 us  [on_device(): field = lax.all_to_all(variance, ('space', 'date'), 0, 0, tiled=True)]
    all_to_all x1 -> x0, starting transfers between devices: 10.3 us -> none  [on_device(): field = lax.all_to_all(variance, ('space', 'date'), 0, 0, tiled=True)]
    all_to_all x1 -> x0, waiting for transfers between devices: 7.2 us -> none  [on_device(): field = lax.all_to_all(variance, ('space', 'date'), 0, 0, tiled=True)]
    ppermute x7, waiting for transfers between devices: 29.1 us -> 22 us  [swap(): lax.ppermute(block, 'date', [(i, i ^ k) for i in range(count)])]
    ppermute x7, starting transfers between devices: 14.9 us -> 12.7 us  [swap(): lax.ppermute(block, 'date', [(i, i ^ k) for i in range(count)])]
    pallas_call x3 -> x2, Pallas kernels: 3.88 us -> 5.58 us  [the longest x1 3.82 us: packed_blocks(): pl.pallas_call(functools.partial(pack_kernel, count), out_shape=[shape] *...]
    unnamed x4 -> x2, local copies, waits for them, and re-layouts: 2.33 us -> 0.93 us
  transfers between devices with their start and end apart: 8 -> 7, of which waited for: 5 -> 3; matrix products, arithmetic and copies ran while one was open for 0% -> 0% of each run, Pallas kernels for 2% -> 2%
where the time goes in v3:
time: 71 us; the launch traced here: 70.8 us
  blocking collectives  23.1 us (33%)
  waiting for transfers between devices  22 us (31%)
  starting transfers between devices  12.7 us (18%)
  Pallas kernels  11.4 us (16%)
  local copies, waits for them, and re-layouts  0.93 us (1%)
    all_to_all x2, blocking collectives, on_device(): field = lax.all_to_all(variance, ('space', 'date'), 0, 0, tiled=True)  23.1 us
    ppermute x7, waiting for transfers between devices, swap(): lax.ppermute(block, 'date', [(i, i ^ k) for i in range(count)])  22 us
    ppermute x7, starting transfers between devices, swap(): lax.ppermute(block, 'date', [(i, i ^ k) for i in range(count)])  12.7 us
    pallas_call x1, Pallas kernels, packed_blocks(): pl.pallas_call(functools.partial(pack_kernel, count), out_shape=[shape] *...  3.82 us
    pallas_call x1, Pallas kernels, on_device(): pl.pallas_call(functools.partial(second_kernel, shape), out_shape=[jax.Sh...  3.42 us
    pallas_call x1, Pallas kernels, on_device(): pl.pallas_call(functools.partial(first_kernel, (bands, dates, parts), len...  1.76 us
    pallas_call x1, Pallas kernels, on_device(): pl.pallas_call(functools.partial(absorb_kernel, (bands, dates, parts)), o...  1.59 us
  transfers between devices with their start and end apart: 7, of which 3 were waited for; matrix products, arithmetic and copies ran while one was open for 0% of the time, Pallas kernels for 2%

profile of v3, /device:TPU:0, one launch (start us, length us, event | category | flops | bytes accessed | tf_op | source)
XLA Modules:
  0.0 70.8 jit_solution(6146108126425359534)
XLA Ops:
  0.6 3.8 %pack.1 = (bf16[784,128]{1,0:T(8,128)(2,1)}, bf16[784,128]{1,0:T(8,128)(2,1)}, bf16[784,128]{1,0:T(8,128)(2,1)}, bf16[784,128]{1,0:T(8,128)(2,1)}, bf16[784,128]...) custom-call(s32[24]{0:T(128)} %day_ref.1, ...), custom_call_target="tpu_custom_call" | custom-call | tf_op jit(solution)/shard_map/pack/pallas_call | solution.py:131
  4.5 4.1 %collective-permute-start = (bf16[784,128]{1,0:T(8,128)(2,1)}, bf16[784,128]{1,0:T(8,128)(2,1)S(1)}, u32[]{:S(2)}, u32[]{:S(2)}) collective-permute-start(bf16[784,128]{1,0:T(8,128)(2,1)} %get-tuple-element.32), channel_id=1, source_target_pairs={{0,4},{1,5},{2,6},{3,7},{4,0},{5,1},{6,2},{7,3},{8,12},{9,13},{10,... | collective-permute-start | bytes 602120 | tf_op jit(solution)/shard_map/ppermute | solution.py:504
  8.6 1.3 %collective-permute-start.2 = (bf16[784,128]{1,0:T(8,128)(2,1)}, bf16[784,128]{1,0:T(8,128)(2,1)S(1)}, u32[]{:S(2)}, u32[]{:S(2)}) collective-permute-start(bf16[784,128]{1,0:T(8,128)(2,1)} %get-tuple-element.35), channel_id=1, source_target_pairs={{0,6},{1,7},{2,4},{3,5},{4,2},{5,3},{6,0},{7,1},{8,14},{9,15},{10,... | collective-permute-start | bytes 602120 | tf_op jit(solution)/shard_map/ppermute | solution.py:504
  9.9 1.5 %collective-permute-start.4 = (bf16[784,128]{1,0:T(8,128)(2,1)}, bf16[784,128]{1,0:T(8,128)(2,1)S(1)}, u32[]{:S(2)}, u32[]{:S(2)}) collective-permute-start(bf16[784,128]{1,0:T(8,128)(2,1)} %get-tuple-element.38), channel_id=1, source_target_pairs={{0,1},{1,0},{2,3},{3,2},{4,5},{5,4},{6,7},{7,6},{8,9},{9,8},{10,11... | collective-permute-start | bytes 602120 | tf_op jit(solution)/shard_map/ppermute | solution.py:504
  11.4 0.2 collective-permute-start.5
  11.6 1.8 %collective-permute-start.6 = (bf16[784,128]{1,0:T(8,128)(2,1)}, bf16[784,128]{1,0:T(8,128)(2,1)S(1)}, u32[]{:S(2)}, u32[]{:S(2)}) collective-permute-start(bf16[784,128]{1,0:T(8,128)(2,1)} %get-tuple-element.40), channel_id=1, source_target_pairs={{0,3},{1,2},{2,1},{3,0},{4,7},{5,6},{6,5},{7,4},{8,11},{9,10},{10,... | collective-permute-start | bytes 602120 | tf_op jit(solution)/shard_map/ppermute | solution.py:504
  13.4 9.8 %collective-permute-done.refs_4_ = bf16[784,128]{1,0:T(8,128)(2,1)S(1)} collective-permute-done((bf16[784,128]{1,0:T(8,128)(2,1)}, bf16[784,128]{1,0:T(8,128)(2,1)S(1)}, u32[]{:S(2)}, u32[]{:S(2)}) %collective-permute-start) | collective-permute-done | bytes 200736 | tf_op jit(solution)/shard_map/ppermute | solution.py:504
  23.2 0.9 %collective-permute-start.1 = (bf16[784,128]{1,0:T(8,128)(2,1)}, bf16[784,128]{1,0:T(8,128)(2,1)S(1)}, u32[]{:S(2)}, u32[]{:S(2)}) collective-permute-start(bf16[784,128]{1,0:T(8,128)(2,1)} %get-tuple-element.33), channel_id=1, source_target_pairs={{0,5},{1,4},{2,7},{3,6},{4,1},{5,0},{6,3},{7,2},{8,13},{9,12},{10,... | collective-permute-start | bytes 602120 | tf_op jit(solution)/shard_map/ppermute | solution.py:504
  24.2 0.0 collective-permute-done.2.refs_5_
  24.2 2.8 %collective-permute-start.3 = (bf16[784,128]{1,0:T(8,128)(2,1)}, bf16[784,128]{1,0:T(8,128)(2,1)S(1)}, u32[]{:S(2)}, u32[]{:S(2)}) collective-permute-start(bf16[784,128]{1,0:T(8,128)(2,1)} %get-tuple-element.36), channel_id=1, source_target_pairs={{0,7},{1,6},{2,5},{3,4},{4,3},{5,2},{6,1},{7,0},{8,15},{9,14},{10,... | collective-permute-start | bytes 602120 | tf_op jit(solution)/shard_map/ppermute | solution.py:504
  27.0 0.0 collective-permute-done.4.refs_1_
  27.0 0.0 collective-permute-done.5.refs_2_
  27.0 3.5 %collective-permute-done.6.refs_3_ = bf16[784,128]{1,0:T(8,128)(2,1)S(1)} collective-permute-done((bf16[784,128]{1,0:T(8,128)(2,1)}, bf16[784,128]{1,0:T(8,128)(2,1)S(1)}, u32[]{:S(2)}, u32[]{:S(2)}) %collective-permute-start.6) | collective-permute-done | bytes 200736 | tf_op jit(solution)/shard_map/ppermute | solution.py:504
  30.4 0.0 copy-start
  30.4 0.9 %copy-done = bf16[784,128]{1,0:T(8,128)(2,1)S(1)} copy-done((bf16[784,128]{1,0:T(8,128)(2,1)S(1)}, bf16[784,128]{1,0:T(8,128)(2,1)}, u32[]{:S(2)}) %copy-start) | copy-done | bytes 200728
  31.4 1.6 %absorb.1 = (bf16[96,576]{1,0:T(8,128)(2,1)S(1)}, bf16[432,576]{1,0:T(8,128)(2,1)S(1)}, bf16[576,192]{1,0:T(8,128)(2,1)S(1)}, bf16[576,896]{1,0:T(8,128)(2,1)S(1...) custom-call(bf16[784,128]{1,0:T(8,128)(2,1)S(1)} %copy-done, ...), custom_call_target="tpu_custom_call" | custom-call | tf_op jit(solution)/shard_map/absorb/pallas_call | solution.py:532
  33.0 8.7 %collective-permute-done.1.refs_0_ = bf16[784,128]{1,0:T(8,128)(2,1)S(1)} collective-permute-done((bf16[784,128]{1,0:T(8,128)(2,1)}, bf16[784,128]{1,0:T(8,128)(2,1)S(1)}, u32[]{:S(2)}, u32[]{:S(2)}) %collective-permute-start.1) | collective-permute-done | bytes 200736 | tf_op jit(solution)/shard_map/ppermute | solution.py:504
  41.7 0.0 collective-permute-done.3.refs_1_
  41.7 1.8 %first.1 = (bf16[96,192]{1,0:T(8,128)(2,1)S(1)}, bf16[432,192]{1,0:T(8,128)(2,1)S(1)}, bf16[192,192]{1,0:T(8,128)(2,1)S(1)}, bf16[192,896]{1,0:T(8,128)(2,1)S(1)...) custom-call(bf16[784,128]{1,0:T(8,128)(2,1)S(1)} %collective-permute, ...), custom_call_target="tpu_custom_call" | custom-call | tf_op jit(solution)/shard_map/first/pallas_call | solution.py:541
  43.5 14.2 %all_to_all.10.refs_0_ = f32[32,4,128]{2,1,0:T(4,128)S(1)} all-to-all(f32[32,4,128]{2,1,0:T(4,128)S(1)} %get-tuple-element.48), channel_id=1, replica_groups=mesh['space'=4,'date'=8] {'space','date'}, dimensions={0} | all-to-all | bytes 131072 | tf_op jit(solution)/shard_map/all_to_all | solution.py:551
  57.6 3.4 %second.1 = (f32[7,8,8,64]{3,2,1,0:T(8,128)}, f32[32,4,128]{2,1,0:T(4,128)S(1)}) custom-call(f32[32,4,128]{2,1,0:T(4,128)S(1)} %all_to_all.10.refs_0_, bf16[96,576]{1,0:T(8,128)(2,1)S(1)} %get-tuple-element.49.refs_1_, bf16[432,576]{1,0:T(8,128)(2,1)S(1)} %get-tuple-element.50.refs_2_, bf16[576,192]{1,0:T(8,128)(2,1)S(1)} %get-tuple-element.43.refs_2_.refs_3_, ...), custom_call_target="tpu_custom_call" | custom-call | tf_op jit(solution)/shard_map/second/pallas_call | solution.py:553
  61.1 9.0 %all_to_all.11.field_ref = f32[32,4,128]{2,1,0:T(4,128)S(1)} all-to-all(f32[32,4,128]{2,1,0:T(4,128)S(1)} %get-tuple-element.59), channel_id=1, replica_groups=mesh['space'=4,'date'=8] {'space','date'}, dimensions={0} | all-to-all | bytes 131072 | tf_op jit(solution)/shard_map/all_to_all | solution.py:564
  70.0 0.8 %last.1 = f32[8,64]{1,0:T(8,128)} custom-call(f32[32,4,128]{2,1,0:T(4,128)S(1)} %all_to_all.11.field_ref), custom_call_target="tpu_custom_call" | custom-call | tf_op jit(solution)/shard_map/last/pallas_call | solution.py:565
Async XLA Ops:
  4.5 18.8 %collective-permute-start = (bf16[784,128]{1,0:T(8,128)(2,1)}, bf16[784,128]{1,0:T(8,128)(2,1)S(1)}, u32[]{:S(2)}, u32[]{:S(2)}) collective-permute-start(bf16[784,128]{1,0:T(8,128)(2,1)} %get-tuple-element.32), channel_id=1, source_target_pairs={{0,4},{1,5},{2,6},{3,7},{4,0},{5,1},{6,2},{7,3},{8,12},{9,13},{10,... | collective-permute-start | bytes 602120 | tf_op jit(solution)/shard_map/ppermute | solution.py:504
  8.6 15.6 %collective-permute-start.2 = (bf16[784,128]{1,0:T(8,128)(2,1)}, bf16[784,128]{1,0:T(8,128)(2,1)S(1)}, u32[]{:S(2)}, u32[]{:S(2)}) collective-permute-start(bf16[784,128]{1,0:T(8,128)(2,1)} %get-tuple-element.35), channel_id=1, source_target_pairs={{0,6},{1,7},{2,4},{3,5},{4,2},{5,3},{6,0},{7,1},{8,14},{9,15},{10,... | collective-permute-start | bytes 602120 | tf_op jit(solution)/shard_map/ppermute | solution.py:504
  9.9 17.1 %collective-permute-start.4 = (bf16[784,128]{1,0:T(8,128)(2,1)}, bf16[784,128]{1,0:T(8,128)(2,1)S(1)}, u32[]{:S(2)}, u32[]{:S(2)}) collective-permute-start(bf16[784,128]{1,0:T(8,128)(2,1)} %get-tuple-element.38), channel_id=1, source_target_pairs={{0,1},{1,0},{2,3},{3,2},{4,5},{5,4},{6,7},{7,6},{8,9},{9,8},{10,11... | collective-permute-start | bytes 602120 | tf_op jit(solution)/shard_map/ppermute | solution.py:504
  11.4 15.6 %collective-permute-start.5 = (bf16[784,128]{1,0:T(8,128)(2,1)}, bf16[784,128]{1,0:T(8,128)(2,1)S(1)}, u32[]{:S(2)}, u32[]{:S(2)}) collective-permute-start(bf16[784,128]{1,0:T(8,128)(2,1)} %get-tuple-element.39), channel_id=1, source_target_pairs={{0,2},{1,3},{2,0},{3,1},{4,6},{5,7},{6,4},{7,5},{8,10},{9,11},{10,... | collective-permute-start | bytes 602120 | tf_op jit(solution)/shard_map/ppermute | solution.py:504
  11.6 18.8 %collective-permute-start.6 = (bf16[784,128]{1,0:T(8,128)(2,1)}, bf16[784,128]{1,0:T(8,128)(2,1)S(1)}, u32[]{:S(2)}, u32[]{:S(2)}) collective-permute-start(bf16[784,128]{1,0:T(8,128)(2,1)} %get-tuple-element.40), channel_id=1, source_target_pairs={{0,3},{1,2},{2,1},{3,0},{4,7},{5,6},{6,5},{7,4},{8,11},{9,10},{10,... | collective-permute-start | bytes 602120 | tf_op jit(solution)/shard_map/ppermute | solution.py:504
  23.2 18.5 %collective-permute-start.1 = (bf16[784,128]{1,0:T(8,128)(2,1)}, bf16[784,128]{1,0:T(8,128)(2,1)S(1)}, u32[]{:S(2)}, u32[]{:S(2)}) collective-permute-start(bf16[784,128]{1,0:T(8,128)(2,1)} %get-tuple-element.33), channel_id=1, source_target_pairs={{0,5},{1,4},{2,7},{3,6},{4,1},{5,0},{6,3},{7,2},{8,13},{9,12},{10,... | collective-permute-start | bytes 602120 | tf_op jit(solution)/shard_map/ppermute | solution.py:504
  24.2 17.6 %collective-permute-start.3 = (bf16[784,128]{1,0:T(8,128)(2,1)}, bf16[784,128]{1,0:T(8,128)(2,1)S(1)}, u32[]{:S(2)}, u32[]{:S(2)}) collective-permute-start(bf16[784,128]{1,0:T(8,128)(2,1)} %get-tuple-element.36), channel_id=1, source_target_pairs={{0,7},{1,6},{2,5},{3,4},{4,3},{5,2},{6,1},{7,0},{8,15},{9,14},{10,... | collective-permute-start | bytes 602120 | tf_op jit(solution)/shard_map/ppermute | solution.py:504
  30.4 0.9 %copy-start = (bf16[784,128]{1,0:T(8,128)(2,1)S(1)}, bf16[784,128]{1,0:T(8,128)(2,1)}, u32[]{:S(2)}) copy-start(bf16[784,128]{1,0:T(8,128)(2,1)} %get-tuple-element.37.refs_0_) | copy-start | bytes 602116

commit v4 on v3

--- a/solution.py
+++ b/solution.py
@@ -19,6 +19,11 @@
 pairs = [(i, j) for i in range(TERMS) for j in range(i, TERMS)]
 f32 = jnp.float32
 bf16 = jnp.bfloat16
+
+
+def split2_kernel(x):
+    high = x.astype(bf16)
+    return high, (x - high.astype(f32)).astype(bf16)
 
 
 def split3_kernel(x):
@@ -48,15 +53,15 @@
     out_ref[...] = design_info(day_ref, dates)
 
 
-def pack_kernel(count, day_ref, obs_ref, valid_ref, *refs):
-    half = count // 2
-    outs = refs[:count]
-    obs_here, valid_here, out_here, in_sems, out_sems = refs[count:]
+def pack_kernel(steps, day_ref, obs_ref, valid_ref, *refs):
+    outs = refs[: 2 * len(steps)]
+    day_here, obs_here, valid_here, sems, day_sem = refs[2 * len(steps) :]
     me = lax.axis_index("date")
     odd = lax.rem(me, 2) == 1
     bands, dates = obs_ref.shape[:2]
     rows = dates * 4
-    steps = (*range(half // 2, half), *range(half // 2))
+    day_copy = pltpu.make_async_copy(day_ref, day_here, day_sem)
+    day_copy.start()
     arrivals = []
     for place, step in enumerate(steps):
         tile = lax.div(me, 2) ^ step
@@ -64,22 +69,22 @@
         arrivals.append(
             (
                 pltpu.make_async_copy(
-                    obs_ref.at[:, :, :, lanes], obs_here.at[place], in_sems.at[2 * place]
+                    obs_ref.at[:, :, :, lanes], obs_here.at[place], sems.at[2 * place]
                 ),
                 pltpu.make_async_copy(
-                    valid_ref.at[:, :, lanes], valid_here.at[place], in_sems.at[2 * place + 1]
+                    valid_ref.at[:, :, lanes], valid_here.at[place], sems.at[2 * place + 1]
                 ),
             )
         )
         for copy in arrivals[place]:
             copy.start()
-    info = design_info(day_ref, dates)
+    day_copy.wait()
+    info = design_info(day_here, dates)
     pairs_of_dates = dates // 2
     row = lax.broadcasted_iota(jnp.int32, (pairs_of_dates, 8, LANES), 1)
     lane = lax.broadcasted_iota(jnp.int32, (pairs_of_dates, 8, LANES), 2)
     top = row < 4
     left = lane < 64
-    leaving = []
     for place, step in enumerate(steps):
         for copy in arrivals[place]:
             copy.wait()
@@ -103,18 +108,10 @@
             same = jnp.where(odd, odd_block, even_block)
             other = jnp.where(odd, even_block, odd_block)
             here = slice(band * rows, (band + 1) * rows)
-            out_here[2 * place, here, :] = same.reshape(rows, LANES).astype(bf16)
-            out_here[2 * place + 1, here, :] = other.reshape(rows, LANES).astype(bf16)
+            outs[2 * place][here, :] = same.reshape(rows, LANES).astype(bf16)
+            outs[2 * place + 1][here, :] = other.reshape(rows, LANES).astype(bf16)
         for n in (0, 1):
-            out_here[2 * place + n, (bands + 1) * rows :, :] = info
-            leaving.append(
-                pltpu.make_async_copy(
-                    out_here.at[2 * place + n], outs[2 * step + n], out_sems.at[2 * place + n]
-                )
-            )
-            leaving[-1].start()
-    for copy in leaving:
-        copy.wait()
+            outs[2 * place + n][(bands + 1) * rows :, :] = info
 
 
 def packed_blocks(obs, valid, days, count, me, width):
@@ -126,23 +123,26 @@
     size = (bands + 1) * dates * parts
     half = count // 2
     if width == 64 and rows == 8:
-        shape = jax.ShapeDtypeStruct((size + INFO_ROWS, LANES), bf16)
         hbm = pl.BlockSpec(memory_space=pltpu.HBM)
-        return pl.pallas_call(
-            functools.partial(pack_kernel, count),
-            out_shape=[shape] * count,
-            in_specs=[smem, hbm, hbm],
-            out_specs=[hbm] * count,
-            scratch_shapes=[
-                pltpu.VMEM((half, bands, dates, rows, LANES), bf16),
-                pltpu.VMEM((half, dates, rows, LANES), jnp.int32),
-                pltpu.VMEM((count, size + INFO_ROWS, LANES), bf16),
-                pltpu.SemaphoreType.DMA((count,)),
-                pltpu.SemaphoreType.DMA((count,)),
-            ],
-            compiler_params=pltpu.CompilerParams(vmem_limit_bytes=PACK_VMEM_BYTES),
-            name="pack",
-        )(days, obs, valid)
+        blocks = [None] * count
+        for steps in (range(half // 2, half), range(half // 2)):
+            tiles = len(steps)
+            blocks[2 * steps[0] : 2 * steps[-1] + 2] = pl.pallas_call(
+                functools.partial(pack_kernel, tuple(steps)),
+                out_shape=[jax.ShapeDtypeStruct((size + INFO_ROWS, LANES), bf16)] * (2 * tiles),
+                in_specs=[hbm] * 3,
+                out_specs=[vmem] * (2 * tiles),
+                scratch_shapes=[
+                    pltpu.SMEM((dates,), jnp.int32),
+                    pltpu.VMEM((tiles, bands, dates, rows, LANES), bf16),
+                    pltpu.VMEM((tiles, dates, rows, LANES), jnp.int32),
+                    pltpu.SemaphoreType.DMA((2 * tiles,)),
+                    pltpu.SemaphoreType.DMA,
+                ],
+                compiler_params=pltpu.CompilerParams(vmem_limit_bytes=PACK_VMEM_BYTES),
+                name="pack",
+            )(days, obs, valid)
+        return blocks
     info = pl.pallas_call(
         functools.partial(info_kernel, dates),
         out_shape=jax.ShapeDtypeStruct((INFO_ROWS, LANES), bf16),
@@ -414,7 +414,7 @@
     field_ref = refs[0]
     groups = [refs[1:7], refs[7:13]]
     coefficient_ref, variance_ref = refs[13:15]
-    weight_ref, w_parts, wy_parts = refs[15], refs[16:19], refs[19:22]
+    weight_ref, w_parts, wy_parts = refs[15], refs[16:18], refs[18:20]
     smooth = smoothed(field_ref, parts, width, rows, spaces, count)
     smooth = to_lanes(smooth, parts, width)
     scale = 1.0 / (TUKEY * TUKEY * (smooth + EPS))
@@ -430,11 +430,11 @@
             mask = mask_ref[here, :].astype(f32)
             weight = mask * (left_over * left_over).reshape(step, LANES)
             weight_ref[there, :] = weight
-            for ref, part in zip(w_parts, split3_kernel(weight)):
+            for ref, part in zip(w_parts, split2_kernel(weight)):
                 ref[there, :] = part
             for b in range(bands):
                 y = y_ref[here, b * LANES : (b + 1) * LANES].astype(f32)
-                for ref, part in zip(wy_parts, split3_kernel(weight * y)):
+                for ref, part in zip(wy_parts, split2_kernel(weight * y)):
                     ref[there, b * LANES : (b + 1) * LANES] = part
 
     def moments(place, b_refs, size):
@@ -444,7 +444,6 @@
             there = slice(base, base + group[3].shape[0])
             total = total + add_parts(dot(a_ref[...], b_refs[0][there, :]), size)
             total = total + add_parts(dot(a_ref[0 : 2 * size, :], b_refs[1][there, :]), size)
-            total = total + dot(a_ref[0:size, :], b_refs[2][there, :])
         return total
 
     cross_sum = moments(0, wy_parts, TERMS * parts)
@@ -507,8 +506,9 @@
         swap(k)
     for k in range(1, half):
         swap(k)
-    for k in range(half + 1, count, 2):
-        swap(k, after=k - 1)
+    for k in range(half, count, 2):
+        swap(k + 1, after=k ^ 2)
+
     early_blocks = [*received[:half], *received[half::2]]
     late_blocks = received[half + 1 :: 2]
 
@@ -556,8 +556,8 @@
         in_specs=[vmem] * 13,
         out_specs=[vmem] * 2,
         scratch_shapes=[pltpu.VMEM((total, LANES), f32)]
-        + [pltpu.VMEM((total, LANES), bf16)] * 3
-        + [pltpu.VMEM((total, bands * LANES), bf16)] * 3,
+        + [pltpu.VMEM((total, LANES), bf16)] * 2
+        + [pltpu.VMEM((total, bands * LANES), bf16)] * 2,
         compiler_params=params,
         name="second",
     )(field, *early, early_power, *late, late_power)

time: 71 us -> 68.2 us (0.961)
  waiting for transfers between devices: 22 us -> 10.7 us
  starting transfers between devices: 12.7 us -> 21.6 us
  blocking collectives: 23.1 us -> 22.3 us
    ppermute x7, waiting for transfers between devices: 22 us -> 10.7 us  [swap(): lax.ppermute(block, 'date', [(i, i ^ k) for i in range(count)])]
    ppermute x7, starting transfers between devices: 12.7 us -> 21.6 us  [swap(): lax.ppermute(block, 'date', [(i, i ^ k) for i in range(count)])]
    pallas_call x1 -> x2, Pallas kernels: 3.82 us -> 4.88 us  [packed_blocks(): pl.pallas_call(functools.partial(pack_kernel, tuple(steps)), out_shape=[j...]
    all_to_all x2, blocking collectives: 23.1 us -> 22.3 us  [on_device(): field = lax.all_to_all(variance, ('space', 'date'), 0, 0, tiled=True)]
  transfers between devices with their start and end apart: 7 -> 7, of which waited for: 3 -> 3; matrix products, arithmetic and copies ran while one was open for 0% -> 0% of each run, Pallas kernels for 2% -> 6%
where the time goes in v4:
time: 68.2 us; the launch traced here: 68 us
  blocking collectives  22.3 us (33%)
  starting transfers between devices  21.6 us (32%)
  Pallas kernels  11.9 us (17%)
  waiting for transfers between devices  10.7 us (16%)
  local copies, waits for them, and re-layouts  0.93 us (1%)
  between operations  0.7 us (1%)
    all_to_all x2, blocking collectives, on_device(): field = lax.all_to_all(variance, ('space', 'date'), 0, 0, tiled=True)  22.3 us
    ppermute x7, starting transfers between devices, swap(): lax.ppermute(block, 'date', [(i, i ^ k) for i in range(count)])  21.6 us
    ppermute x7, waiting for transfers between devices, swap(): lax.ppermute(block, 'date', [(i, i ^ k) for i in range(count)])  10.7 us
    pallas_call x2, Pallas kernels, packed_blocks(): pl.pallas_call(functools.partial(pack_kernel, tuple(steps)), out_shape=[j...  4.88 us
    pallas_call x1, Pallas kernels, on_device(): pl.pallas_call(functools.partial(second_kernel, shape), out_shape=[jax.Sh...  2.85 us
    pallas_call x1, Pallas kernels, on_device(): pl.pallas_call(functools.partial(first_kernel, (bands, dates, parts), len...  1.76 us
    pallas_call x1, Pallas kernels, on_device(): pl.pallas_call(functools.partial(absorb_kernel, (bands, dates, parts)), o...  1.59 us
  transfers between devices with their start and end apart: 7, of which 3 were waited for; matrix products, arithmetic and copies ran while one was open for 0% of the time, Pallas kernels for 6%

profile of v4, /device:TPU:0, one launch (start us, length us, event | category | flops | bytes accessed | tf_op | source)
XLA Modules:
  0.0 68.0 jit_solution(1680157491646092776)
XLA Ops:
  0.6 2.4 %pack.2 = (bf16[784,128]{1,0:T(8,128)(2,1)}, bf16[784,128]{1,0:T(8,128)(2,1)}, bf16[784,128]{1,0:T(8,128)(2,1)}, bf16[784,128]{1,0:T(8,128)(2,1)}) custom-call(s32[24]{0:T(128)} %day_ref.3, bf16[7,24,8,512]{3,2,1,0:T(8,128)(2,1)} %obs_ref.3, s32[24,8,512]{2,1,0:T(8,128)} %valid_ref.3), custom_call_target="tpu_custom_call" | custom-call | tf_op jit(solution)/shard_map/pack/pallas_call | solution.py:130
  3.1 0.0 copy-start.2
  3.1 0.0 copy-start.1
  3.1 5.1 %collective-permute-start = (bf16[784,128]{1,0:T(8,128)(2,1)}, bf16[784,128]{1,0:T(8,128)(2,1)S(1)}, u32[]{:S(2)}, u32[]{:S(2)}) collective-permute-start(bf16[784,128]{1,0:T(8,128)(2,1)} %get-tuple-element.32), channel_id=1, source_target_pairs={{0,6},{1,7},{2,4},{3,5},{4,2},{5,3},{6,0},{7,1},{8,14},{9,15},{10,... | collective-permute-start | bytes 602120 | tf_op jit(solution)/shard_map/ppermute | solution.py:503
  8.2 0.0 collective-permute-start.2
  8.2 2.4 %pack.3 = (bf16[784,128]{1,0:T(8,128)(2,1)}, bf16[784,128]{1,0:T(8,128)(2,1)}, bf16[784,128]{1,0:T(8,128)(2,1)}, bf16[784,128]{1,0:T(8,128)(2,1)}) custom-call(s32[24]{0:T(128)} %day_ref.3, bf16[7,24,8,512]{3,2,1,0:T(8,128)(2,1)} %obs_ref.3, s32[24,8,512]{2,1,0:T(8,128)} %valid_ref.3), custom_call_target="tpu_custom_call" | custom-call | tf_op jit(solution)/shard_map/pack/pallas_call | solution.py:130
  10.7 1.6 %collective-permute-start.4 = (bf16[784,128]{1,0:T(8,128)(2,1)}, bf16[784,128]{1,0:T(8,128)(2,1)S(1)}, u32[]{:S(2)}, u32[]{:S(2)}) collective-permute-start(bf16[784,128]{1,0:T(8,128)(2,1)} %get-tuple-element.38), channel_id=1, source_target_pairs={{0,1},{1,0},{2,3},{3,2},{4,5},{5,4},{6,7},{7,6},{8,9},{9,8},{10,11... | collective-permute-start | bytes 602120 | tf_op jit(solution)/shard_map/ppermute | solution.py:503
  12.2 0.8 %collective-permute-start.5 = (bf16[784,128]{1,0:T(8,128)(2,1)}, bf16[784,128]{1,0:T(8,128)(2,1)S(1)}, u32[]{:S(2)}, u32[]{:S(2)}) collective-permute-start(bf16[784,128]{1,0:T(8,128)(2,1)} %get-tuple-element.39), channel_id=1, source_target_pairs={{0,2},{1,3},{2,0},{3,1},{4,6},{5,7},{6,4},{7,5},{8,10},{9,11},{10,... | collective-permute-start | bytes 602120 | tf_op jit(solution)/shard_map/ppermute | solution.py:503
  13.0 1.2 %collective-permute-start.6 = (bf16[784,128]{1,0:T(8,128)(2,1)}, bf16[784,128]{1,0:T(8,128)(2,1)S(1)}, u32[]{:S(2)}, u32[]{:S(2)}) collective-permute-start(bf16[784,128]{1,0:T(8,128)(2,1)} %get-tuple-element.40), channel_id=1, source_target_pairs={{0,3},{1,2},{2,1},{3,0},{4,7},{5,6},{6,5},{7,4},{8,11},{9,10},{10,... | collective-permute-start | bytes 602120 | tf_op jit(solution)/shard_map/ppermute | solution.py:503
  14.2 0.1 collective-permute-done.refs_5_
  14.3 0.0 copy-done.2
  14.3 10.5 %collective-permute-start.1 = (bf16[784,128]{1,0:T(8,128)(2,1)S(1)}, bf16[784,128]{1,0:T(8,128)(2,1)S(1)}, u32[]{:S(2)}, u32[]{:S(2)}) collective-permute-start(bf16[784,128]{1,0:T(8,128)(2,1)S(1)} %copy-done.2), channel_id=1, source_target_pairs={{0,5},{1,4},{2,7},{3,6},{4,1},{5,0},{6,3},{7,2},{8,13},{9,12},{10,... | collective-permute-start | bytes 602120 | tf_op jit(solution)/shard_map/ppermute | solution.py:503
  24.8 3.1 %collective-permute-done.2.refs_4_ = bf16[784,128]{1,0:T(8,128)(2,1)S(1)} collective-permute-done((bf16[784,128]{1,0:T(8,128)(2,1)}, bf16[784,128]{1,0:T(8,128)(2,1)S(1)}, u32[]{:S(2)}, u32[]{:S(2)}) %collective-permute-start.2) | collective-permute-done | bytes 200736 | tf_op jit(solution)/shard_map/ppermute | solution.py:503
  28.0 0.0 copy-done.1
  28.0 2.4 %collective-permute-start.3 = (bf16[784,128]{1,0:T(8,128)(2,1)S(1)}, bf16[784,128]{1,0:T(8,128)(2,1)S(1)}, u32[]{:S(2)}, u32[]{:S(2)}) collective-permute-start(bf16[784,128]{1,0:T(8,128)(2,1)S(1)} %copy-done.1), channel_id=1, source_target_pairs={{0,7},{1,6},{2,5},{3,4},{4,3},{5,2},{6,1},{7,0},{8,15},{9,14},{10,... | collective-permute-start | bytes 602120 | tf_op jit(solution)/shard_map/ppermute | solution.py:503
  30.4 0.0 collective-permute-done.4.refs_1_
  30.4 0.0 collective-permute-done.5.refs_2_
  30.4 0.0 collective-permute-done.6.refs_3_
  30.4 0.0 copy-start
  30.4 0.9 %copy-done = bf16[784,128]{1,0:T(8,128)(2,1)S(1)} copy-done((bf16[784,128]{1,0:T(8,128)(2,1)S(1)}, bf16[784,128]{1,0:T(8,128)(2,1)}, u32[]{:S(2)}) %copy-start) | copy-done | bytes 200728
  31.3 1.6 %absorb.1 = (bf16[96,576]{1,0:T(8,128)(2,1)S(1)}, bf16[432,576]{1,0:T(8,128)(2,1)S(1)}, bf16[576,192]{1,0:T(8,128)(2,1)S(1)}, bf16[576,896]{1,0:T(8,128)(2,1)S(1...) custom-call(bf16[784,128]{1,0:T(8,128)(2,1)S(1)} %copy-done, ...), custom_call_target="tpu_custom_call" | custom-call | tf_op jit(solution)/shard_map/absorb/pallas_call | solution.py:532
  32.9 7.4 %collective-permute-done.1.refs_0_ = bf16[784,128]{1,0:T(8,128)(2,1)S(1)} collective-permute-done((bf16[784,128]{1,0:T(8,128)(2,1)S(1)}, bf16[784,128]{1,0:T(8,128)(2,1)S(1)}, u32[]{:S(2)}, u32[]{:S(2)}) %collective-permute-start.1) | collective-permute-done | bytes 200736 | tf_op jit(solution)/shard_map/ppermute | solution.py:503
  40.3 0.0 collective-permute-done.3.refs_1_
  40.3 1.8 %first.1 = (bf16[96,192]{1,0:T(8,128)(2,1)S(1)}, bf16[432,192]{1,0:T(8,128)(2,1)S(1)}, bf16[192,192]{1,0:T(8,128)(2,1)S(1)}, bf16[192,896]{1,0:T(8,128)(2,1)S(1)...) custom-call(bf16[784,128]{1,0:T(8,128)(2,1)S(1)} %collective-permute, ...), custom_call_target="tpu_custom_call" | custom-call | tf_op jit(solution)/shard_map/first/pallas_call | solution.py:541
  42.1 13.3 %all_to_all.10.refs_0_ = f32[32,4,128]{2,1,0:T(4,128)S(1)} all-to-all(f32[32,4,128]{2,1,0:T(4,128)S(1)} %get-tuple-element.48), channel_id=1, replica_groups=mesh['space'=4,'date'=8] {'space','date'}, dimensions={0} | all-to-all | bytes 131072 | tf_op jit(solution)/shard_map/all_to_all | solution.py:551
  55.4 2.9 %second.1 = (f32[7,8,8,64]{3,2,1,0:T(8,128)}, f32[32,4,128]{2,1,0:T(4,128)S(1)}) custom-call(f32[32,4,128]{2,1,0:T(4,128)S(1)} %all_to_all.10.refs_0_, bf16[96,576]{1,0:T(8,128)(2,1)S(1)} %get-tuple-element.49.refs_1_, bf16[432,576]{1,0:T(8,128)(2,1)S(1)} %get-tuple-element.50.refs_2_, bf16[576,192]{1,0:T(8,128)(2,1)S(1)} %get-tuple-element.43.refs_2_.refs_3_, ...), custom_call_target="tpu_custom_call" | custom-call | tf_op jit(solution)/shard_map/second/pallas_call | solution.py:553
  58.2 9.0 %all_to_all.11.field_ref = f32[32,4,128]{2,1,0:T(4,128)S(1)} all-to-all(f32[32,4,128]{2,1,0:T(4,128)S(1)} %get-tuple-element.59), channel_id=1, replica_groups=mesh['space'=4,'date'=8] {'space','date'}, dimensions={0} | all-to-all | bytes 131072 | tf_op jit(solution)/shard_map/all_to_all | solution.py:564
  67.2 0.8 %last.1 = f32[8,64]{1,0:T(8,128)} custom-call(f32[32,4,128]{2,1,0:T(4,128)S(1)} %all_to_all.11.field_ref), custom_call_target="tpu_custom_call" | custom-call | tf_op jit(solution)/shard_map/last/pallas_call | solution.py:565
Async XLA Ops:
  3.1 11.3 %copy-start.2 = (bf16[784,128]{1,0:T(8,128)(2,1)S(1)}, bf16[784,128]{1,0:T(8,128)(2,1)}, u32[]{:S(2)}) copy-start(bf16[784,128]{1,0:T(8,128)(2,1)} %get-tuple-element.33) | copy-start | bytes 602116
  3.1 24.9 %copy-start.1 = (bf16[784,128]{1,0:T(8,128)(2,1)S(1)}, bf16[784,128]{1,0:T(8,128)(2,1)}, u32[]{:S(2)}) copy-start(bf16[784,128]{1,0:T(8,128)(2,1)} %get-tuple-element.36) | copy-start | bytes 602116
  3.1 11.2 %collective-permute-start = (bf16[784,128]{1,0:T(8,128)(2,1)}, bf16[784,128]{1,0:T(8,128)(2,1)S(1)}, u32[]{:S(2)}, u32[]{:S(2)}) collective-permute-start(bf16[784,128]{1,0:T(8,128)(2,1)} %get-tuple-element.32), channel_id=1, source_target_pairs={{0,6},{1,7},{2,4},{3,5},{4,2},{5,3},{6,0},{7,1},{8,14},{9,15},{10,... | collective-permute-start | bytes 602120 | tf_op jit(solution)/shard_map/ppermute | solution.py:503
  8.2 19.7 %collective-permute-start.2 = (bf16[784,128]{1,0:T(8,128)(2,1)}, bf16[784,128]{1,0:T(8,128)(2,1)S(1)}, u32[]{:S(2)}, u32[]{:S(2)}) collective-permute-start(bf16[784,128]{1,0:T(8,128)(2,1)} %get-tuple-element.35), channel_id=1, source_target_pairs={{0,4},{1,5},{2,6},{3,7},{4,0},{5,1},{6,2},{7,3},{8,12},{9,13},{10,... | collective-permute-start | bytes 602120 | tf_op jit(solution)/shard_map/ppermute | solution.py:503
  10.7 19.7 %collective-permute-start.4 = (bf16[784,128]{1,0:T(8,128)(2,1)}, bf16[784,128]{1,0:T(8,128)(2,1)S(1)}, u32[]{:S(2)}, u32[]{:S(2)}) collective-permute-start(bf16[784,128]{1,0:T(8,128)(2,1)} %get-tuple-element.38), channel_id=1, source_target_pairs={{0,1},{1,0},{2,3},{3,2},{4,5},{5,4},{6,7},{7,6},{8,9},{9,8},{10,11... | collective-permute-start | bytes 602120 | tf_op jit(solution)/shard_map/ppermute | solution.py:503
  12.2 18.2 %collective-permute-start.5 = (bf16[784,128]{1,0:T(8,128)(2,1)}, bf16[784,128]{1,0:T(8,128)(2,1)S(1)}, u32[]{:S(2)}, u32[]{:S(2)}) collective-permute-start(bf16[784,128]{1,0:T(8,128)(2,1)} %get-tuple-element.39), channel_id=1, source_target_pairs={{0,2},{1,3},{2,0},{3,1},{4,6},{5,7},{6,4},{7,5},{8,10},{9,11},{10,... | collective-permute-start | bytes 602120 | tf_op jit(solution)/shard_map/ppermute | solution.py:503
  13.0 17.4 %collective-permute-start.6 = (bf16[784,128]{1,0:T(8,128)(2,1)}, bf16[784,128]{1,0:T(8,128)(2,1)S(1)}, u32[]{:S(2)}, u32[]{:S(2)}) collective-permute-start(bf16[784,128]{1,0:T(8,128)(2,1)} %get-tuple-element.40), channel_id=1, source_target_pairs={{0,3},{1,2},{2,1},{3,0},{4,7},{5,6},{6,5},{7,4},{8,11},{9,10},{10,... | collective-permute-start | bytes 602120 | tf_op jit(solution)/shard_map/ppermute | solution.py:503
  14.3 26.0 %collective-permute-start.1 = (bf16[784,128]{1,0:T(8,128)(2,1)S(1)}, bf16[784,128]{1,0:T(8,128)(2,1)S(1)}, u32[]{:S(2)}, u32[]{:S(2)}) collective-permute-start(bf16[784,128]{1,0:T(8,128)(2,1)S(1)} %copy-done.2), channel_id=1, source_target_pairs={{0,5},{1,4},{2,7},{3,6},{4,1},{5,0},{6,3},{7,2},{8,13},{9,12},{10,... | collective-permute-start | bytes 602120 | tf_op jit(solution)/shard_map/ppermute | solution.py:503
  28.0 12.3 %collective-permute-start.3 = (bf16[784,128]{1,0:T(8,128)(2,1)S(1)}, bf16[784,128]{1,0:T(8,128)(2,1)S(1)}, u32[]{:S(2)}, u32[]{:S(2)}) collective-permute-start(bf16[784,128]{1,0:T(8,128)(2,1)S(1)} %copy-done.1), channel_id=1, source_target_pairs={{0,7},{1,6},{2,5},{3,4},{4,3},{5,2},{6,1},{7,0},{8,15},{9,14},{10,... | collective-permute-start | bytes 602120 | tf_op jit(solution)/shard_map/ppermute | solution.py:503
  30.4 0.9 %copy-start = (bf16[784,128]{1,0:T(8,128)(2,1)S(1)}, bf16[784,128]{1,0:T(8,128)(2,1)}, u32[]{:S(2)}) copy-start(bf16[784,128]{1,0:T(8,128)(2,1)} %get-tuple-element.37.refs_0_) | copy-start | bytes 602116

commit v5 on v4

--- a/solution.py
+++ b/solution.py
@@ -53,9 +53,9 @@
     out_ref[...] = design_info(day_ref, dates)
 
 
-def pack_kernel(steps, day_ref, obs_ref, valid_ref, *refs):
+def pack_kernel(steps, far, day_ref, obs_ref, valid_ref, *refs):
     outs = refs[: 2 * len(steps)]
-    day_here, obs_here, valid_here, sems, day_sem = refs[2 * len(steps) :]
+    day_here, obs_here, valid_here, sems, day_sem = refs[-5:]
     me = lax.axis_index("date")
     odd = lax.rem(me, 2) == 1
     bands, dates = obs_ref.shape[:2]
@@ -110,8 +110,9 @@
             here = slice(band * rows, (band + 1) * rows)
             outs[2 * place][here, :] = same.reshape(rows, LANES).astype(bf16)
             outs[2 * place + 1][here, :] = other.reshape(rows, LANES).astype(bf16)
-        for n in (0, 1):
-            outs[2 * place + n][(bands + 1) * rows :, :] = info
+        outs[2 * place][(bands + 1) * rows :, :] = info
+        if not far:
+            outs[2 * place + 1][(bands + 1) * rows :, :] = info
 
 
 def packed_blocks(obs, valid, days, count, me, width):
@@ -125,13 +126,17 @@
     if width == 64 and rows == 8:
         hbm = pl.BlockSpec(memory_space=pltpu.HBM)
         blocks = [None] * count
+        long_shape = jax.ShapeDtypeStruct((size + INFO_ROWS, LANES), bf16)
+        short_shape = jax.ShapeDtypeStruct((size, LANES), bf16)
         for steps in (range(half // 2, half), range(half // 2)):
             tiles = len(steps)
-            blocks[2 * steps[0] : 2 * steps[-1] + 2] = pl.pallas_call(
-                functools.partial(pack_kernel, tuple(steps)),
-                out_shape=[jax.ShapeDtypeStruct((size + INFO_ROWS, LANES), bf16)] * (2 * tiles),
+            far = steps[0] > 0
+            shapes = [long_shape, short_shape if far else long_shape] * tiles
+            given = pl.pallas_call(
+                functools.partial(pack_kernel, tuple(steps), far),
+                out_shape=shapes,
                 in_specs=[hbm] * 3,
-                out_specs=[vmem] * (2 * tiles),
+                out_specs=[vmem] * len(shapes),
                 scratch_shapes=[
                     pltpu.SMEM((dates,), jnp.int32),
                     pltpu.VMEM((tiles, bands, dates, rows, LANES), bf16),
@@ -142,6 +147,7 @@
                 compiler_params=pltpu.CompilerParams(vmem_limit_bytes=PACK_VMEM_BYTES),
                 name="pack",
             )(days, obs, valid)
+            blocks[2 * steps[0] : 2 * steps[-1] + 2] = given
         return blocks
     info = pl.pallas_call(
         functools.partial(info_kernel, dates),
@@ -157,7 +163,9 @@
     whole = jnp.concatenate(
         [whole, jnp.broadcast_to(info[None], (count, INFO_ROWS, LANES))], axis=1
     )
-    return [lax.dynamic_index_in_dim(whole, me ^ k, 0, keepdims=False) for k in range(count)]
+    blocks = [lax.dynamic_index_in_dim(whole, me ^ k, 0, keepdims=False) for k in range(count)]
+    blocks[half + 1 :: 2] = [block[:size] for block in blocks[half + 1 :: 2]]
+    return blocks
 
 
 def solve(gram, cross, bands):
@@ -260,17 +268,17 @@
     return left, gram_left, x_wide
 
 
-def absorb(blocks, bands, dates, parts, outs, product_ref):
-    left_ref, gram_left_ref, x_ref, y_ref, mask_ref = outs
+def keep_design(infos, dates, parts, outs):
+    left, gram_left, x_wide = design_of(infos, dates, parts)
+    used = len(pairs) * parts
+    outs[0][...] = left
+    for c in range(3):
+        outs[1][c * used : (c + 1) * used, :] = gram_left[c]
+    outs[2][...] = x_wide
+
+
+def absorb(blocks, bands, dates, parts, left_ref, gram_left_ref, y_ref, mask_ref, product_ref):
     rows = dates * parts
-    left, gram_left, x_wide = design_of(
-        [block[(bands + 1) * rows :, :] for block in blocks], dates, parts
-    )
-    left_ref[...] = left
-    x_ref[...] = x_wide
-    used = len(pairs) * parts
-    for c in range(3):
-        gram_left_ref[c * used : (c + 1) * used, :] = gram_left[c]
     for n, block in enumerate(blocks):
         here = slice(n * rows, (n + 1) * rows)
         mask = block[bands * rows : (bands + 1) * rows, :]
@@ -280,24 +288,21 @@
             y_ref[here, b * LANES : (b + 1) * LANES] = y
             product_ref[here, b * LANES : (b + 1) * LANES] = y * mask
     cross_sum = add_parts(dot(left_ref[...], product_ref[...]), TERMS * parts)
-    gram_sum = add_parts(dot(gram_left_ref[...], mask_ref[...]), used)
+    gram_sum = add_parts(dot(gram_left_ref[...], mask_ref[...]), len(pairs) * parts)
     return cross_sum, gram_sum
 
 
-def single_blocks(refs):
-    blocks = []
-    for ref in refs:
-        blocks += [ref] if len(ref.shape) == 2 else [ref.at[n] for n in range(ref.shape[0])]
-    return blocks
-
-
-def absorb_kernel(shape, *refs):
+def absorb_kernel(shape, early_count, late_count, *refs):
     bands, dates, parts = shape
-    outs, sums, product_ref = refs[-8:-3], refs[-3:-1], refs[-1]
-    blocks = single_blocks(refs[:-8])
-    cross_sum, gram_sum = absorb(blocks, bands, dates, parts, outs, product_ref)
-    sums[0][...] = cross_sum
-    sums[1][...] = gram_sum
+    blocks, info_ref = refs[:early_count], refs[early_count]
+    infos = [info_ref[n * INFO_ROWS : (n + 1) * INFO_ROWS, :] for n in range(late_count)]
+    early, late, sums = refs[-11:-6], refs[-6:-3], refs[-3:-1]
+    start = (bands + 1) * dates * parts
+    keep_design([block[start:, :] for block in blocks], dates, parts, early[:3])
+    keep_design(infos, dates, parts, late)
+    sums[0][...], sums[1][...] = absorb(
+        blocks, bands, dates, parts, early[0], early[1], early[3], early[4], refs[-1]
+    )
 
 
 def fit_and_spread(parts, bands, gram_sum, cross_sum, groups):
@@ -332,14 +337,15 @@
     return beta, spread / (1.0 + gram[0, 0])
 
 
-def first_kernel(shape, arrays, *refs):
+def first_kernel(shape, late_count, *refs):
     bands, dates, parts = shape
-    blocks = single_blocks(refs[:arrays])
-    early_x, early_y, early_mask, early_cross, early_gram = refs[arrays : arrays + 5]
-    outs = refs[arrays + 5 : arrays + 10]
-    early_power, late_power, variance_ref, product_ref = refs[arrays + 10 :]
-    cross_sum, gram_sum = absorb(blocks, bands, dates, parts, outs, product_ref)
-    _, _, x_ref, y_ref, mask_ref = outs
+    blocks = refs[:late_count]
+    left_ref, gram_left_ref, x_ref = refs[late_count : late_count + 3]
+    early_x, early_y, early_mask, early_cross, early_gram = refs[late_count + 3 : late_count + 8]
+    y_ref, mask_ref, early_power, late_power, variance_ref, product_ref = refs[late_count + 8 :]
+    cross_sum, gram_sum = absorb(
+        blocks, bands, dates, parts, left_ref, gram_left_ref, y_ref, mask_ref, product_ref
+    )
     groups = [
         (early_y, early_x, early_power, lambda here: early_mask[here, :].astype(f32)),
         (y_ref, x_ref, late_power, lambda here: mask_ref[here, :].astype(f32)),
@@ -509,14 +515,20 @@
     for k in range(half, count, 2):
         swap(k + 1, after=k ^ 2)
 
+    infos = jnp.concatenate([block[-INFO_ROWS:] for block in received[half::2]], axis=0)
+    infos = lax.ppermute(infos, "date", [(i, i ^ 1) for i in range(count)])
     early_blocks = [*received[:half], *received[half::2]]
     late_blocks = received[half + 1 :: 2]
 
-    def group_shapes(total):
+    def design_shapes(total):
         return [
             jax.ShapeDtypeStruct((3 * TERMS * parts, total), bf16),
             jax.ShapeDtypeStruct((3 * len(pairs) * parts, total), bf16),
             jax.ShapeDtypeStruct((total, 6 * TERMS * parts), bf16),
+        ]
+
+    def data_shapes(total):
+        return [
             jax.ShapeDtypeStruct((total, bands * LANES), bf16),
             jax.ShapeDtypeStruct((total, LANES), bf16),
         ]
@@ -529,24 +541,29 @@
         jax.ShapeDtypeStruct((len(pairs) * parts, LANES), f32),
     ]
     send = jax.ShapeDtypeStruct((spaces * count, parts, LANES), f32)
-    *early, early_cross, early_gram = pl.pallas_call(
-        functools.partial(absorb_kernel, (bands, dates, parts)),
-        out_shape=group_shapes(early_rows) + sums,
-        in_specs=[vmem] * len(early_blocks),
-        out_specs=[vmem] * 7,
+    given = pl.pallas_call(
+        functools.partial(absorb_kernel, (bands, dates, parts), early_count, late_count),
+        out_shape=design_shapes(early_rows)
+        + data_shapes(early_rows)
+        + design_shapes(late_rows)
+        + sums,
+        in_specs=[vmem] * (early_count + 1),
+        out_specs=[vmem] * 10,
         scratch_shapes=[pltpu.VMEM((early_rows, bands * LANES), bf16)],
         compiler_params=params,
         name="absorb",
-    )(*early_blocks)
-    *late, early_power, late_power, variance = pl.pallas_call(
-        functools.partial(first_kernel, (bands, dates, parts), len(late_blocks)),
-        out_shape=group_shapes(late_rows) + [power(early_rows), power(late_rows), send],
-        in_specs=[vmem] * (len(late_blocks) + 5),
-        out_specs=[vmem] * 8,
+    )(*early_blocks, infos)
+    early, late, early_sums = given[:5], given[5:8], given[8:]
+    *late_data, early_power, late_power, variance = pl.pallas_call(
+        functools.partial(first_kernel, (bands, dates, parts), late_count),
+        out_shape=data_shapes(late_rows) + [power(early_rows), power(late_rows), send],
+        in_specs=[vmem] * (late_count + 8),
+        out_specs=[vmem] * 5,
         scratch_shapes=[pltpu.VMEM((late_rows, bands * LANES), bf16)],
         compiler_params=params,
         name="first",
-    )(*late_blocks, early[2], early[3], early[4], early_cross, early_gram)
+    )(*late_blocks, *late, *early[2:], *early_sums)
+    late = [*late, *late_data]
 
     field = lax.all_to_all(variance, ("space", "date"), 0, 0, tiled=True)
     total = early_rows + late_rows

time: 68.2 us -> 67.3 us (0.987)
  waiting for transfers between devices: 10.7 us -> 9.38 us
    ppermute x7, waiting for transfers between devices: 10.7 us -> 5.49 us  [swap(): lax.ppermute(block, 'date', [(i, i ^ k) for i in range(count)])]
    ppermute x0 -> x1, waiting for transfers between devices: none -> 3.88 us  [on_device(): infos = lax.ppermute(infos, 'date', [(i, i ^ 1) for i in range(count)])]
  transfers between devices with their start and end apart: 7 -> 8, of which waited for: 3 -> 4; matrix products, arithmetic and copies ran while one was open for 0% -> 0% of each run, Pallas kernels for 6% -> 7%
where the time goes in v5:
time: 67.3 us; the launch traced here: 67.1 us
  starting transfers between devices  22.2 us (33%)
  blocking collectives  22.2 us (33%)
  Pallas kernels  11.7 us (17%)
  waiting for transfers between devices  9.38 us (14%)
  local copies, waits for them, and re-layouts  0.94 us (1%)
  between operations  0.69 us (1%)
    all_to_all x2, blocking collectives, on_device(): field = lax.all_to_all(variance, ('space', 'date'), 0, 0, tiled=True)  22.2 us
    ppermute x7, starting transfers between devices, swap(): lax.ppermute(block, 'date', [(i, i ^ k) for i in range(count)])  21.6 us
    ppermute x7, waiting for transfers between devices, swap(): lax.ppermute(block, 'date', [(i, i ^ k) for i in range(count)])  5.49 us
    pallas_call x2, Pallas kernels, packed_blocks(): pl.pallas_call(functools.partial(pack_kernel, tuple(steps), far), out_sha...  4.87 us
    ppermute x1, waiting for transfers between devices, on_device(): infos = lax.ppermute(infos, 'date', [(i, i ^ 1) for i in range(count)])  3.88 us
    pallas_call x1, Pallas kernels, on_device(): pl.pallas_call(functools.partial(second_kernel, shape), out_shape=[jax.Sh...  2.85 us
    pallas_call x1, Pallas kernels, on_device(): pl.pallas_call(functools.partial(absorb_kernel, (bands, dates, parts), ea...  1.96 us
  transfers between devices with their start and end apart: 8, of which 4 were waited for; matrix products, arithmetic and copies ran while one was open for 0% of the time, Pallas kernels for 7%

profile of v5, /device:TPU:0, one launch (start us, length us, event | category | flops | bytes accessed | tf_op | source)
XLA Modules:
  0.0 67.1 jit_solution(4602514298454989854)
XLA Ops:
  0.6 2.4 %pack.2 = (bf16[784,128]{1,0:T(8,128)(2,1)}, bf16[768,128]{1,0:T(8,128)(2,1)}, bf16[784,128]{1,0:T(8,128)(2,1)}, bf16[768,128]{1,0:T(8,128)(2,1)}) custom-call(s32[24]{0:T(128)} %day_ref.3, bf16[7,24,8,512]{3,2,1,0:T(8,128)(2,1)} %obs_ref.3, s32[24,8,512]{2,1,0:T(8,128)} %valid_ref.3), custom_call_target="tpu_custom_call" | custom-call | tf_op jit(solution)/shard_map/pack/pallas_call | solution.py:135
  3.1 0.0 copy-start.2
  3.1 0.0 copy-start.1
  3.1 5.1 %collective-permute-start = (bf16[784,128]{1,0:T(8,128)(2,1)}, bf16[784,128]{1,0:T(8,128)(2,1)S(1)}, u32[]{:S(2)}, u32[]{:S(2)}) collective-permute-start(bf16[784,128]{1,0:T(8,128)(2,1)} %get-tuple-element.32), channel_id=1, source_target_pairs={{0,6},{1,7},{2,4},{3,5},{4,2},{5,3},{6,0},{7,1},{8,14},{9,15},{10,... | collective-permute-start | bytes 602120 | tf_op jit(solution)/shard_map/ppermute | solution.py:509
  8.2 0.0 collective-permute-start.2
  8.2 2.4 %pack.3 = (bf16[784,128]{1,0:T(8,128)(2,1)}, bf16[784,128]{1,0:T(8,128)(2,1)}, bf16[784,128]{1,0:T(8,128)(2,1)}, bf16[784,128]{1,0:T(8,128)(2,1)}) custom-call(s32[24]{0:T(128)} %day_ref.3, bf16[7,24,8,512]{3,2,1,0:T(8,128)(2,1)} %obs_ref.3, s32[24,8,512]{2,1,0:T(8,128)} %valid_ref.3), custom_call_target="tpu_custom_call" | custom-call | tf_op jit(solution)/shard_map/pack/pallas_call | solution.py:135
  10.6 1.6 %collective-permute-start.4 = (bf16[784,128]{1,0:T(8,128)(2,1)}, bf16[784,128]{1,0:T(8,128)(2,1)S(1)}, u32[]{:S(2)}, u32[]{:S(2)}) collective-permute-start(bf16[784,128]{1,0:T(8,128)(2,1)} %get-tuple-element.38), channel_id=1, source_target_pairs={{0,1},{1,0},{2,3},{3,2},{4,5},{5,4},{6,7},{7,6},{8,9},{9,8},{10,11... | collective-permute-start | bytes 602120 | tf_op jit(solution)/shard_map/ppermute | solution.py:509
  12.2 0.8 %collective-permute-start.5 = (bf16[784,128]{1,0:T(8,128)(2,1)}, bf16[784,128]{1,0:T(8,128)(2,1)S(1)}, u32[]{:S(2)}, u32[]{:S(2)}) collective-permute-start(bf16[784,128]{1,0:T(8,128)(2,1)} %get-tuple-element.39), channel_id=1, source_target_pairs={{0,2},{1,3},{2,0},{3,1},{4,6},{5,7},{6,4},{7,5},{8,10},{9,11},{10,... | collective-permute-start | bytes 602120 | tf_op jit(solution)/shard_map/ppermute | solution.py:509
  13.0 1.2 %collective-permute-start.6 = (bf16[784,128]{1,0:T(8,128)(2,1)}, bf16[784,128]{1,0:T(8,128)(2,1)S(1)}, u32[]{:S(2)}, u32[]{:S(2)}) collective-permute-start(bf16[784,128]{1,0:T(8,128)(2,1)} %get-tuple-element.40), channel_id=1, source_target_pairs={{0,3},{1,2},{2,1},{3,0},{4,7},{5,6},{6,5},{7,4},{8,11},{9,10},{10,... | collective-permute-start | bytes 602120 | tf_op jit(solution)/shard_map/ppermute | solution.py:509
  14.2 0.1 collective-permute-done.refs_5_
  14.3 0.0 copy-done.2
  14.3 10.5 %collective-permute-start.1 = (bf16[768,128]{1,0:T(8,128)(2,1)S(1)}, bf16[768,128]{1,0:T(8,128)(2,1)S(1)}, u32[]{:S(2)}, u32[]{:S(2)}) collective-permute-start(bf16[768,128]{1,0:T(8,128)(2,1)S(1)} %copy-done.2), channel_id=1, source_target_pairs={{0,5},{1,4},{2,7},{3,6},{4,1},{5,0},{6,3},{7,2},{8,13},{9,12},{10,... | collective-permute-start | bytes 589832 | tf_op jit(solution)/shard_map/ppermute | solution.py:509
  24.8 3.1 %collective-permute-done.2.refs_4_ = bf16[784,128]{1,0:T(8,128)(2,1)S(1)} collective-permute-done((bf16[784,128]{1,0:T(8,128)(2,1)}, bf16[784,128]{1,0:T(8,128)(2,1)S(1)}, u32[]{:S(2)}, u32[]{:S(2)}) %collective-permute-start.2) | collective-permute-done | bytes 200736 | tf_op jit(solution)/shard_map/ppermute | solution.py:509
  27.9 0.0 copy-done.1
  27.9 2.4 %collective-permute-start.3 = (bf16[768,128]{1,0:T(8,128)(2,1)S(1)}, bf16[768,128]{1,0:T(8,128)(2,1)S(1)}, u32[]{:S(2)}, u32[]{:S(2)}) collective-permute-start(bf16[768,128]{1,0:T(8,128)(2,1)S(1)} %copy-done.1), channel_id=1, source_target_pairs={{0,7},{1,6},{2,5},{3,4},{4,3},{5,2},{6,1},{7,0},{8,15},{9,14},{10,... | collective-permute-start | bytes 589832 | tf_op jit(solution)/shard_map/ppermute | solution.py:509
  30.4 0.0 collective-permute-done.4.refs_1_
  30.4 0.6 collective-permute-start.7
  31.0 0.0 collective-permute-done.5.refs_2_
  31.0 0.0 collective-permute-done.6.refs_3_
  31.0 3.9 %collective-permute-done.7.refs_6_ = bf16[32,128]{1,0:T(8,128)(2,1)S(1)} collective-permute-done((bf16[32,128]{1,0:T(8,128)(2,1)S(1)}, bf16[32,128]{1,0:T(8,128)(2,1)S(1)}, u32[]{:S(2)}, u32[]{:S(2)}) %collective-permute-start.7) | collective-permute-done | bytes 8224 | tf_op jit(solution)/shard_map/ppermute | solution.py:519
  34.9 0.0 copy-start
  34.9 0.9 %copy-done = bf16[784,128]{1,0:T(8,128)(2,1)S(1)} copy-done((bf16[784,128]{1,0:T(8,128)(2,1)S(1)}, bf16[784,128]{1,0:T(8,128)(2,1)}, u32[]{:S(2)}) %copy-start) | copy-done | bytes 200728
  35.8 2.0 %absorb.1 = (bf16[96,576]{1,0:T(8,128)(2,1)S(1)}, bf16[432,576]{1,0:T(8,128)(2,1)S(1)}, bf16[576,192]{1,0:T(8,128)(2,1)S(1)}, bf16[576,896]{1,0:T(8,128)(2,1)S(1...) custom-call(bf16[784,128]{1,0:T(8,128)(2,1)S(1)} %copy-done, ...), custom_call_target="tpu_custom_call" | custom-call | tf_op jit(solution)/shard_map/absorb/pallas_call | solution.py:544
  37.8 2.2 %collective-permute-done.1.refs_0_ = bf16[768,128]{1,0:T(8,128)(2,1)S(1)} collective-permute-done((bf16[768,128]{1,0:T(8,128)(2,1)S(1)}, bf16[768,128]{1,0:T(8,128)(2,1)S(1)}, u32[]{:S(2)}, u32[]{:S(2)}) %collective-permute-start.1) | collective-permute-done | bytes 196640 | tf_op jit(solution)/shard_map/ppermute | solution.py:509
  40.0 0.0 collective-permute-done.3.refs_1_
  40.0 1.2 %first.1 = (bf16[192,896]{1,0:T(8,128)(2,1)S(1)}, bf16[192,128]{1,0:T(8,128)(2,1)S(1)}, f32[576,128]{1,0:T(8,128)S(1)}, f32[192,128]{1,0:T(8,128)S(1)}, f32[32,4,128]{2,1,0:T(4,128)S(1)}) custom-call(bf16[768,128]{1,0:T(8,128)(2,1)S(1)} %collective-permute-done.1.refs_0_, bf16[768,128]{1,0:T(8,128)(2,1)S(1)} %collective-permute-done.3.refs_1_, ...), custom_call_target="tpu_custom_call" | custom-call | tf_op jit(solution)/shard_map/first/pallas_call | solution.py:557
  41.3 13.2 %all_to_all.10.refs_0_ = f32[32,4,128]{2,1,0:T(4,128)S(1)} all-to-all(f32[32,4,128]{2,1,0:T(4,128)S(1)} %get-tuple-element.51), channel_id=1, replica_groups=mesh['space'=4,'date'=8] {'space','date'}, dimensions={0} | all-to-all | bytes 131072 | tf_op jit(solution)/shard_map/all_to_all | solution.py:568
  54.5 2.9 %second.1 = (f32[7,8,8,64]{3,2,1,0:T(8,128)}, f32[32,4,128]{2,1,0:T(4,128)S(1)}) custom-call(f32[32,4,128]{2,1,0:T(4,128)S(1)} %all_to_all.10.refs_0_, bf16[96,576]{1,0:T(8,128)(2,1)S(1)} %get-tuple-element.52.refs_1_, bf16[432,576]{1,0:T(8,128)(2,1)S(1)} %get-tuple-element.53.refs_2_, bf16[576,192]{1,0:T(8,128)(2,1)S(1)} %get-tuple-element.46.refs_5_.refs_3_, ...), custom_call_target="tpu_custom_call" | custom-call | tf_op jit(solution)/shard_map/second/pallas_call | solution.py:570
  57.3 9.0 %all_to_all.11.field_ref = f32[32,4,128]{2,1,0:T(4,128)S(1)} all-to-all(f32[32,4,128]{2,1,0:T(4,128)S(1)} %get-tuple-element.59), channel_id=1, replica_groups=mesh['space'=4,'date'=8] {'space','date'}, dimensions={0} | all-to-all | bytes 131072 | tf_op jit(solution)/shard_map/all_to_all | solution.py:581
  66.3 0.8 %last.1 = f32[8,64]{1,0:T(8,128)} custom-call(f32[32,4,128]{2,1,0:T(4,128)S(1)} %all_to_all.11.field_ref), custom_call_target="tpu_custom_call" | custom-call | tf_op jit(solution)/shard_map/last/pallas_call | solution.py:582
  (3 shorter events, 0.0 us)
Async XLA Ops:
  3.1 11.3 %copy-start.2 = (bf16[768,128]{1,0:T(8,128)(2,1)S(1)}, bf16[768,128]{1,0:T(8,128)(2,1)}, u32[]{:S(2)}) copy-start(bf16[768,128]{1,0:T(8,128)(2,1)} %get-tuple-element.33) | copy-start | bytes 589828
  3.1 24.9 %copy-start.1 = (bf16[768,128]{1,0:T(8,128)(2,1)S(1)}, bf16[768,128]{1,0:T(8,128)(2,1)}, u32[]{:S(2)}) copy-start(bf16[768,128]{1,0:T(8,128)(2,1)} %get-tuple-element.36) | copy-start | bytes 589828
  3.1 11.2 %collective-permute-start = (bf16[784,128]{1,0:T(8,128)(2,1)}, bf16[784,128]{1,0:T(8,128)(2,1)S(1)}, u32[]{:S(2)}, u32[]{:S(2)}) collective-permute-start(bf16[784,128]{1,0:T(8,128)(2,1)} %get-tuple-element.32), channel_id=1, source_target_pairs={{0,6},{1,7},{2,4},{3,5},{4,2},{5,3},{6,0},{7,1},{8,14},{9,15},{10,... | collective-permute-start | bytes 602120 | tf_op jit(solution)/shard_map/ppermute | solution.py:509
  8.2 19.7 %collective-permute-start.2 = (bf16[784,128]{1,0:T(8,128)(2,1)}, bf16[784,128]{1,0:T(8,128)(2,1)S(1)}, u32[]{:S(2)}, u32[]{:S(2)}) collective-permute-start(bf16[784,128]{1,0:T(8,128)(2,1)} %get-tuple-element.35), channel_id=1, source_target_pairs={{0,4},{1,5},{2,6},{3,7},{4,0},{5,1},{6,2},{7,3},{8,12},{9,13},{10,... | collective-permute-start | bytes 602120 | tf_op jit(solution)/shard_map/ppermute | solution.py:509
  10.6 19.7 %collective-permute-start.4 = (bf16[784,128]{1,0:T(8,128)(2,1)}, bf16[784,128]{1,0:T(8,128)(2,1)S(1)}, u32[]{:S(2)}, u32[]{:S(2)}) collective-permute-start(bf16[784,128]{1,0:T(8,128)(2,1)} %get-tuple-element.38), channel_id=1, source_target_pairs={{0,1},{1,0},{2,3},{3,2},{4,5},{5,4},{6,7},{7,6},{8,9},{9,8},{10,11... | collective-permute-start | bytes 602120 | tf_op jit(solution)/shard_map/ppermute | solution.py:509
  12.2 18.8 %collective-permute-start.5 = (bf16[784,128]{1,0:T(8,128)(2,1)}, bf16[784,128]{1,0:T(8,128)(2,1)S(1)}, u32[]{:S(2)}, u32[]{:S(2)}) collective-permute-start(bf16[784,128]{1,0:T(8,128)(2,1)} %get-tuple-element.39), channel_id=1, source_target_pairs={{0,2},{1,3},{2,0},{3,1},{4,6},{5,7},{6,4},{7,5},{8,10},{9,11},{10,... | collective-permute-start | bytes 602120 | tf_op jit(solution)/shard_map/ppermute | solution.py:509
  13.0 18.0 %collective-permute-start.6 = (bf16[784,128]{1,0:T(8,128)(2,1)}, bf16[784,128]{1,0:T(8,128)(2,1)S(1)}, u32[]{:S(2)}, u32[]{:S(2)}) collective-permute-start(bf16[784,128]{1,0:T(8,128)(2,1)} %get-tuple-element.40), channel_id=1, source_target_pairs={{0,3},{1,2},{2,1},{3,0},{4,7},{5,6},{6,5},{7,4},{8,11},{9,10},{10,... | collective-permute-start | bytes 602120 | tf_op jit(solution)/shard_map/ppermute | solution.py:509
  14.3 25.7 %collective-permute-start.1 = (bf16[768,128]{1,0:T(8,128)(2,1)S(1)}, bf16[768,128]{1,0:T(8,128)(2,1)S(1)}, u32[]{:S(2)}, u32[]{:S(2)}) collective-permute-start(bf16[768,128]{1,0:T(8,128)(2,1)S(1)} %copy-done.2), channel_id=1, source_target_pairs={{0,5},{1,4},{2,7},{3,6},{4,1},{5,0},{6,3},{7,2},{8,13},{9,12},{10,... | collective-permute-start | bytes 589832 | tf_op jit(solution)/shard_map/ppermute | solution.py:509
  27.9 12.1 %collective-permute-start.3 = (bf16[768,128]{1,0:T(8,128)(2,1)S(1)}, bf16[768,128]{1,0:T(8,128)(2,1)S(1)}, u32[]{:S(2)}, u32[]{:S(2)}) collective-permute-start(bf16[768,128]{1,0:T(8,128)(2,1)S(1)} %copy-done.1), channel_id=1, source_target_pairs={{0,7},{1,6},{2,5},{3,4},{4,3},{5,2},{6,1},{7,0},{8,15},{9,14},{10,... | collective-permute-start | bytes 589832 | tf_op jit(solution)/shard_map/ppermute | solution.py:509
  30.4 4.5 %collective-permute-start.7 = (bf16[32,128]{1,0:T(8,128)(2,1)S(1)}, bf16[32,128]{1,0:T(8,128)(2,1)S(1)}, u32[]{:S(2)}, u32[]{:S(2)}) collective-permute-start(bf16[32,128]{1,0:T(8,128)(2,1)S(1)} %pad_maximum_fusion), channel_id=1, source_target_pairs={{0,1},{1,0},{2,3},{3,2},{4,5},{5,4},{6,7},{7,6},{8,9},{9,8},{10,11... | collective-permute-start | bytes 24584 | tf_op jit(solution)/shard_map/ppermute | solution.py:519
  34.9 0.9 %copy-start = (bf16[784,128]{1,0:T(8,128)(2,1)S(1)}, bf16[784,128]{1,0:T(8,128)(2,1)}, u32[]{:S(2)}) copy-start(bf16[784,128]{1,0:T(8,128)(2,1)} %get-tuple-element.37.refs_0_) | copy-start | bytes 602116

commit v6 on v5

--- a/solution.py
+++ b/solution.py
@@ -277,18 +277,24 @@
     outs[2][...] = x_wide
 
 
-def absorb(blocks, bands, dates, parts, left_ref, gram_left_ref, y_ref, mask_ref, product_ref):
+def absorb(blocks, bands, dates, parts, left_ref, gram_left_ref, y_ref, mask_ref):
     rows = dates * parts
+    masks = []
+    products = []
     for n, block in enumerate(blocks):
         here = slice(n * rows, (n + 1) * rows)
         mask = block[bands * rows : (bands + 1) * rows, :]
         mask_ref[here, :] = mask
+        masks.append(mask)
+        product = []
         for b in range(bands):
             y = block[b * rows : (b + 1) * rows, :]
             y_ref[here, b * LANES : (b + 1) * LANES] = y
-            product_ref[here, b * LANES : (b + 1) * LANES] = y * mask
-    cross_sum = add_parts(dot(left_ref[...], product_ref[...]), TERMS * parts)
-    gram_sum = add_parts(dot(gram_left_ref[...], mask_ref[...]), len(pairs) * parts)
+            product.append(y * mask)
+        products.append(jnp.concatenate(product, axis=1))
+    product = jnp.concatenate(products, axis=0)
+    cross_sum = add_parts(dot(left_ref[...], product), TERMS * parts)
+    gram_sum = add_parts(dot(gram_left_ref[...], jnp.concatenate(masks, axis=0)), len(pairs) * parts)
     return cross_sum, gram_sum
 
 
@@ -296,12 +302,12 @@
     bands, dates, parts = shape
     blocks, info_ref = refs[:early_count], refs[early_count]
     infos = [info_ref[n * INFO_ROWS : (n + 1) * INFO_ROWS, :] for n in range(late_count)]
-    early, late, sums = refs[-11:-6], refs[-6:-3], refs[-3:-1]
+    early, late, sums = refs[-10:-5], refs[-5:-2], refs[-2:]
     start = (bands + 1) * dates * parts
     keep_design([block[start:, :] for block in blocks], dates, parts, early[:3])
     keep_design(infos, dates, parts, late)
     sums[0][...], sums[1][...] = absorb(
-        blocks, bands, dates, parts, early[0], early[1], early[3], early[4], refs[-1]
+        blocks, bands, dates, parts, early[0], early[1], early[3], early[4]
     )
 
 
@@ -318,21 +324,19 @@
     )
     high, mid, low = split3_kernel(flat)
     right = jnp.concatenate([high, high, high, mid, mid, low], axis=0)
-    step = 96
     spread = jnp.zeros((8, LANES), f32)
     for y_ref, x_ref, power_ref, weight_of in groups:
-        for start in range(0, y_ref.shape[0], step):
-            here = slice(start, start + step)
-            misfit = y_ref[here, :].astype(f32) - dot(x_ref[here, :], right)
-            power = jnp.zeros((step, LANES), f32)
-            for b in range(bands):
-                part = misfit[:, b * LANES : (b + 1) * LANES]
-                power = power + part * part
-            power = power / bands
-            if power_ref is not None:
-                power_ref[here, :] = power
-            weighted = weight_of(here) * power
-            spread = spread + jnp.sum(weighted.reshape(step // 8, 8, LANES), axis=0)
+        size = y_ref.shape[0]
+        misfit = y_ref[...].astype(f32) - dot(x_ref[...], right)
+        power = jnp.zeros((size, LANES), f32)
+        for b in range(bands):
+            part = misfit[:, b * LANES : (b + 1) * LANES]
+            power = power + part * part
+        power = power / bands
+        if power_ref is not None:
+            power_ref[...] = power
+        weighted = weight_of() * power
+        spread = spread + jnp.sum(weighted.reshape(size // 8, 8, LANES), axis=0)
     spread = add_parts(spread, parts)
     return beta, spread / (1.0 + gram[0, 0])
 
@@ -342,13 +346,13 @@
     blocks = refs[:late_count]
     left_ref, gram_left_ref, x_ref = refs[late_count : late_count + 3]
     early_x, early_y, early_mask, early_cross, early_gram = refs[late_count + 3 : late_count + 8]
-    y_ref, mask_ref, early_power, late_power, variance_ref, product_ref = refs[late_count + 8 :]
+    y_ref, mask_ref, early_power, late_power, variance_ref = refs[late_count + 8 :]
     cross_sum, gram_sum = absorb(
-        blocks, bands, dates, parts, left_ref, gram_left_ref, y_ref, mask_ref, product_ref
+        blocks, bands, dates, parts, left_ref, gram_left_ref, y_ref, mask_ref
     )
     groups = [
-        (early_y, early_x, early_power, lambda here: early_mask[here, :].astype(f32)),
-        (y_ref, x_ref, late_power, lambda here: mask_ref[here, :].astype(f32)),
+        (early_y, early_x, early_power, lambda: early_mask[...].astype(f32)),
+        (y_ref, x_ref, late_power, lambda: mask_ref[...].astype(f32)),
     ]
     _, variance = fit_and_spread(
         parts, bands, gram_sum + early_gram[...], cross_sum + early_cross[...], groups
@@ -420,52 +424,46 @@
     field_ref = refs[0]
     groups = [refs[1:7], refs[7:13]]
     coefficient_ref, variance_ref = refs[13:15]
-    weight_ref, w_parts, wy_parts = refs[15], refs[16:18], refs[18:20]
+    weight_ref = refs[15]
     smooth = smoothed(field_ref, parts, width, rows, spaces, count)
     smooth = to_lanes(smooth, parts, width)
     scale = 1.0 / (TUKEY * TUKEY * (smooth + EPS))
     scale = jnp.concatenate([scale] * (8 // parts), axis=0)
     early = groups[0][3].shape[0]
-    step = 96
-    for base, (_, _, _, y_ref, mask_ref, power_ref) in zip((0, early), groups):
-        for start in range(0, y_ref.shape[0], step):
-            here = slice(start, start + step)
-            there = slice(base + start, base + start + step)
-            power = power_ref[here, :].reshape(step // 8, 8, LANES)
-            left_over = 1.0 - jnp.minimum(power * scale[None], 1.0)
-            mask = mask_ref[here, :].astype(f32)
-            weight = mask * (left_over * left_over).reshape(step, LANES)
-            weight_ref[there, :] = weight
-            for ref, part in zip(w_parts, split2_kernel(weight)):
-                ref[there, :] = part
-            for b in range(bands):
-                y = y_ref[here, b * LANES : (b + 1) * LANES].astype(f32)
-                for ref, part in zip(wy_parts, split2_kernel(weight * y)):
-                    ref[there, b * LANES : (b + 1) * LANES] = part
-
-    def moments(place, b_refs, size):
-        total = 0.0
-        for base, group in zip((0, early), groups):
-            a_ref = group[place]
-            there = slice(base, base + group[3].shape[0])
-            total = total + add_parts(dot(a_ref[...], b_refs[0][there, :]), size)
-            total = total + add_parts(dot(a_ref[0 : 2 * size, :], b_refs[1][there, :]), size)
-        return total
-
-    cross_sum = moments(0, wy_parts, TERMS * parts)
-    gram_sum = moments(1, w_parts, len(pairs) * parts)
+    cross_sum = gram_sum = 0.0
+    for base, (left_ref, gram_left_ref, _, y_ref, mask_ref, power_ref) in zip((0, early), groups):
+        size = y_ref.shape[0]
+        power = power_ref[...].reshape(size // 8, 8, LANES)
+        left_over = 1.0 - jnp.minimum(power * scale[None], 1.0)
+        mask = mask_ref[...].astype(f32)
+        weight = mask * (left_over * left_over).reshape(size, LANES)
+        weight_ref[base : base + size, :] = weight
+        wy_parts = [[], []]
+        for b in range(bands):
+            y = y_ref[:, b * LANES : (b + 1) * LANES].astype(f32)
+            for n, part in enumerate(split2_kernel(weight * y)):
+                wy_parts[n].append(part)
+        wy_parts = [jnp.concatenate(part, axis=1) for part in wy_parts]
+
+        def moments(a_ref, b_parts, used):
+            total = add_parts(dot(a_ref[...], b_parts[0]), used)
+            return total + add_parts(dot(a_ref[0 : 2 * used, :], b_parts[1]), used)
+
+        cross_sum = cross_sum + moments(left_ref, wy_parts, TERMS * parts)
+        gram_sum = gram_sum + moments(gram_left_ref, split2_kernel(weight), len(pairs) * parts)
+
     beta, variance = fit_and_spread(
         parts,
         bands,
         gram_sum,
         cross_sum,
         [
-            (groups[0][3], groups[0][2], None, lambda here: weight_ref[here, :]),
+            (groups[0][3], groups[0][2], None, lambda: weight_ref[0:early, :]),
             (
                 groups[1][3],
                 groups[1][2],
                 None,
-                lambda here: weight_ref[here.start + early : here.stop + early, :],
+                lambda: weight_ref[early:, :],
             ),
         ],
     )
@@ -549,7 +547,6 @@
         + sums,
         in_specs=[vmem] * (early_count + 1),
         out_specs=[vmem] * 10,
-        scratch_shapes=[pltpu.VMEM((early_rows, bands * LANES), bf16)],
         compiler_params=params,
         name="absorb",
     )(*early_blocks, infos)
@@ -559,7 +556,6 @@
         out_shape=data_shapes(late_rows) + [power(early_rows), power(late_rows), send],
         in_specs=[vmem] * (late_count + 8),
         out_specs=[vmem] * 5,
-        scratch_shapes=[pltpu.VMEM((late_rows, bands * LANES), bf16)],
         compiler_params=params,
         name="first",
     )(*late_blocks, *late, *early[2:], *early_sums)
@@ -572,9 +568,7 @@
         out_shape=[jax.ShapeDtypeStruct((bands, TERMS, rows, width), f32), send],
         in_specs=[vmem] * 13,
         out_specs=[vmem] * 2,
-        scratch_shapes=[pltpu.VMEM((total, LANES), f32)]
-        + [pltpu.VMEM((total, LANES), bf16)] * 2
-        + [pltpu.VMEM((total, bands * LANES), bf16)] * 2,
+        scratch_shapes=[pltpu.VMEM((total, LANES), f32)],
         compiler_params=params,
         name="second",
     )(field, *early, early_power, *late, late_power)

time: 67.3 us -> 66.8 us (level)
  no operation moved by 1% of the time
where the time goes in v6:
time: 66.8 us; the launch traced here: 66.6 us
  starting transfers between devices  22.2 us (33%)
  blocking collectives  22.2 us (33%)
  Pallas kernels  11.1 us (17%)
  waiting for transfers between devices  9.45 us (14%)
  local copies, waits for them, and re-layouts  0.94 us (1%)
  between operations  0.69 us (1%)
    all_to_all x2, blocking collectives, on_device(): field = lax.all_to_all(variance, ('space', 'date'), 0, 0, tiled=True)  22.2 us
    ppermute x7, starting transfers between devices, swap(): lax.ppermute(block, 'date', [(i, i ^ k) for i in range(count)])  21.6 us
    ppermute x7, waiting for transfers between devices, swap(): lax.ppermute(block, 'date', [(i, i ^ k) for i in range(count)])  5.56 us
    pallas_call x2, Pallas kernels, packed_blocks(): pl.pallas_call(functools.partial(pack_kernel, tuple(steps), far), out_sha...  4.87 us
    ppermute x1, waiting for transfers between devices, on_device(): infos = lax.ppermute(infos, 'date', [(i, i ^ 1) for i in range(count)])  3.88 us
    pallas_call x1, Pallas kernels, on_device(): pl.pallas_call(functools.partial(second_kernel, shape), out_shape=[jax.Sh...  2.48 us
    pallas_call x1, Pallas kernels, on_device(): pl.pallas_call(functools.partial(absorb_kernel, (bands, dates, parts), ea...  1.9 us
  transfers between devices with their start and end apart: 8, of which 4 were waited for; matrix products, arithmetic and copies ran while one was open for 0% of the time, Pallas kernels for 7%

profile of v6, /device:TPU:0, one launch (start us, length us, event | category | flops | bytes accessed | tf_op | source)
XLA Modules:
  0.0 66.6 jit_solution(7579892831691206142)
XLA Ops:
  0.6 2.4 %pack.2 = (bf16[784,128]{1,0:T(8,128)(2,1)}, bf16[768,128]{1,0:T(8,128)(2,1)}, bf16[784,128]{1,0:T(8,128)(2,1)}, bf16[768,128]{1,0:T(8,128)(2,1)}) custom-call(s32[24]{0:T(128)} %day_ref.3, bf16[7,24,8,512]{3,2,1,0:T(8,128)(2,1)} %obs_ref.3, s32[24,8,512]{2,1,0:T(8,128)} %valid_ref.3), custom_call_target="tpu_custom_call" | custom-call | tf_op jit(solution)/shard_map/pack/pallas_call | solution.py:135
  3.1 0.0 copy-start.2
  3.1 0.0 copy-start.1
  3.1 5.1 %collective-permute-start = (bf16[784,128]{1,0:T(8,128)(2,1)}, bf16[784,128]{1,0:T(8,128)(2,1)S(1)}, u32[]{:S(2)}, u32[]{:S(2)}) collective-permute-start(bf16[784,128]{1,0:T(8,128)(2,1)} %get-tuple-element.32), channel_id=1, source_target_pairs={{0,6},{1,7},{2,4},{3,5},{4,2},{5,3},{6,0},{7,1},{8,14},{9,15},{10,... | collective-permute-start | bytes 602120 | tf_op jit(solution)/shard_map/ppermute | solution.py:507
  8.2 0.0 collective-permute-start.2
  8.2 2.4 %pack.3 = (bf16[784,128]{1,0:T(8,128)(2,1)}, bf16[784,128]{1,0:T(8,128)(2,1)}, bf16[784,128]{1,0:T(8,128)(2,1)}, bf16[784,128]{1,0:T(8,128)(2,1)}) custom-call(s32[24]{0:T(128)} %day_ref.3, bf16[7,24,8,512]{3,2,1,0:T(8,128)(2,1)} %obs_ref.3, s32[24,8,512]{2,1,0:T(8,128)} %valid_ref.3), custom_call_target="tpu_custom_call" | custom-call | tf_op jit(solution)/shard_map/pack/pallas_call | solution.py:135
  10.6 1.6 %collective-permute-start.4 = (bf16[784,128]{1,0:T(8,128)(2,1)}, bf16[784,128]{1,0:T(8,128)(2,1)S(1)}, u32[]{:S(2)}, u32[]{:S(2)}) collective-permute-start(bf16[784,128]{1,0:T(8,128)(2,1)} %get-tuple-element.38), channel_id=1, source_target_pairs={{0,1},{1,0},{2,3},{3,2},{4,5},{5,4},{6,7},{7,6},{8,9},{9,8},{10,11... | collective-permute-start | bytes 602120 | tf_op jit(solution)/shard_map/ppermute | solution.py:507
  12.2 0.8 %collective-permute-start.5 = (bf16[784,128]{1,0:T(8,128)(2,1)}, bf16[784,128]{1,0:T(8,128)(2,1)S(1)}, u32[]{:S(2)}, u32[]{:S(2)}) collective-permute-start(bf16[784,128]{1,0:T(8,128)(2,1)} %get-tuple-element.39), channel_id=1, source_target_pairs={{0,2},{1,3},{2,0},{3,1},{4,6},{5,7},{6,4},{7,5},{8,10},{9,11},{10,... | collective-permute-start | bytes 602120 | tf_op jit(solution)/shard_map/ppermute | solution.py:507
  13.0 1.2 %collective-permute-start.6 = (bf16[784,128]{1,0:T(8,128)(2,1)}, bf16[784,128]{1,0:T(8,128)(2,1)S(1)}, u32[]{:S(2)}, u32[]{:S(2)}) collective-permute-start(bf16[784,128]{1,0:T(8,128)(2,1)} %get-tuple-element.40), channel_id=1, source_target_pairs={{0,3},{1,2},{2,1},{3,0},{4,7},{5,6},{6,5},{7,4},{8,11},{9,10},{10,... | collective-permute-start | bytes 602120 | tf_op jit(solution)/shard_map/ppermute | solution.py:507
  14.2 0.1 collective-permute-done.refs_5_
  14.3 0.0 copy-done.2
  14.3 10.5 %collective-permute-start.1 = (bf16[768,128]{1,0:T(8,128)(2,1)S(1)}, bf16[768,128]{1,0:T(8,128)(2,1)S(1)}, u32[]{:S(2)}, u32[]{:S(2)}) collective-permute-start(bf16[768,128]{1,0:T(8,128)(2,1)S(1)} %copy-done.2), channel_id=1, source_target_pairs={{0,5},{1,4},{2,7},{3,6},{4,1},{5,0},{6,3},{7,2},{8,13},{9,12},{10,... | collective-permute-start | bytes 589832 | tf_op jit(solution)/shard_map/ppermute | solution.py:507
  24.8 3.1 %collective-permute-done.2.refs_4_ = bf16[784,128]{1,0:T(8,128)(2,1)S(1)} collective-permute-done((bf16[784,128]{1,0:T(8,128)(2,1)}, bf16[784,128]{1,0:T(8,128)(2,1)S(1)}, u32[]{:S(2)}, u32[]{:S(2)}) %collective-permute-start.2) | collective-permute-done | bytes 200736 | tf_op jit(solution)/shard_map/ppermute | solution.py:507
  27.9 0.0 copy-done.1
  27.9 2.4 %collective-permute-start.3 = (bf16[768,128]{1,0:T(8,128)(2,1)S(1)}, bf16[768,128]{1,0:T(8,128)(2,1)S(1)}, u32[]{:S(2)}, u32[]{:S(2)}) collective-permute-start(bf16[768,128]{1,0:T(8,128)(2,1)S(1)} %copy-done.1), channel_id=1, source_target_pairs={{0,7},{1,6},{2,5},{3,4},{4,3},{5,2},{6,1},{7,0},{8,15},{9,14},{10,... | collective-permute-start | bytes 589832 | tf_op jit(solution)/shard_map/ppermute | solution.py:507
  30.4 0.0 collective-permute-done.4.refs_1_
  30.4 0.6 collective-permute-start.7
  31.0 0.0 collective-permute-done.5.refs_2_
  31.0 0.0 collective-permute-done.6.refs_3_
  31.0 3.9 %collective-permute-done.7.refs_6_ = bf16[32,128]{1,0:T(8,128)(2,1)S(1)} collective-permute-done((bf16[32,128]{1,0:T(8,128)(2,1)S(1)}, bf16[32,128]{1,0:T(8,128)(2,1)S(1)}, u32[]{:S(2)}, u32[]{:S(2)}) %collective-permute-start.7) | collective-permute-done | bytes 8224 | tf_op jit(solution)/shard_map/ppermute | solution.py:517
  34.9 0.0 copy-start
  34.9 0.9 %copy-done = bf16[784,128]{1,0:T(8,128)(2,1)S(1)} copy-done((bf16[784,128]{1,0:T(8,128)(2,1)S(1)}, bf16[784,128]{1,0:T(8,128)(2,1)}, u32[]{:S(2)}) %copy-start) | copy-done | bytes 200728
  35.8 1.9 %absorb.1 = (bf16[96,576]{1,0:T(8,128)(2,1)S(1)}, bf16[432,576]{1,0:T(8,128)(2,1)S(1)}, bf16[576,192]{1,0:T(8,128)(2,1)S(1)}, bf16[576,896]{1,0:T(8,128)(2,1)S(1...) custom-call(bf16[784,128]{1,0:T(8,128)(2,1)S(1)} %copy-done, ...), custom_call_target="tpu_custom_call" | custom-call | tf_op jit(solution)/shard_map/absorb/pallas_call | solution.py:542
  37.7 2.3 %collective-permute-done.1.refs_0_ = bf16[768,128]{1,0:T(8,128)(2,1)S(1)} collective-permute-done((bf16[768,128]{1,0:T(8,128)(2,1)S(1)}, bf16[768,128]{1,0:T(8,128)(2,1)S(1)}, u32[]{:S(2)}, u32[]{:S(2)}) %collective-permute-start.1) | collective-permute-done | bytes 196640 | tf_op jit(solution)/shard_map/ppermute | solution.py:507
  40.0 0.0 collective-permute-done.3.refs_1_
  40.0 1.1 %first.1 = (bf16[192,896]{1,0:T(8,128)(2,1)S(1)}, bf16[192,128]{1,0:T(8,128)(2,1)S(1)}, f32[576,128]{1,0:T(8,128)S(1)}, f32[192,128]{1,0:T(8,128)S(1)}, f32[32,4,128]{2,1,0:T(4,128)S(1)}) custom-call(bf16[768,128]{1,0:T(8,128)(2,1)S(1)} %collective-permute-done.1.refs_0_, bf16[768,128]{1,0:T(8,128)(2,1)S(1)} %collective-permute-done.3.refs_1_, ...), custom_call_target="tpu_custom_call" | custom-call | tf_op jit(solution)/shard_map/first/pallas_call | solution.py:554
  41.1 13.2 %all_to_all.10.refs_0_ = f32[32,4,128]{2,1,0:T(4,128)S(1)} all-to-all(f32[32,4,128]{2,1,0:T(4,128)S(1)} %get-tuple-element.51), channel_id=1, replica_groups=mesh['space'=4,'date'=8] {'space','date'}, dimensions={0} | all-to-all | bytes 131072 | tf_op jit(solution)/shard_map/all_to_all | solution.py:564
  54.4 2.5 %second.1 = (f32[7,8,8,64]{3,2,1,0:T(8,128)}, f32[32,4,128]{2,1,0:T(4,128)S(1)}) custom-call(f32[32,4,128]{2,1,0:T(4,128)S(1)} %all_to_all.10.refs_0_, bf16[96,576]{1,0:T(8,128)(2,1)S(1)} %get-tuple-element.52.refs_1_, bf16[432,576]{1,0:T(8,128)(2,1)S(1)} %get-tuple-element.53.refs_2_, bf16[576,192]{1,0:T(8,128)(2,1)S(1)} %get-tuple-element.46.refs_5_.refs_3_, ...), custom_call_target="tpu_custom_call" | custom-call | tf_op jit(solution)/shard_map/second/pallas_call | solution.py:566
  56.9 9.0 %all_to_all.11.field_ref = f32[32,4,128]{2,1,0:T(4,128)S(1)} all-to-all(f32[32,4,128]{2,1,0:T(4,128)S(1)} %get-tuple-element.59), channel_id=1, replica_groups=mesh['space'=4,'date'=8] {'space','date'}, dimensions={0} | all-to-all | bytes 131072 | tf_op jit(solution)/shard_map/all_to_all | solution.py:575
  65.8 0.8 %last.1 = f32[8,64]{1,0:T(8,128)} custom-call(f32[32,4,128]{2,1,0:T(4,128)S(1)} %all_to_all.11.field_ref), custom_call_target="tpu_custom_call" | custom-call | tf_op jit(solution)/shard_map/last/pallas_call | solution.py:576
  (3 shorter events, 0.0 us)
Async XLA Ops:
  3.1 11.3 %copy-start.2 = (bf16[768,128]{1,0:T(8,128)(2,1)S(1)}, bf16[768,128]{1,0:T(8,128)(2,1)}, u32[]{:S(2)}) copy-start(bf16[768,128]{1,0:T(8,128)(2,1)} %get-tuple-element.33) | copy-start | bytes 589828
  3.1 24.9 %copy-start.1 = (bf16[768,128]{1,0:T(8,128)(2,1)S(1)}, bf16[768,128]{1,0:T(8,128)(2,1)}, u32[]{:S(2)}) copy-start(bf16[768,128]{1,0:T(8,128)(2,1)} %get-tuple-element.36) | copy-start | bytes 589828
  3.1 11.2 %collective-permute-start = (bf16[784,128]{1,0:T(8,128)(2,1)}, bf16[784,128]{1,0:T(8,128)(2,1)S(1)}, u32[]{:S(2)}, u32[]{:S(2)}) collective-permute-start(bf16[784,128]{1,0:T(8,128)(2,1)} %get-tuple-element.32), channel_id=1, source_target_pairs={{0,6},{1,7},{2,4},{3,5},{4,2},{5,3},{6,0},{7,1},{8,14},{9,15},{10,... | collective-permute-start | bytes 602120 | tf_op jit(solution)/shard_map/ppermute | solution.py:507
  8.2 19.7 %collective-permute-start.2 = (bf16[784,128]{1,0:T(8,128)(2,1)}, bf16[784,128]{1,0:T(8,128)(2,1)S(1)}, u32[]{:S(2)}, u32[]{:S(2)}) collective-permute-start(bf16[784,128]{1,0:T(8,128)(2,1)} %get-tuple-element.35), channel_id=1, source_target_pairs={{0,4},{1,5},{2,6},{3,7},{4,0},{5,1},{6,2},{7,3},{8,12},{9,13},{10,... | collective-permute-start | bytes 602120 | tf_op jit(solution)/shard_map/ppermute | solution.py:507
  10.6 19.7 %collective-permute-start.4 = (bf16[784,128]{1,0:T(8,128)(2,1)}, bf16[784,128]{1,0:T(8,128)(2,1)S(1)}, u32[]{:S(2)}, u32[]{:S(2)}) collective-permute-start(bf16[784,128]{1,0:T(8,128)(2,1)} %get-tuple-element.38), channel_id=1, source_target_pairs={{0,1},{1,0},{2,3},{3,2},{4,5},{5,4},{6,7},{7,6},{8,9},{9,8},{10,11... | collective-permute-start | bytes 602120 | tf_op jit(solution)/shard_map/ppermute | solution.py:507
  12.2 18.8 %collective-permute-start.5 = (bf16[784,128]{1,0:T(8,128)(2,1)}, bf16[784,128]{1,0:T(8,128)(2,1)S(1)}, u32[]{:S(2)}, u32[]{:S(2)}) collective-permute-start(bf16[784,128]{1,0:T(8,128)(2,1)} %get-tuple-element.39), channel_id=1, source_target_pairs={{0,2},{1,3},{2,0},{3,1},{4,6},{5,7},{6,4},{7,5},{8,10},{9,11},{10,... | collective-permute-start | bytes 602120 | tf_op jit(solution)/shard_map/ppermute | solution.py:507
  13.0 18.0 %collective-permute-start.6 = (bf16[784,128]{1,0:T(8,128)(2,1)}, bf16[784,128]{1,0:T(8,128)(2,1)S(1)}, u32[]{:S(2)}, u32[]{:S(2)}) collective-permute-start(bf16[784,128]{1,0:T(8,128)(2,1)} %get-tuple-element.40), channel_id=1, source_target_pairs={{0,3},{1,2},{2,1},{3,0},{4,7},{5,6},{6,5},{7,4},{8,11},{9,10},{10,... | collective-permute-start | bytes 602120 | tf_op jit(solution)/shard_map/ppermute | solution.py:507
  14.3 25.7 %collective-permute-start.1 = (bf16[768,128]{1,0:T(8,128)(2,1)S(1)}, bf16[768,128]{1,0:T(8,128)(2,1)S(1)}, u32[]{:S(2)}, u32[]{:S(2)}) collective-permute-start(bf16[768,128]{1,0:T(8,128)(2,1)S(1)} %copy-done.2), channel_id=1, source_target_pairs={{0,5},{1,4},{2,7},{3,6},{4,1},{5,0},{6,3},{7,2},{8,13},{9,12},{10,... | collective-permute-start | bytes 589832 | tf_op jit(solution)/shard_map/ppermute | solution.py:507
  27.9 12.1 %collective-permute-start.3 = (bf16[768,128]{1,0:T(8,128)(2,1)S(1)}, bf16[768,128]{1,0:T(8,128)(2,1)S(1)}, u32[]{:S(2)}, u32[]{:S(2)}) collective-permute-start(bf16[768,128]{1,0:T(8,128)(2,1)S(1)} %copy-done.1), channel_id=1, source_target_pairs={{0,7},{1,6},{2,5},{3,4},{4,3},{5,2},{6,1},{7,0},{8,15},{9,14},{10,... | collective-permute-start | bytes 589832 | tf_op jit(solution)/shard_map/ppermute | solution.py:507
  30.4 4.5 %collective-permute-start.7 = (bf16[32,128]{1,0:T(8,128)(2,1)S(1)}, bf16[32,128]{1,0:T(8,128)(2,1)S(1)}, u32[]{:S(2)}, u32[]{:S(2)}) collective-permute-start(bf16[32,128]{1,0:T(8,128)(2,1)S(1)} %pad_maximum_fusion), channel_id=1, source_target_pairs={{0,1},{1,0},{2,3},{3,2},{4,5},{5,4},{6,7},{7,6},{8,9},{9,8},{10,11... | collective-permute-start | bytes 24584 | tf_op jit(solution)/shard_map/ppermute | solution.py:517
  34.9 0.9 %copy-start = (bf16[784,128]{1,0:T(8,128)(2,1)S(1)}, bf16[784,128]{1,0:T(8,128)(2,1)}, u32[]{:S(2)}) copy-start(bf16[784,128]{1,0:T(8,128)(2,1)} %get-tuple-element.37.refs_0_) | copy-start | bytes 602116

commit v7 on v6

--- a/solution.py
+++ b/solution.py
@@ -332,13 +332,12 @@
         for b in range(bands):
             part = misfit[:, b * LANES : (b + 1) * LANES]
             power = power + part * part
-        power = power / bands
         if power_ref is not None:
             power_ref[...] = power
         weighted = weight_of() * power
         spread = spread + jnp.sum(weighted.reshape(size // 8, 8, LANES), axis=0)
     spread = add_parts(spread, parts)
-    return beta, spread / (1.0 + gram[0, 0])
+    return beta, spread / (bands * (1.0 + gram[0, 0]))
 
 
 def first_kernel(shape, late_count, *refs):
@@ -427,7 +426,7 @@
     weight_ref = refs[15]
     smooth = smoothed(field_ref, parts, width, rows, spaces, count)
     smooth = to_lanes(smooth, parts, width)
-    scale = 1.0 / (TUKEY * TUKEY * (smooth + EPS))
+    scale = 1.0 / (bands * (TUKEY * TUKEY) * (smooth + EPS))
     scale = jnp.concatenate([scale] * (8 // parts), axis=0)
     early = groups[0][3].shape[0]
     cross_sum = gram_sum = 0.0
@@ -449,8 +448,8 @@
             total = add_parts(dot(a_ref[...], b_parts[0]), used)
             return total + add_parts(dot(a_ref[0 : 2 * used, :], b_parts[1]), used)
 
+        gram_sum = gram_sum + moments(gram_left_ref, split2_kernel(weight), len(pairs) * parts)
         cross_sum = cross_sum + moments(left_ref, wy_parts, TERMS * parts)
-        gram_sum = gram_sum + moments(gram_left_ref, split2_kernel(weight), len(pairs) * parts)
 
     beta, variance = fit_and_spread(
         parts,

time: 66.8 us -> 66.6 us (level)
  no operation moved by 1% of the time
where the time goes in v7:
time: 66.6 us; the launch traced here: 66.4 us
  starting transfers between devices  22.2 us (33%)
  blocking collectives  22.2 us (33%)
  Pallas kernels  10.9 us (16%)
  waiting for transfers between devices  9.45 us (14%)
  local copies, waits for them, and re-layouts  0.94 us (1%)
  between operations  0.69 us (1%)
    all_to_all x2, blocking collectives, on_device(): field = lax.all_to_all(variance, ('space', 'date'), 0, 0, tiled=True)  22.2 us
    ppermute x7, starting transfers between devices, swap(): lax.ppermute(block, 'date', [(i, i ^ k) for i in range(count)])  21.6 us
    ppermute x7, waiting for transfers between devices, swap(): lax.ppermute(block, 'date', [(i, i ^ k) for i in range(count)])  5.56 us
    pallas_call x2, Pallas kernels, packed_blocks(): pl.pallas_call(functools.partial(pack_kernel, tuple(steps), far), out_sha...  4.87 us
    ppermute x1, waiting for transfers between devices, on_device(): infos = lax.ppermute(infos, 'date', [(i, i ^ 1) for i in range(count)])  3.88 us
    pallas_call x1, Pallas kernels, on_device(): pl.pallas_call(functools.partial(second_kernel, shape), out_shape=[jax.Sh...  2.28 us
    pallas_call x1, Pallas kernels, on_device(): pl.pallas_call(functools.partial(absorb_kernel, (bands, dates, parts), ea...  1.9 us
  transfers between devices with their start and end apart: 8, of which 4 were waited for; matrix products, arithmetic and copies ran while one was open for 0% of the time, Pallas kernels for 7%

profile of v7, /device:TPU:0, one launch (start us, length us, event | category | flops | bytes accessed | tf_op | source)
XLA Modules:
  0.0 66.4 jit_solution(7005155472194472517)
XLA Ops:
  0.6 2.4 %pack.2 = (bf16[784,128]{1,0:T(8,128)(2,1)}, bf16[768,128]{1,0:T(8,128)(2,1)}, bf16[784,128]{1,0:T(8,128)(2,1)}, bf16[768,128]{1,0:T(8,128)(2,1)}) custom-call(s32[24]{0:T(128)} %day_ref.3, bf16[7,24,8,512]{3,2,1,0:T(8,128)(2,1)} %obs_ref.3, s32[24,8,512]{2,1,0:T(8,128)} %valid_ref.3), custom_call_target="tpu_custom_call" | custom-call | tf_op jit(solution)/shard_map/pack/pallas_call | solution.py:135
  3.1 0.0 copy-start.2
  3.1 0.0 copy-start.1
  3.1 5.1 %collective-permute-start = (bf16[784,128]{1,0:T(8,128)(2,1)}, bf16[784,128]{1,0:T(8,128)(2,1)S(1)}, u32[]{:S(2)}, u32[]{:S(2)}) collective-permute-start(bf16[784,128]{1,0:T(8,128)(2,1)} %get-tuple-element.32), channel_id=1, source_target_pairs={{0,6},{1,7},{2,4},{3,5},{4,2},{5,3},{6,0},{7,1},{8,14},{9,15},{10,... | collective-permute-start | bytes 602120 | tf_op jit(solution)/shard_map/ppermute | solution.py:506
  8.2 0.0 collective-permute-start.2
  8.2 2.4 %pack.3 = (bf16[784,128]{1,0:T(8,128)(2,1)}, bf16[784,128]{1,0:T(8,128)(2,1)}, bf16[784,128]{1,0:T(8,128)(2,1)}, bf16[784,128]{1,0:T(8,128)(2,1)}) custom-call(s32[24]{0:T(128)} %day_ref.3, bf16[7,24,8,512]{3,2,1,0:T(8,128)(2,1)} %obs_ref.3, s32[24,8,512]{2,1,0:T(8,128)} %valid_ref.3), custom_call_target="tpu_custom_call" | custom-call | tf_op jit(solution)/shard_map/pack/pallas_call | solution.py:135
  10.6 1.6 %collective-permute-start.4 = (bf16[784,128]{1,0:T(8,128)(2,1)}, bf16[784,128]{1,0:T(8,128)(2,1)S(1)}, u32[]{:S(2)}, u32[]{:S(2)}) collective-permute-start(bf16[784,128]{1,0:T(8,128)(2,1)} %get-tuple-element.38), channel_id=1, source_target_pairs={{0,1},{1,0},{2,3},{3,2},{4,5},{5,4},{6,7},{7,6},{8,9},{9,8},{10,11... | collective-permute-start | bytes 602120 | tf_op jit(solution)/shard_map/ppermute | solution.py:506
  12.2 0.8 %collective-permute-start.5 = (bf16[784,128]{1,0:T(8,128)(2,1)}, bf16[784,128]{1,0:T(8,128)(2,1)S(1)}, u32[]{:S(2)}, u32[]{:S(2)}) collective-permute-start(bf16[784,128]{1,0:T(8,128)(2,1)} %get-tuple-element.39), channel_id=1, source_target_pairs={{0,2},{1,3},{2,0},{3,1},{4,6},{5,7},{6,4},{7,5},{8,10},{9,11},{10,... | collective-permute-start | bytes 602120 | tf_op jit(solution)/shard_map/ppermute | solution.py:506
  13.0 1.2 %collective-permute-start.6 = (bf16[784,128]{1,0:T(8,128)(2,1)}, bf16[784,128]{1,0:T(8,128)(2,1)S(1)}, u32[]{:S(2)}, u32[]{:S(2)}) collective-permute-start(bf16[784,128]{1,0:T(8,128)(2,1)} %get-tuple-element.40), channel_id=1, source_target_pairs={{0,3},{1,2},{2,1},{3,0},{4,7},{5,6},{6,5},{7,4},{8,11},{9,10},{10,... | collective-permute-start | bytes 602120 | tf_op jit(solution)/shard_map/ppermute | solution.py:506
  14.2 0.1 collective-permute-done.refs_5_
  14.3 0.0 copy-done.2
  14.3 10.5 %collective-permute-start.1 = (bf16[768,128]{1,0:T(8,128)(2,1)S(1)}, bf16[768,128]{1,0:T(8,128)(2,1)S(1)}, u32[]{:S(2)}, u32[]{:S(2)}) collective-permute-start(bf16[768,128]{1,0:T(8,128)(2,1)S(1)} %copy-done.2), channel_id=1, source_target_pairs={{0,5},{1,4},{2,7},{3,6},{4,1},{5,0},{6,3},{7,2},{8,13},{9,12},{10,... | collective-permute-start | bytes 589832 | tf_op jit(solution)/shard_map/ppermute | solution.py:506
  24.8 3.1 %collective-permute-done.2.refs_4_ = bf16[784,128]{1,0:T(8,128)(2,1)S(1)} collective-permute-done((bf16[784,128]{1,0:T(8,128)(2,1)}, bf16[784,128]{1,0:T(8,128)(2,1)S(1)}, u32[]{:S(2)}, u32[]{:S(2)}) %collective-permute-start.2) | collective-permute-done | bytes 200736 | tf_op jit(solution)/shard_map/ppermute | solution.py:506
  27.9 0.0 copy-done.1
  27.9 2.4 %collective-permute-start.3 = (bf16[768,128]{1,0:T(8,128)(2,1)S(1)}, bf16[768,128]{1,0:T(8,128)(2,1)S(1)}, u32[]{:S(2)}, u32[]{:S(2)}) collective-permute-start(bf16[768,128]{1,0:T(8,128)(2,1)S(1)} %copy-done.1), channel_id=1, source_target_pairs={{0,7},{1,6},{2,5},{3,4},{4,3},{5,2},{6,1},{7,0},{8,15},{9,14},{10,... | collective-permute-start | bytes 589832 | tf_op jit(solution)/shard_map/ppermute | solution.py:506
  30.4 0.0 collective-permute-done.4.refs_1_
  30.4 0.6 collective-permute-start.7
  31.0 0.0 collective-permute-done.5.refs_2_
  31.0 0.0 collective-permute-done.6.refs_3_
  31.0 3.9 %collective-permute-done.7.refs_6_ = bf16[32,128]{1,0:T(8,128)(2,1)S(1)} collective-permute-done((bf16[32,128]{1,0:T(8,128)(2,1)S(1)}, bf16[32,128]{1,0:T(8,128)(2,1)S(1)}, u32[]{:S(2)}, u32[]{:S(2)}) %collective-permute-start.7) | collective-permute-done | bytes 8224 | tf_op jit(solution)/shard_map/ppermute | solution.py:516
  34.9 0.0 copy-start
  34.9 0.9 %copy-done = bf16[784,128]{1,0:T(8,128)(2,1)S(1)} copy-done((bf16[784,128]{1,0:T(8,128)(2,1)S(1)}, bf16[784,128]{1,0:T(8,128)(2,1)}, u32[]{:S(2)}) %copy-start) | copy-done | bytes 200728
  35.8 1.9 %absorb.1 = (bf16[96,576]{1,0:T(8,128)(2,1)S(1)}, bf16[432,576]{1,0:T(8,128)(2,1)S(1)}, bf16[576,192]{1,0:T(8,128)(2,1)S(1)}, bf16[576,896]{1,0:T(8,128)(2,1)S(1...) custom-call(bf16[784,128]{1,0:T(8,128)(2,1)S(1)} %copy-done, ...), custom_call_target="tpu_custom_call" | custom-call | tf_op jit(solution)/shard_map/absorb/pallas_call | solution.py:541
  37.7 2.3 %collective-permute-done.1.refs_0_ = bf16[768,128]{1,0:T(8,128)(2,1)S(1)} collective-permute-done((bf16[768,128]{1,0:T(8,128)(2,1)S(1)}, bf16[768,128]{1,0:T(8,128)(2,1)S(1)}, u32[]{:S(2)}, u32[]{:S(2)}) %collective-permute-start.1) | collective-permute-done | bytes 196640 | tf_op jit(solution)/shard_map/ppermute | solution.py:506
  40.0 0.0 collective-permute-done.3.refs_1_
  40.0 1.1 %first.1 = (bf16[192,896]{1,0:T(8,128)(2,1)S(1)}, bf16[192,128]{1,0:T(8,128)(2,1)S(1)}, f32[576,128]{1,0:T(8,128)S(1)}, f32[192,128]{1,0:T(8,128)S(1)}, f32[32,4,128]{2,1,0:T(4,128)S(1)}) custom-call(bf16[768,128]{1,0:T(8,128)(2,1)S(1)} %collective-permute-done.1.refs_0_, bf16[768,128]{1,0:T(8,128)(2,1)S(1)} %collective-permute-done.3.refs_1_, ...), custom_call_target="tpu_custom_call" | custom-call | tf_op jit(solution)/shard_map/first/pallas_call | solution.py:553
  41.1 13.2 %all_to_all.10.refs_0_ = f32[32,4,128]{2,1,0:T(4,128)S(1)} all-to-all(f32[32,4,128]{2,1,0:T(4,128)S(1)} %get-tuple-element.51), channel_id=1, replica_groups=mesh['space'=4,'date'=8] {'space','date'}, dimensions={0} | all-to-all | bytes 131072 | tf_op jit(solution)/shard_map/all_to_all | solution.py:563
  54.4 2.3 %second.1 = (f32[7,8,8,64]{3,2,1,0:T(8,128)}, f32[32,4,128]{2,1,0:T(4,128)S(1)}) custom-call(f32[32,4,128]{2,1,0:T(4,128)S(1)} %all_to_all.10.refs_0_, bf16[96,576]{1,0:T(8,128)(2,1)S(1)} %get-tuple-element.52.refs_1_, bf16[432,576]{1,0:T(8,128)(2,1)S(1)} %get-tuple-element.53.refs_2_, bf16[576,192]{1,0:T(8,128)(2,1)S(1)} %get-tuple-element.46.refs_5_.refs_3_, ...), custom_call_target="tpu_custom_call" | custom-call | tf_op jit(solution)/shard_map/second/pallas_call | solution.py:565
  56.6 9.0 %all_to_all.11.field_ref = f32[32,4,128]{2,1,0:T(4,128)S(1)} all-to-all(f32[32,4,128]{2,1,0:T(4,128)S(1)} %get-tuple-element.59), channel_id=1, replica_groups=mesh['space'=4,'date'=8] {'space','date'}, dimensions={0} | all-to-all | bytes 131072 | tf_op jit(solution)/shard_map/all_to_all | solution.py:574
  65.6 0.8 %last.1 = f32[8,64]{1,0:T(8,128)} custom-call(f32[32,4,128]{2,1,0:T(4,128)S(1)} %all_to_all.11.field_ref), custom_call_target="tpu_custom_call" | custom-call | tf_op jit(solution)/shard_map/last/pallas_call | solution.py:575
  (3 shorter events, 0.0 us)
Async XLA Ops:
  3.1 11.3 %copy-start.2 = (bf16[768,128]{1,0:T(8,128)(2,1)S(1)}, bf16[768,128]{1,0:T(8,128)(2,1)}, u32[]{:S(2)}) copy-start(bf16[768,128]{1,0:T(8,128)(2,1)} %get-tuple-element.33) | copy-start | bytes 589828
  3.1 24.9 %copy-start.1 = (bf16[768,128]{1,0:T(8,128)(2,1)S(1)}, bf16[768,128]{1,0:T(8,128)(2,1)}, u32[]{:S(2)}) copy-start(bf16[768,128]{1,0:T(8,128)(2,1)} %get-tuple-element.36) | copy-start | bytes 589828
  3.1 11.2 %collective-permute-start = (bf16[784,128]{1,0:T(8,128)(2,1)}, bf16[784,128]{1,0:T(8,128)(2,1)S(1)}, u32[]{:S(2)}, u32[]{:S(2)}) collective-permute-start(bf16[784,128]{1,0:T(8,128)(2,1)} %get-tuple-element.32), channel_id=1, source_target_pairs={{0,6},{1,7},{2,4},{3,5},{4,2},{5,3},{6,0},{7,1},{8,14},{9,15},{10,... | collective-permute-start | bytes 602120 | tf_op jit(solution)/shard_map/ppermute | solution.py:506
  8.2 19.7 %collective-permute-start.2 = (bf16[784,128]{1,0:T(8,128)(2,1)}, bf16[784,128]{1,0:T(8,128)(2,1)S(1)}, u32[]{:S(2)}, u32[]{:S(2)}) collective-permute-start(bf16[784,128]{1,0:T(8,128)(2,1)} %get-tuple-element.35), channel_id=1, source_target_pairs={{0,4},{1,5},{2,6},{3,7},{4,0},{5,1},{6,2},{7,3},{8,12},{9,13},{10,... | collective-permute-start | bytes 602120 | tf_op jit(solution)/shard_map/ppermute | solution.py:506
  10.6 19.7 %collective-permute-start.4 = (bf16[784,128]{1,0:T(8,128)(2,1)}, bf16[784,128]{1,0:T(8,128)(2,1)S(1)}, u32[]{:S(2)}, u32[]{:S(2)}) collective-permute-start(bf16[784,128]{1,0:T(8,128)(2,1)} %get-tuple-element.38), channel_id=1, source_target_pairs={{0,1},{1,0},{2,3},{3,2},{4,5},{5,4},{6,7},{7,6},{8,9},{9,8},{10,11... | collective-permute-start | bytes 602120 | tf_op jit(solution)/shard_map/ppermute | solution.py:506
  12.2 18.8 %collective-permute-start.5 = (bf16[784,128]{1,0:T(8,128)(2,1)}, bf16[784,128]{1,0:T(8,128)(2,1)S(1)}, u32[]{:S(2)}, u32[]{:S(2)}) collective-permute-start(bf16[784,128]{1,0:T(8,128)(2,1)} %get-tuple-element.39), channel_id=1, source_target_pairs={{0,2},{1,3},{2,0},{3,1},{4,6},{5,7},{6,4},{7,5},{8,10},{9,11},{10,... | collective-permute-start | bytes 602120 | tf_op jit(solution)/shard_map/ppermute | solution.py:506
  13.0 18.0 %collective-permute-start.6 = (bf16[784,128]{1,0:T(8,128)(2,1)}, bf16[784,128]{1,0:T(8,128)(2,1)S(1)}, u32[]{:S(2)}, u32[]{:S(2)}) collective-permute-start(bf16[784,128]{1,0:T(8,128)(2,1)} %get-tuple-element.40), channel_id=1, source_target_pairs={{0,3},{1,2},{2,1},{3,0},{4,7},{5,6},{6,5},{7,4},{8,11},{9,10},{10,... | collective-permute-start | bytes 602120 | tf_op jit(solution)/shard_map/ppermute | solution.py:506
  14.3 25.7 %collective-permute-start.1 = (bf16[768,128]{1,0:T(8,128)(2,1)S(1)}, bf16[768,128]{1,0:T(8,128)(2,1)S(1)}, u32[]{:S(2)}, u32[]{:S(2)}) collective-permute-start(bf16[768,128]{1,0:T(8,128)(2,1)S(1)} %copy-done.2), channel_id=1, source_target_pairs={{0,5},{1,4},{2,7},{3,6},{4,1},{5,0},{6,3},{7,2},{8,13},{9,12},{10,... | collective-permute-start | bytes 589832 | tf_op jit(solution)/shard_map/ppermute | solution.py:506
  27.9 12.1 %collective-permute-start.3 = (bf16[768,128]{1,0:T(8,128)(2,1)S(1)}, bf16[768,128]{1,0:T(8,128)(2,1)S(1)}, u32[]{:S(2)}, u32[]{:S(2)}) collective-permute-start(bf16[768,128]{1,0:T(8,128)(2,1)S(1)} %copy-done.1), channel_id=1, source_target_pairs={{0,7},{1,6},{2,5},{3,4},{4,3},{5,2},{6,1},{7,0},{8,15},{9,14},{10,... | collective-permute-start | bytes 589832 | tf_op jit(solution)/shard_map/ppermute | solution.py:506
  30.4 4.5 %collective-permute-start.7 = (bf16[32,128]{1,0:T(8,128)(2,1)S(1)}, bf16[32,128]{1,0:T(8,128)(2,1)S(1)}, u32[]{:S(2)}, u32[]{:S(2)}) collective-permute-start(bf16[32,128]{1,0:T(8,128)(2,1)S(1)} %pad_maximum_fusion), channel_id=1, source_target_pairs={{0,1},{1,0},{2,3},{3,2},{4,5},{5,4},{6,7},{7,6},{8,9},{9,8},{10,11... | collective-permute-start | bytes 24584 | tf_op jit(solution)/shard_map/ppermute | solution.py:516
  34.9 0.9 %copy-start = (bf16[784,128]{1,0:T(8,128)(2,1)S(1)}, bf16[784,128]{1,0:T(8,128)(2,1)}, u32[]{:S(2)}) copy-start(bf16[784,128]{1,0:T(8,128)(2,1)} %get-tuple-element.37.refs_0_) | copy-start | bytes 602116

commit v8 on v7

--- a/solution.py
+++ b/solution.py
@@ -507,7 +507,7 @@
 
     for k in range(half, count, 2):
         swap(k)
-    for k in range(1, half):
+    for k in reversed(range(1, half)):
         swap(k)
     for k in range(half, count, 2):
         swap(k + 1, after=k ^ 2)

time: 66.6 us -> 66.6 us (level)
  no operation moved by 1% of the time
where the time goes in v8:
time: 66.6 us; the launch traced here: 66.4 us
  starting transfers between devices  22.2 us (33%)
  blocking collectives  22.2 us (33%)
  Pallas kernels  10.9 us (16%)
  waiting for transfers between devices  9.45 us (14%)
  local copies, waits for them, and re-layouts  0.94 us (1%)
  between operations  0.69 us (1%)
    all_to_all x2, blocking collectives, on_device(): field = lax.all_to_all(variance, ('space', 'date'), 0, 0, tiled=True)  22.2 us
    ppermute x7, starting transfers between devices, swap(): lax.ppermute(block, 'date', [(i, i ^ k) for i in range(count)])  21.6 us
    ppermute x7, waiting for transfers between devices, swap(): lax.ppermute(block, 'date', [(i, i ^ k) for i in range(count)])  5.56 us
    pallas_call x2, Pallas kernels, packed_blocks(): pl.pallas_call(functools.partial(pack_kernel, tuple(steps), far), out_sha...  4.87 us
    ppermute x1, waiting for transfers between devices, on_device(): infos = lax.ppermute(infos, 'date', [(i, i ^ 1) for i in range(count)])  3.88 us
    pallas_call x1, Pallas kernels, on_device(): pl.pallas_call(functools.partial(second_kernel, shape), out_shape=[jax.Sh...  2.28 us
    pallas_call x1, Pallas kernels, on_device(): pl.pallas_call(functools.partial(absorb_kernel, (bands, dates, parts), ea...  1.9 us
  transfers between devices with their start and end apart: 8, of which 4 were waited for; matrix products, arithmetic and copies ran while one was open for 0% of the time, Pallas kernels for 7%

profile of v8, /device:TPU:0, one launch (start us, length us, event | category | flops | bytes accessed | tf_op | source)
XLA Modules:
  0.0 66.4 jit_solution(7005155472194472517)
XLA Ops:
  0.6 2.4 %pack.2 = (bf16[784,128]{1,0:T(8,128)(2,1)}, bf16[768,128]{1,0:T(8,128)(2,1)}, bf16[784,128]{1,0:T(8,128)(2,1)}, bf16[768,128]{1,0:T(8,128)(2,1)}) custom-call(s32[24]{0:T(128)} %day_ref.3, bf16[7,24,8,512]{3,2,1,0:T(8,128)(2,1)} %obs_ref.3, s32[24,8,512]{2,1,0:T(8,128)} %valid_ref.3), custom_call_target="tpu_custom_call" | custom-call | tf_op jit(solution)/shard_map/pack/pallas_call | solution.py:135
  3.1 0.0 copy-start.2
  3.1 0.0 copy-start.1
  3.1 5.1 %collective-permute-start = (bf16[784,128]{1,0:T(8,128)(2,1)}, bf16[784,128]{1,0:T(8,128)(2,1)S(1)}, u32[]{:S(2)}, u32[]{:S(2)}) collective-permute-start(bf16[784,128]{1,0:T(8,128)(2,1)} %get-tuple-element.32), channel_id=1, source_target_pairs={{0,6},{1,7},{2,4},{3,5},{4,2},{5,3},{6,0},{7,1},{8,14},{9,15},{10,... | collective-permute-start | bytes 602120 | tf_op jit(solution)/shard_map/ppermute | solution.py:506
  8.2 0.0 collective-permute-start.2
  8.2 2.4 %pack.3 = (bf16[784,128]{1,0:T(8,128)(2,1)}, bf16[784,128]{1,0:T(8,128)(2,1)}, bf16[784,128]{1,0:T(8,128)(2,1)}, bf16[784,128]{1,0:T(8,128)(2,1)}) custom-call(s32[24]{0:T(128)} %day_ref.3, bf16[7,24,8,512]{3,2,1,0:T(8,128)(2,1)} %obs_ref.3, s32[24,8,512]{2,1,0:T(8,128)} %valid_ref.3), custom_call_target="tpu_custom_call" | custom-call | tf_op jit(solution)/shard_map/pack/pallas_call | solution.py:135
  10.6 1.6 %collective-permute-start.4 = (bf16[784,128]{1,0:T(8,128)(2,1)}, bf16[784,128]{1,0:T(8,128)(2,1)S(1)}, u32[]{:S(2)}, u32[]{:S(2)}) collective-permute-start(bf16[784,128]{1,0:T(8,128)(2,1)} %get-tuple-element.38), channel_id=1, source_target_pairs={{0,1},{1,0},{2,3},{3,2},{4,5},{5,4},{6,7},{7,6},{8,9},{9,8},{10,11... | collective-permute-start | bytes 602120 | tf_op jit(solution)/shard_map/ppermute | solution.py:506
  12.2 0.8 %collective-permute-start.5 = (bf16[784,128]{1,0:T(8,128)(2,1)}, bf16[784,128]{1,0:T(8,128)(2,1)S(1)}, u32[]{:S(2)}, u32[]{:S(2)}) collective-permute-start(bf16[784,128]{1,0:T(8,128)(2,1)} %get-tuple-element.39), channel_id=1, source_target_pairs={{0,2},{1,3},{2,0},{3,1},{4,6},{5,7},{6,4},{7,5},{8,10},{9,11},{10,... | collective-permute-start | bytes 602120 | tf_op jit(solution)/shard_map/ppermute | solution.py:506
  13.0 1.2 %collective-permute-start.6 = (bf16[784,128]{1,0:T(8,128)(2,1)}, bf16[784,128]{1,0:T(8,128)(2,1)S(1)}, u32[]{:S(2)}, u32[]{:S(2)}) collective-permute-start(bf16[784,128]{1,0:T(8,128)(2,1)} %get-tuple-element.40), channel_id=1, source_target_pairs={{0,3},{1,2},{2,1},{3,0},{4,7},{5,6},{6,5},{7,4},{8,11},{9,10},{10,... | collective-permute-start | bytes 602120 | tf_op jit(solution)/shard_map/ppermute | solution.py:506
  14.2 0.1 collective-permute-done.refs_5_
  14.3 0.0 copy-done.2
  14.3 10.5 %collective-permute-start.1 = (bf16[768,128]{1,0:T(8,128)(2,1)S(1)}, bf16[768,128]{1,0:T(8,128)(2,1)S(1)}, u32[]{:S(2)}, u32[]{:S(2)}) collective-permute-start(bf16[768,128]{1,0:T(8,128)(2,1)S(1)} %copy-done.2), channel_id=1, source_target_pairs={{0,5},{1,4},{2,7},{3,6},{4,1},{5,0},{6,3},{7,2},{8,13},{9,12},{10,... | collective-permute-start | bytes 589832 | tf_op jit(solution)/shard_map/ppermute | solution.py:506
  24.8 3.1 %collective-permute-done.2.refs_4_ = bf16[784,128]{1,0:T(8,128)(2,1)S(1)} collective-permute-done((bf16[784,128]{1,0:T(8,128)(2,1)}, bf16[784,128]{1,0:T(8,128)(2,1)S(1)}, u32[]{:S(2)}, u32[]{:S(2)}) %collective-permute-start.2) | collective-permute-done | bytes 200736 | tf_op jit(solution)/shard_map/ppermute | solution.py:506
  27.9 0.0 copy-done.1
  27.9 2.4 %collective-permute-start.3 = (bf16[768,128]{1,0:T(8,128)(2,1)S(1)}, bf16[768,128]{1,0:T(8,128)(2,1)S(1)}, u32[]{:S(2)}, u32[]{:S(2)}) collective-permute-start(bf16[768,128]{1,0:T(8,128)(2,1)S(1)} %copy-done.1), channel_id=1, source_target_pairs={{0,7},{1,6},{2,5},{3,4},{4,3},{5,2},{6,1},{7,0},{8,15},{9,14},{10,... | collective-permute-start | bytes 589832 | tf_op jit(solution)/shard_map/ppermute | solution.py:506
  30.4 0.0 collective-permute-done.4.refs_1_
  30.4 0.6 collective-permute-start.7
  31.0 0.0 collective-permute-done.5.refs_2_
  31.0 0.0 collective-permute-done.6.refs_3_
  31.0 3.9 %collective-permute-done.7.refs_6_ = bf16[32,128]{1,0:T(8,128)(2,1)S(1)} collective-permute-done((bf16[32,128]{1,0:T(8,128)(2,1)S(1)}, bf16[32,128]{1,0:T(8,128)(2,1)S(1)}, u32[]{:S(2)}, u32[]{:S(2)}) %collective-permute-start.7) | collective-permute-done | bytes 8224 | tf_op jit(solution)/shard_map/ppermute | solution.py:516
  34.9 0.0 copy-start
  34.9 0.9 %copy-done = bf16[784,128]{1,0:T(8,128)(2,1)S(1)} copy-done((bf16[784,128]{1,0:T(8,128)(2,1)S(1)}, bf16[784,128]{1,0:T(8,128)(2,1)}, u32[]{:S(2)}) %copy-start) | copy-done | bytes 200728
  35.8 1.9 %absorb.1 = (bf16[96,576]{1,0:T(8,128)(2,1)S(1)}, bf16[432,576]{1,0:T(8,128)(2,1)S(1)}, bf16[576,192]{1,0:T(8,128)(2,1)S(1)}, bf16[576,896]{1,0:T(8,128)(2,1)S(1...) custom-call(bf16[784,128]{1,0:T(8,128)(2,1)S(1)} %copy-done, ...), custom_call_target="tpu_custom_call" | custom-call | tf_op jit(solution)/shard_map/absorb/pallas_call | solution.py:541
  37.7 2.3 %collective-permute-done.1.refs_0_ = bf16[768,128]{1,0:T(8,128)(2,1)S(1)} collective-permute-done((bf16[768,128]{1,0:T(8,128)(2,1)S(1)}, bf16[768,128]{1,0:T(8,128)(2,1)S(1)}, u32[]{:S(2)}, u32[]{:S(2)}) %collective-permute-start.1) | collective-permute-done | bytes 196640 | tf_op jit(solution)/shard_map/ppermute | solution.py:506
  40.0 0.0 collective-permute-done.3.refs_1_
  40.0 1.1 %first.1 = (bf16[192,896]{1,0:T(8,128)(2,1)S(1)}, bf16[192,128]{1,0:T(8,128)(2,1)S(1)}, f32[576,128]{1,0:T(8,128)S(1)}, f32[192,128]{1,0:T(8,128)S(1)}, f32[32,4,128]{2,1,0:T(4,128)S(1)}) custom-call(bf16[768,128]{1,0:T(8,128)(2,1)S(1)} %collective-permute-done.1.refs_0_, bf16[768,128]{1,0:T(8,128)(2,1)S(1)} %collective-permute-done.3.refs_1_, ...), custom_call_target="tpu_custom_call" | custom-call | tf_op jit(solution)/shard_map/first/pallas_call | solution.py:553
  41.1 13.2 %all_to_all.10.refs_0_ = f32[32,4,128]{2,1,0:T(4,128)S(1)} all-to-all(f32[32,4,128]{2,1,0:T(4,128)S(1)} %get-tuple-element.51), channel_id=1, replica_groups=mesh['space'=4,'date'=8] {'space','date'}, dimensions={0} | all-to-all | bytes 131072 | tf_op jit(solution)/shard_map/all_to_all | solution.py:563
  54.4 2.3 %second.1 = (f32[7,8,8,64]{3,2,1,0:T(8,128)}, f32[32,4,128]{2,1,0:T(4,128)S(1)}) custom-call(f32[32,4,128]{2,1,0:T(4,128)S(1)} %all_to_all.10.refs_0_, bf16[96,576]{1,0:T(8,128)(2,1)S(1)} %get-tuple-element.52.refs_1_, bf16[432,576]{1,0:T(8,128)(2,1)S(1)} %get-tuple-element.53.refs_2_, bf16[576,192]{1,0:T(8,128)(2,1)S(1)} %get-tuple-element.46.refs_5_.refs_3_, ...), custom_call_target="tpu_custom_call" | custom-call | tf_op jit(solution)/shard_map/second/pallas_call | solution.py:565
  56.6 9.0 %all_to_all.11.field_ref = f32[32,4,128]{2,1,0:T(4,128)S(1)} all-to-all(f32[32,4,128]{2,1,0:T(4,128)S(1)} %get-tuple-element.59), channel_id=1, replica_groups=mesh['space'=4,'date'=8] {'space','date'}, dimensions={0} | all-to-all | bytes 131072 | tf_op jit(solution)/shard_map/all_to_all | solution.py:574
  65.6 0.8 %last.1 = f32[8,64]{1,0:T(8,128)} custom-call(f32[32,4,128]{2,1,0:T(4,128)S(1)} %all_to_all.11.field_ref), custom_call_target="tpu_custom_call" | custom-call | tf_op jit(solution)/shard_map/last/pallas_call | solution.py:575
  (3 shorter events, 0.0 us)
Async XLA Ops:
  3.1 11.3 %copy-start.2 = (bf16[768,128]{1,0:T(8,128)(2,1)S(1)}, bf16[768,128]{1,0:T(8,128)(2,1)}, u32[]{:S(2)}) copy-start(bf16[768,128]{1,0:T(8,128)(2,1)} %get-tuple-element.33) | copy-start | bytes 589828
  3.1 24.9 %copy-start.1 = (bf16[768,128]{1,0:T(8,128)(2,1)S(1)}, bf16[768,128]{1,0:T(8,128)(2,1)}, u32[]{:S(2)}) copy-start(bf16[768,128]{1,0:T(8,128)(2,1)} %get-tuple-element.36) | copy-start | bytes 589828
  3.1 11.2 %collective-permute-start = (bf16[784,128]{1,0:T(8,128)(2,1)}, bf16[784,128]{1,0:T(8,128)(2,1)S(1)}, u32[]{:S(2)}, u32[]{:S(2)}) collective-permute-start(bf16[784,128]{1,0:T(8,128)(2,1)} %get-tuple-element.32), channel_id=1, source_target_pairs={{0,6},{1,7},{2,4},{3,5},{4,2},{5,3},{6,0},{7,1},{8,14},{9,15},{10,... | collective-permute-start | bytes 602120 | tf_op jit(solution)/shard_map/ppermute | solution.py:506
  8.2 19.7 %collective-permute-start.2 = (bf16[784,128]{1,0:T(8,128)(2,1)}, bf16[784,128]{1,0:T(8,128)(2,1)S(1)}, u32[]{:S(2)}, u32[]{:S(2)}) collective-permute-start(bf16[784,128]{1,0:T(8,128)(2,1)} %get-tuple-element.35), channel_id=1, source_target_pairs={{0,4},{1,5},{2,6},{3,7},{4,0},{5,1},{6,2},{7,3},{8,12},{9,13},{10,... | collective-permute-start | bytes 602120 | tf_op jit(solution)/shard_map/ppermute | solution.py:506
  10.6 19.7 %collective-permute-start.4 = (bf16[784,128]{1,0:T(8,128)(2,1)}, bf16[784,128]{1,0:T(8,128)(2,1)S(1)}, u32[]{:S(2)}, u32[]{:S(2)}) collective-permute-start(bf16[784,128]{1,0:T(8,128)(2,1)} %get-tuple-element.38), channel_id=1, source_target_pairs={{0,1},{1,0},{2,3},{3,2},{4,5},{5,4},{6,7},{7,6},{8,9},{9,8},{10,11... | collective-permute-start | bytes 602120 | tf_op jit(solution)/shard_map/ppermute | solution.py:506
  12.2 18.8 %collective-permute-start.5 = (bf16[784,128]{1,0:T(8,128)(2,1)}, bf16[784,128]{1,0:T(8,128)(2,1)S(1)}, u32[]{:S(2)}, u32[]{:S(2)}) collective-permute-start(bf16[784,128]{1,0:T(8,128)(2,1)} %get-tuple-element.39), channel_id=1, source_target_pairs={{0,2},{1,3},{2,0},{3,1},{4,6},{5,7},{6,4},{7,5},{8,10},{9,11},{10,... | collective-permute-start | bytes 602120 | tf_op jit(solution)/shard_map/ppermute | solution.py:506
  13.0 18.0 %collective-permute-start.6 = (bf16[784,128]{1,0:T(8,128)(2,1)}, bf16[784,128]{1,0:T(8,128)(2,1)S(1)}, u32[]{:S(2)}, u32[]{:S(2)}) collective-permute-start(bf16[784,128]{1,0:T(8,128)(2,1)} %get-tuple-element.40), channel_id=1, source_target_pairs={{0,3},{1,2},{2,1},{3,0},{4,7},{5,6},{6,5},{7,4},{8,11},{9,10},{10,... | collective-permute-start | bytes 602120 | tf_op jit(solution)/shard_map/ppermute | solution.py:506
  14.3 25.7 %collective-permute-start.1 = (bf16[768,128]{1,0:T(8,128)(2,1)S(1)}, bf16[768,128]{1,0:T(8,128)(2,1)S(1)}, u32[]{:S(2)}, u32[]{:S(2)}) collective-permute-start(bf16[768,128]{1,0:T(8,128)(2,1)S(1)} %copy-done.2), channel_id=1, source_target_pairs={{0,5},{1,4},{2,7},{3,6},{4,1},{5,0},{6,3},{7,2},{8,13},{9,12},{10,... | collective-permute-start | bytes 589832 | tf_op jit(solution)/shard_map/ppermute | solution.py:506
  27.9 12.1 %collective-permute-start.3 = (bf16[768,128]{1,0:T(8,128)(2,1)S(1)}, bf16[768,128]{1,0:T(8,128)(2,1)S(1)}, u32[]{:S(2)}, u32[]{:S(2)}) collective-permute-start(bf16[768,128]{1,0:T(8,128)(2,1)S(1)} %copy-done.1), channel_id=1, source_target_pairs={{0,7},{1,6},{2,5},{3,4},{4,3},{5,2},{6,1},{7,0},{8,15},{9,14},{10,... | collective-permute-start | bytes 589832 | tf_op jit(solution)/shard_map/ppermute | solution.py:506
  30.4 4.5 %collective-permute-start.7 = (bf16[32,128]{1,0:T(8,128)(2,1)S(1)}, bf16[32,128]{1,0:T(8,128)(2,1)S(1)}, u32[]{:S(2)}, u32[]{:S(2)}) collective-permute-start(bf16[32,128]{1,0:T(8,128)(2,1)S(1)} %pad_maximum_fusion), channel_id=1, source_target_pairs={{0,1},{1,0},{2,3},{3,2},{4,5},{5,4},{6,7},{7,6},{8,9},{9,8},{10,11... | collective-permute-start | bytes 24584 | tf_op jit(solution)/shard_map/ppermute | solution.py:516
  34.9 0.9 %copy-start = (bf16[784,128]{1,0:T(8,128)(2,1)S(1)}, bf16[784,128]{1,0:T(8,128)(2,1)}, u32[]{:S(2)}) copy-start(bf16[784,128]{1,0:T(8,128)(2,1)} %get-tuple-element.37.refs_0_) | copy-start | bytes 602116
